TPU v7x, 128 devices: a whole 4x4x4 slice. The times are simulated.
128 devices in a mesh: member: 8 (over y_lo, z), region: 16 (over x, y_hi, core).
Axes of the slice: x: 4, y: 4 (y_hi: 2, y_lo: 2; y = y_hi * 2 + y_lo), z: 4, core: 2. Of those that a mesh axis runs over, the one named last changes fastest.
Arguments:
- latent_vertex_values: bfloat16 [64, 8192, 512], P('member', 'region'), may hold values from -6 to 6
- background_field: bfloat16 [64, 16384, 128], P('member', 'region'), may hold values from -6 to 6
- edge_senders: int32 [8192, 6], P('region'), may hold values from 448 to 1087, as said below
- grid_parent: int32 [16384], P('region'), may hold values from 0 to 511
- w_send: bfloat16 [512, 512], replicated, may hold values from -0.25 to 0.25
- w_recv: bfloat16 [512, 512], replicated, may hold values from -0.25 to 0.25
- w_node: bfloat16 [512, 512], replicated, may hold values from -0.25 to 0.25
- w_agg: bfloat16 [512, 512], replicated, may hold values from -0.109375 to 0.109375
- w_out: bfloat16 [512, 512], replicated, may hold values from -0.25 to 0.25
- norm_gain: float32 [512], replicated, may hold values from 0.25 to 1.75
- w_dec: bfloat16 [512, 128], replicated, may hold values from -0.25 to 0.25
- obs_loc: int32 [32768], P(('member', 'region')), may hold values from 0 to 16383
- obs_count: int32 [128], P(('member', 'region')), may hold values from 1 to 256, 16384 in all
- obs_value: float32 [32768], P(('member', 'region')), may hold values from -6 to 6
- obs_var: float32 [32768], P(('member', 'region')), may hold values from 0.25 to 4
- obs_nbr: int32 [32, 16384], P(None, ('member', 'region')), may hold values from 0 to 767
- loc_weight: float32 [32, 16384], P(None, ('member', 'region')), may hold values from 0.1 to 1
Outputs:
- processed_vertex_values: bfloat16 [64, 8192, 512], P('member', 'region')
- assimilated_field: bfloat16 [64, 16384, 128], P('member', 'region')
Inputs may be any that keep to these rules, and one draw needn't show every extreme that they name: edge_senders[n, e] indexes the extended rows of n's region (the 512 nodes of the previous region, its own, then those of the next region, regions in a cycle); an entry outside the own region lies in the last 64 nodes of the previous region or the first 64 nodes of the next. `grid_parent`: a node of the grid point's own region. `obs_loc`: c * 128 + p: channel c at point p of the slot's tile. A tile's live observations are its first obs_count slots. `obs_nbr`: indexes the extended slots of the point's tile: the previous tile's, its own, then the next tile's.
All inputs are finite; a program needn't handle non-finite values. No bound on the sum of `obs_count` on one device may be relied on, other than what follows from the above.
Results may differ from a plain program's by a relative error of at most 0.008.
Values may be sent and summed in bfloat16 or wider, within the bound.
No kernel may reach another device: no remote copies, remote signals or barrier semaphores. Data moves between devices by JAX's collectives and lax.ppermute only.
A program may use at most 128 MiB of HBM per device.

v0:
```python
import jax
import jax.numpy as jnp
from jax import lax
from jax.sharding import PartitionSpec as P

NS_ITERS = 6


def padded(array, sides, width, wrap):
    for axis, dim in sides:
        count, length = (lax.axis_size(axis), array.shape[dim])
        up = [(i, (i + 1) % count) for i in range(count if wrap else count - 1)]
        down = [(j, i) for i, j in up]
        last = lax.slice_in_dim(array, length - width, length, axis=dim)
        first = lax.slice_in_dim(array, 0, width, axis=dim)
        before = lax.ppermute(last, axis, up)
        after = lax.ppermute(first, axis, down)
        array = jnp.concatenate([before, array, after], axis=dim)
    return array


def layer_norm(values, gain):
    mean = jnp.mean(values, axis=-1, keepdims=True)
    centred = values - mean
    var = jnp.mean(centred * centred, axis=-1, keepdims=True)
    return centred / jnp.sqrt(var + 1e-05) * gain


def transform(ens, payload, nbr, loc):
    members = ens.shape[0]
    hp = lax.Precision.HIGHEST
    ypert = payload[:members]
    rinv = payload[members]
    dres = payload[members + 1]
    xval = ens.astype(jnp.float32)
    xpert = xval - jnp.mean(xval, axis=0, keepdims=True)
    ylocal = ypert[:, nbr]
    wlocal = loc * rinv[nbr]
    dlocal = loc * dres[nbr]
    eye = jnp.eye(members, dtype=jnp.float32)[:, :, None]
    amat = (
        jnp.einsum("ilp,jlp->ijp", ylocal * wlocal[None], ylocal, precision=hp)
        + (members - 1.0) * eye
    )
    scale = jnp.sqrt(jnp.sum(amat * amat, axis=(0, 1)))
    ymat = amat / scale
    zmat = jnp.broadcast_to(eye, amat.shape)
    for step in range(NS_ITERS):
        tmat = 1.5 * eye - 0.5 * jnp.einsum("ijp,jkp->ikp", zmat, ymat, precision=hp)
        ymat = jnp.einsum("ijp,jkp->ikp", ymat, tmat, precision=hp)
        zmat = jnp.einsum("ijp,jkp->ikp", tmat, zmat, precision=hp)
    smat = zmat / jnp.sqrt(scale)
    vec = jnp.einsum("ilp,lp->ip", ylocal, dlocal, precision=hp)
    wbar = jnp.einsum(
        "ijp,jp->ip", smat, jnp.einsum("ijp,jp->ip", smat, vec, precision=hp), precision=hp
    )
    wmat = wbar[:, None, :] + jnp.sqrt(members - 1.0) * smat
    increment = jnp.einsum("jpc,jkp->kpc", xpert, wmat, precision=hp) - xpert
    return increment.astype(jnp.bfloat16)


def shards(
    latent_vertex_values,
    background_field,
    edge_senders,
    grid_parent,
    w_send,
    w_recv,
    w_node,
    w_agg,
    w_out,
    norm_gain,
    w_dec,
    obs_loc,
    obs_count,
    obs_value,
    obs_var,
    obs_nbr,
    loc_weight,
):
    member_per_unit, node_dev, width = latent_vertex_values.shape
    grid_r = background_field.shape[1]
    channel_list = background_field.shape[2]
    member_total = lax.axis_size("member")
    region_total = lax.axis_size("region")
    region_block = grid_r // (member_total * region_total)
    slots = obs_loc.shape[0]
    sent = jnp.einsum(
        "knw,wv->knv", latent_vertex_values, w_send, preferred_element_type=jnp.float32
    ).astype(jnp.bfloat16)
    extended = padded(sent, (("region", 1),), node_dev, True)

    def propagate_dynamics(triple):
        state, rows, background_values = triple
        recv = jnp.dot(state, w_recv, preferred_element_type=jnp.float32)
        gathered = rows[edge_senders]
        agg = jnp.sum(jax.nn.silu(gathered.astype(jnp.float32) + recv[:, None, :]), axis=1).astype(
            jnp.bfloat16
        )
        pre = jnp.dot(state, w_node, preferred_element_type=jnp.float32) + jnp.dot(
            agg, w_agg, preferred_element_type=jnp.float32
        )
        hidden = jax.nn.silu(pre).astype(jnp.bfloat16)
        out = jnp.dot(hidden, w_out, preferred_element_type=jnp.float32)
        decoded_field = (state.astype(jnp.float32) + layer_norm(out, norm_gain)).astype(
            jnp.bfloat16
        )
        decoded = jnp.dot(decoded_field, w_dec, preferred_element_type=jnp.float32)
        predicted = (background_values.astype(jnp.float32) + decoded[grid_parent]).astype(
            jnp.bfloat16
        )
        return (decoded_field, predicted)

    processed_vertex_values, predicted_field = lax.map(
        propagate_dynamics, (latent_vertex_values, extended, background_field)
    )
    departing_portions = predicted_field.reshape(
        member_per_unit, member_total, region_total, region_block, channel_list
    ).transpose(1, 2, 0, 3, 4)
    arrived = lax.all_to_all(
        departing_portions.reshape(
            member_total * region_total, member_per_unit, region_block, channel_list
        ),
        ("member", "region"),
        split_axis=0,
        concat_axis=0,
        tiled=True,
    )
    arrived = arrived.reshape(
        member_total, region_total, member_per_unit, region_block, channel_list
    )
    ensemble = arrived.transpose(0, 2, 1, 3, 4).reshape(
        member_total * member_per_unit, region_total * region_block, channel_list
    )
    members = ensemble.shape[0]
    patch_points = ensemble.shape[1]
    flat_index = obs_loc % patch_points * channel_list + obs_loc // patch_points
    yens = ensemble.reshape(members, -1)[:, flat_index].astype(jnp.float32)
    ybar = jnp.mean(yens, axis=0)
    ypert = yens - ybar[None, :]
    valid = (jnp.arange(slots, dtype=jnp.int32) < obs_count[0]).astype(jnp.float32)
    rinv = valid / obs_var
    dres = (obs_value - ybar) * rinv
    payload = jnp.concatenate([ypert, rinv[None, :], dres[None, :]], axis=0)
    widened = padded(
        payload.astype(jnp.bfloat16), ((("member", "region"), 1),), slots, False
    ).astype(payload.dtype)
    increment = transform(ensemble, widened, obs_nbr, loc_weight)
    returning = increment.reshape(
        member_total, member_per_unit, region_total, region_block, channel_list
    ).transpose(0, 2, 1, 3, 4)
    landed = lax.all_to_all(
        returning.reshape(member_total * region_total, member_per_unit, region_block, channel_list),
        ("member", "region"),
        split_axis=0,
        concat_axis=0,
        tiled=True,
    )
    landed = landed.reshape(member_total, region_total, member_per_unit, region_block, channel_list)
    homebound_portion = landed.transpose(2, 0, 1, 3, 4).reshape(
        member_per_unit, grid_r, channel_list
    )
    assimilated_field = (
        predicted_field.astype(jnp.float32) + homebound_portion.astype(jnp.float32)
    ).astype(jnp.bfloat16)
    return (processed_vertex_values, assimilated_field)


def solution(mesh):
    in_specs = (
        P("member", "region", None),
        P("member", "region", None),
        P("region", None),
        P("region"),
        P(),
        P(),
        P(),
        P(),
        P(),
        P(),
        P(),
        P(("member", "region")),
        P(("member", "region")),
        P(("member", "region")),
        P(("member", "region")),
        P(None, ("member", "region")),
        P(None, ("member", "region")),
    )
    out_specs = (P("member", "region", None), P("member", "region", None))
    return jax.shard_map(shards, mesh=mesh, in_specs=in_specs, out_specs=out_specs, check_vma=False)
```

profile of v0, /device:TPU:1, one launch (start us, length us, event | category | flops | bytes accessed | tf_op | source)
XLA Modules:
  0.0 721.2 jit_solution(2664417900994155701)
XLA Ops:
  1.7 6.5 convolution_convert_fusion
  13.3 89.8 %collective-permute-done = bf16[8,512,512]{2,1,0:T(8,128)(2,1)} collective-permute-done((bf16[8,512,512]{2,1,0:T(8,128)(2,1)}, bf16[8,512,512]{2,1,0:T(8,128)(2,1)}, u32[]{:S(2)}, u32[]{:S(2)}) %collective-permute-start) | collective-permute-done | bytes 4194336 | tf_op jit(solution)/shard_map/ppermute | solution.py:16
  105.7 11.2 %pad_maximum_fusion = bf16[8,1536,512]{2,1,0:T(8,128)(2,1)} fusion(bf16[8,512,512]{2,1,0:T(8,128)(2,1)} %collective-permute-done.1, bf16[8,512,512]{2,1,0:T(8,128)(2,1)} %convolution_convert_fusion, bf16[8,512,512]{2,1,0:T(8,128)(2,1)} %collective-permute-done), kind=kLoop, calls=%fused_computation.32 | loop fusion | flops 37748736 | bytes 25165824 | tf_op jit(solution)/shard_map/concatenate | solution.py:18
  116.9 312.1 %while.12 = (s32[]{:T(128)}, bf16[8,512,512]{2,1,0:T(8,128)(2,1)}, bf16[8,1024,128]{2,1,0:T(8,128)(2,1)}, bf16[8,512,512]{2,1,0:T(8,128)(2,1)}, bf16[512,512]{1,...) while((s32[]{:T(128)}, bf16[8,512,512]{2,1,0:T(8,128)(2,1)}, ...), condition=%wide.region_4.5_spmd, body=%wide.region_0.4_spmd.sunk | while | flops 1154630144 | bytes 49337612 | solution.py:114
  120.2 13.3 %gather_fusion = bf16[3072,512]{1,0:T(8,128)(2,1)} fusion(bf16[1536,512]{1,0:T(8,128)(2,1)S(1)} %dynamic-slice_bitcast_fusion.2, s32[3072]{0:T(1024)S(1)} %broadcast_clamp_fusion.4), kind=kCustom, calls=%fused_computation.clone.1 | custom fusion | bytes 6303744 | tf_op jit(solution)/shard_map/while/body/eval_jaxpr/gather | solution.py:96
  133.5 6.7 reshape.209
  159.2 13.3 %gather_fusion = bf16[3072,512]{1,0:T(8,128)(2,1)} fusion(bf16[1536,512]{1,0:T(8,128)(2,1)S(1)} %dynamic-slice_bitcast_fusion.2, s32[3072]{0:T(1024)S(1)} %broadcast_clamp_fusion.4), kind=kCustom, calls=%fused_computation.clone.1 | custom fusion | bytes 6303744 | tf_op jit(solution)/shard_map/while/body/eval_jaxpr/gather | solution.py:96
  172.5 6.7 reshape.209
  179.2 6.4 multiply_reduce_fusion.5
  198.2 13.3 %gather_fusion = bf16[3072,512]{1,0:T(8,128)(2,1)} fusion(bf16[1536,512]{1,0:T(8,128)(2,1)S(1)} %dynamic-slice_bitcast_fusion.2, s32[3072]{0:T(1024)S(1)} %broadcast_clamp_fusion.4), kind=kCustom, calls=%fused_computation.clone.1 | custom fusion | bytes 6303744 | tf_op jit(solution)/shard_map/while/body/eval_jaxpr/gather | solution.py:96
  211.5 6.7 reshape.209
  237.2 13.3 %gather_fusion = bf16[3072,512]{1,0:T(8,128)(2,1)} fusion(bf16[1536,512]{1,0:T(8,128)(2,1)S(1)} %dynamic-slice_bitcast_fusion.2, s32[3072]{0:T(1024)S(1)} %broadcast_clamp_fusion.4), kind=kCustom, calls=%fused_computation.clone.1 | custom fusion | bytes 6303744 | tf_op jit(solution)/shard_map/while/body/eval_jaxpr/gather | solution.py:96
  250.5 6.7 reshape.209
  257.2 6.4 multiply_reduce_fusion.5
  276.3 13.3 %gather_fusion = bf16[3072,512]{1,0:T(8,128)(2,1)} fusion(bf16[1536,512]{1,0:T(8,128)(2,1)S(1)} %dynamic-slice_bitcast_fusion.2, s32[3072]{0:T(1024)S(1)} %broadcast_clamp_fusion.4), kind=kCustom, calls=%fused_computation.clone.1 | custom fusion | bytes 6303744 | tf_op jit(solution)/shard_map/while/body/eval_jaxpr/gather | solution.py:96
  289.5 6.7 reshape.209
  296.2 6.4 multiply_reduce_fusion.5
  315.3 13.3 %gather_fusion = bf16[3072,512]{1,0:T(8,128)(2,1)} fusion(bf16[1536,512]{1,0:T(8,128)(2,1)S(1)} %dynamic-slice_bitcast_fusion.2, s32[3072]{0:T(1024)S(1)} %broadcast_clamp_fusion.4), kind=kCustom, calls=%fused_computation.clone.1 | custom fusion | bytes 6303744 | tf_op jit(solution)/shard_map/while/body/eval_jaxpr/gather | solution.py:96
  328.5 6.7 reshape.209
  354.3 13.3 %gather_fusion = bf16[3072,512]{1,0:T(8,128)(2,1)} fusion(bf16[1536,512]{1,0:T(8,128)(2,1)S(1)} %dynamic-slice_bitcast_fusion.2, s32[3072]{0:T(1024)S(1)} %broadcast_clamp_fusion.4), kind=kCustom, calls=%fused_computation.clone.1 | custom fusion | bytes 6303744 | tf_op jit(solution)/shard_map/while/body/eval_jaxpr/gather | solution.py:96
  367.6 6.7 reshape.209
  393.3 13.3 %gather_fusion = bf16[3072,512]{1,0:T(8,128)(2,1)} fusion(bf16[1536,512]{1,0:T(8,128)(2,1)S(1)} %dynamic-slice_bitcast_fusion.2, s32[3072]{0:T(1024)S(1)} %broadcast_clamp_fusion.4), kind=kCustom, calls=%fused_computation.clone.1 | custom fusion | bytes 6303744 | tf_op jit(solution)/shard_map/while/body/eval_jaxpr/gather | solution.py:96
  406.6 6.7 reshape.209
  432.6 9.0 %all-to-all-start = ((bf16[128,8,8,128]{3,2,1,0:T(8,128)(2,1)}), bf16[128,8,8,128]{3,2,1,0:T(8,128)(2,1)S(1)}, u32[]{:S(2)}, u32[]{:S(2)}) async-start(bf16[128,8,8,128]{3,2,1,0:T(8,128)(2,1)} %bitcast.253), calls=%async_computation | async-start | bytes 4194304 | tf_op jit(solution)/shard_map/all_to_all | solution.py:120
  442.4 29.3 %all-to-all-done = bf16[128,8,8,128]{3,2,1,0:T(8,128)(2,1)S(1)} async-done(((bf16[128,8,8,128]{3,2,1,0:T(8,128)(2,1)}), bf16[128,8,8,128]{3,2,1,0:T(8,128)(2,1)S(1)}, u32[]{:S(2)}, u32[]{:S(2)}) %all-to-all-start) | async-done | bytes 2097184 | tf_op jit(solution)/shard_map/all_to_all | solution.py:120
  497.9 16.7 %gather_fusion.3 = f32[4096]{0:T(1024)S(1)} fusion(f32[768]{0:T(1024)S(1)} %get-tuple-element.125, s32[4096]{0:T(1024)S(1)} %fusion.111), kind=kCustom, calls=%fused_computation.3 | custom fusion | bytes 49152 | tf_op jit(solution)/shard_map/gather | solution.py:39
  514.6 16.7 %gather_fusion.6 = f32[4096]{0:T(1024)S(1)} fusion(f32[768]{0:T(1024)S(1)} %get-tuple-element.126, s32[4096]{0:T(1024)S(1)} %fusion.111), kind=kCustom, calls=%fused_computation.6 | custom fusion | bytes 49152 | tf_op jit(solution)/shard_map/gather | solution.py:38
  531.4 10.8 %gather_fusion.5 = f32[4096,64]{1,0:T(8,128)S(1)} fusion(f32[64,768]{0,1:T(8,128)S(1)} %slice.31, s32[4096]{0:T(1024)S(1)} %fusion.111), kind=kCustom, calls=%fused_computation.5 | custom fusion | bytes 2113536 | tf_op jit(solution)/shard_map/gather | solution.py:37
  542.2 15.0 %gather_fusion.4 = bf16[4096,64]{1,0:T(8,128)(2,1)} fusion(bf16[64,768]{0,1:T(8,128)(2,1)S(1)} %bitcast.248, s32[4096]{0:T(1024)S(1)} %fusion.111), kind=kCustom, calls=%fused_computation.4 | custom fusion | bytes 1064960 | tf_op jit(solution)/shard_map/gather | solution.py:37
  557.2 6.7 multiply_reduce_fusion.2
  648.5 8.2 %fusion.21 = f32[128,64,64]{2,1,0:T(8,128)S(1)} fusion(f32[128,64,64]{2,1,0:T(8,128)} %fusion.25, f32[128,64,64]{2,1,0:T(8,128)} %fusion.29), kind=kOutput, calls=%fused_computation.47 | convolution fusion | flops 402653184 | bytes 6291456 | tf_op jit(solution)/shard_map/ijp,jkp->ikp/dot_general | solution.py:49
  677.5 39.7 %all_to_all.10 = bf16[128,8,8,128]{3,2,1,0:T(8,128)(2,1)S(1)} all-to-all(bf16[128,8,8,128]{3,2,1,0:T(8,128)(2,1)S(1)} %bitcast.254), channel_id=1, replica_groups=mesh['member'=8,'region'=16] {'member','region'}, dimensions={0} | all-to-all | bytes 4194304 | tf_op jit(solution)/shard_map/all_to_all | solution.py:152
  (322 shorter events, 279.8 us)
Async XLA Ops:
  0.6 11.8 %copy-start.13 = (s32[512,6]{0,1:T(8,128)S(1)}, s32[512,6]{0,1:T(8,128)}, u32[]{:S(2)}) copy-start(s32[512,6]{0,1:T(8,128)} %param.21) | copy-start | bytes 36868
  8.1 95.0 %collective-permute-start = (bf16[8,512,512]{2,1,0:T(8,128)(2,1)}, bf16[8,512,512]{2,1,0:T(8,128)(2,1)}, u32[]{:S(2)}, u32[]{:S(2)}) collective-permute-start(bf16[8,512,512]{2,1,0:T(8,128)(2,1)} %convolution_convert_fusion), channel_id=1, source_target_pairs={{0,1},{1,2},{2,3},{3,4},{4,5},{5,6},{6,7},{7,8},{8,9},{9,10},{10,1... | collective-permute-start | bytes 12582920 | tf_op jit(solution)/shard_map/ppermute | solution.py:16
  12.4 93.2 %collective-permute-start.1 = (bf16[8,512,512]{2,1,0:T(8,128)(2,1)}, bf16[8,512,512]{2,1,0:T(8,128)(2,1)}, u32[]{:S(2)}, u32[]{:S(2)}) collective-permute-start(bf16[8,512,512]{2,1,0:T(8,128)(2,1)} %convolution_convert_fusion), channel_id=1, source_target_pairs={{1,0},{2,1},{3,2},{4,3},{5,4},{6,5},{7,6},{8,7},{9,8},{10,9},{11,1... | collective-permute-start | bytes 12582920 | tf_op jit(solution)/shard_map/ppermute | solution.py:17
  13.3 103.5 %copy-start.5 = (bf16[512,512]{1,0:T(8,128)(2,1)S(1)}, bf16[512,512]{1,0:T(8,128)(2,1)}, u32[]{:S(2)}) copy-start(bf16[512,512]{1,0:T(8,128)(2,1)} %param.24) | copy-start | bytes 1572868
  13.3 103.5 %copy-start.9 = (bf16[512,128]{1,0:T(8,128)(2,1)S(1)}, bf16[512,128]{1,0:T(8,128)(2,1)}, u32[]{:S(2)}) copy-start(bf16[512,128]{1,0:T(8,128)(2,1)} %param.29) | copy-start | bytes 393220
  13.3 103.5 %copy-start.11 = (s32[1024]{0:T(1024)S(1)}, s32[1024]{0:T(1024)}, u32[]{:S(2)}) copy-start(s32[1024]{0:T(1024)} %param.22) | copy-start | bytes 12292
  140.2 6.5 copy-start.4
  149.9 6.0 copy-start.6
  179.2 6.5 copy-start.4
  189.0 6.0 copy-start.6
  218.2 6.5 copy-start.4
  228.0 6.0 copy-start.6
  257.2 6.5 copy-start.4
  267.0 6.0 copy-start.6
  296.2 6.5 copy-start.4
  306.0 6.0 copy-start.6
  335.2 6.5 copy-start.4
  345.0 6.0 copy-start.6
  374.3 6.5 copy-start.4
  413.3 6.5 copy-start.4
  423.1 6.0 copy-start.6
  429.0 13.2 %copy-start.16 = (f32[256]{0:T(256)S(1)}, f32[256]{0:T(256)}, u32[]{:S(2)}) copy-start(f32[256]{0:T(256)} %param.33) | copy-start | bytes 3076
  429.0 13.3 %copy-start.17 = (s32[256]{0:T(256)S(1)}, s32[256]{0:T(256)}, u32[]{:S(2)}) copy-start(s32[256]{0:T(256)} %param.30) | copy-start | bytes 3076
  429.0 13.4 %copy-start.15 = (s32[32,128]{1,0:T(8,128)S(1)}, s32[32,128]{1,0:T(8,128)}, u32[]{:S(2)}) copy-start(s32[32,128]{1,0:T(8,128)} %param.34) | copy-start | bytes 49156
  432.6 39.2 %all-to-all-start = ((bf16[128,8,8,128]{3,2,1,0:T(8,128)(2,1)}), bf16[128,8,8,128]{3,2,1,0:T(8,128)(2,1)S(1)}, u32[]{:S(2)}, u32[]{:S(2)}) async-start(bf16[128,8,8,128]{3,2,1,0:T(8,128)(2,1)} %bitcast.253), calls=%async_computation | async-start | bytes 4194304 | tf_op jit(solution)/shard_map/all_to_all | solution.py:120
  477.8 8.4 %copy-start.18 = (f32[256]{0:T(256)S(1)}, f32[256]{0:T(256)}, u32[]{:S(2)}) copy-start(f32[256]{0:T(256)} %param.32) | copy-start | bytes 3076
  486.5 9.1 %collective-permute-start.2 = (bf16[66,256]{0,1:T(8,128)(2,1)S(1)}, bf16[66,256]{0,1:T(8,128)(2,1)S(1)}, u32[]{:S(2)}, u32[]{:S(2)}) collective-permute-start(bf16[66,256]{0,1:T(8,128)(2,1)S(1)} %pad_maximum_fusion.2), channel_id=1, source_target_pairs={{0,1},{1,2},{2,3},{3,4},{4,5},{5,6},{6,7},{7,8},{8,9},{9,10},{10,1... | collective-permute-start | bytes 101384 | tf_op jit(solution)/shard_map/ppermute | solution.py:16
  490.2 7.1 collective-permute-start.3
  514.6 16.7 %copy-start.14 = (f32[32,128]{1,0:T(8,128)S(1)}, f32[32,128]{1,0:T(8,128)}, u32[]{:S(2)}) copy-start(f32[32,128]{1,0:T(8,128)} %param.35) | copy-start | bytes 49156
  640.9 6.1 copy-start.10
  648.5 8.3 %copy-start.2 = (f32[128,64,64]{2,1,0:T(8,128)S(1)}, f32[128,64,64]{2,1,0:T(8,128)}, u32[]{:S(2)}) copy-start(f32[128,64,64]{2,1,0:T(8,128)} %fusion.29) | copy-start | bytes 6291460
  662.3 7.6 %copy-start.3 = (f32[8,8,16,8,128]{4,1,0,3,2:T(8,128)S(1)}, f32[8,8,16,8,128]{4,1,0,3,2:T(8,128)}, u32[]{:S(2)}) copy-start(f32[8,8,16,8,128]{4,1,0,3,2:T(8,128)} %copy.96) | copy-start | bytes 12582916
  (20 other events, 57.9 us)
where the time goes:
time: 731 us; the launch traced here: 721 us
  local copies, waits for them, and re-layouts  301 us (41%)
  matrix products  151 us (21%)
  waiting for transfers between devices  123 us (17%)
  other arithmetic  83.6 us (11%)
  blocking collectives  39.7 us (5%)
  starting transfers between devices  18.8 us (3%)
    gather x8, local copies, waits for them, and re-layouts, propagate_dynamics(): gathered = rows[edge_senders]  106 us
    ppermute x2, waiting for transfers between devices, padded(): before = lax.ppermute(last, axis, up)  89.8 us
    convert_element_type x8, local copies, waits for them, and re-layouts, propagate_dynamics(): gathered.astype(jnp.float32) + recv[:, None, :]  53.6 us
    reduce_sum x8, other arithmetic, propagate_dynamics(): jnp.sum(jax.nn.silu(gathered.astype(jnp.float32) + recv[:, None, :]), axi...  51.5 us
    all_to_all x1, blocking collectives, shards(): lax.all_to_all(returning.reshape(member_total * region_total, member_per_...  39.7 us
    dot_general x6, matrix products, transform(): jnp.einsum('ijp,jkp->ikp', zmat, ymat, precision=hp)  34.7 us
    dot_general x6, matrix products, transform(): zmat = jnp.einsum('ijp,jkp->ikp', tmat, zmat, precision=hp)  32.7 us
    all_to_all x1, waiting for transfers between devices, shards(): lax.all_to_all(departing_portions.reshape(member_total * region_total, me...  29.3 us
  transfers between devices with their start and end apart: 5, of which 4 were waited for; matrix products, arithmetic and copies ran while one was open for 1% of the time, Pallas kernels for 0%

commit v1 on v0

v1 whole, which is shorter than its diff:
```python
import jax
import jax.numpy as jnp
from jax import lax
from jax.experimental import pallas as pl
from jax.experimental.pallas import tpu as pltpu
from jax.sharding import PartitionSpec as P

NS_ITERS = 6
LANES = 128
RIM = 64
F32 = jnp.float32
BF16 = jnp.bfloat16
MR = ("member", "region")
VM = pl.BlockSpec(memory_space=pltpu.VMEM)
SM = pl.BlockSpec(memory_space=pltpu.SMEM)


def dot(a, b):
    return jnp.dot(a, b, preferred_element_type=F32)


def forecast_kernel(
    edge_ref,
    parent_ref,
    latent_ref,
    before_ref,
    after_ref,
    back_ref,
    w_send_ref,
    w_recv_ref,
    w_node_ref,
    w_agg_ref,
    w_out_ref,
    gain_ref,
    w_dec_ref,
    proc_ref,
    fore_ref,
    send_s,
    recv_s,
    dec_s,
    back_s,
):
    members, nodes, width = latent_ref.shape
    cols = width // LANES
    step = cols * members
    rim = before_ref.shape[1]
    degree = edge_ref.shape[0] // nodes
    grid_r = back_ref.shape[1]

    def scatter_rows(ref, first, member, values):
        for c in range(cols):
            ref[pl.ds(first * step + c * members + member, values.shape[0], stride=step), :] = (
                values[:, c * LANES : (c + 1) * LANES]
            )

    def project(m, carry):
        state = latent_ref[m]
        own = dot(state, w_send_ref[...]).astype(BF16).astype(F32) * 0.5
        scatter_rows(send_s, rim, m, own)
        edge = dot(before_ref[m], w_send_ref[...]).astype(BF16).astype(F32) * 0.5
        scatter_rows(send_s, 0, m, edge)
        edge = dot(after_ref[m], w_send_ref[...]).astype(BF16).astype(F32) * 0.5
        scatter_rows(send_s, rim + nodes, m, edge)
        scatter_rows(recv_s, 0, m, dot(state, w_recv_ref[...]) * 0.5)
        back_s[pl.ds(m, grid_r, stride=members), :] = back_ref[m].astype(F32)
        return carry

    lax.fori_loop(0, members, project, 0)

    def aggregate(n, carry):
        mine = recv_s[pl.ds(pl.multiple_of(n * step, step), step), :]
        total = jnp.zeros_like(mine)
        for e in range(degree):
            row = pl.multiple_of(edge_ref[n * degree + e], step)
            half = send_s[pl.ds(row, step), :] + mine
            total = total + (half + half * jnp.tanh(half))
        recv_s[pl.ds(pl.multiple_of(n * step, step), step), :] = total
        return carry

    lax.fori_loop(0, nodes, aggregate, 0, unroll=4)

    def update(m, carry):
        state = latent_ref[m]
        agg = jnp.concatenate(
            [recv_s[pl.ds(c * members + m, nodes, stride=step), :] for c in range(cols)], axis=1
        ).astype(BF16)
        pre = (dot(state, w_node_ref[...]) + dot(agg, w_agg_ref[...])) * 0.5
        hidden = (pre + pre * jnp.tanh(pre)).astype(BF16)
        out = dot(hidden, w_out_ref[...])
        mean = jnp.mean(out, axis=-1, keepdims=True)
        centred = out - mean
        var = jnp.mean(centred * centred, axis=-1, keepdims=True)
        norm = centred * lax.rsqrt(var + 1e-05) * gain_ref[...]
        proc = (state.astype(F32) + norm).astype(BF16)
        proc_ref[m] = proc
        dec_s[pl.ds(m, nodes, stride=members), :] = dot(proc, w_dec_ref[...])
        return carry

    lax.fori_loop(0, members, update, 0)

    share = fore_ref.shape[1] // members

    def spread(t, carry):
        rows = [
            dec_s[pl.ds(pl.multiple_of(parent_ref[t * share + q], members), members), :]
            for q in range(share)
        ]
        fore_ref[t] = (jnp.concatenate(rows, axis=0) + back_s[pl.ds(t * share * members, share * members), :]).astype(BF16)
        return carry

    lax.fori_loop(0, fore_ref.shape[0], spread, 0, unroll=2)


def forecast(latent, before, after, back, senders, parent, weights):
    members, nodes, width = latent.shape
    grid_r = back.shape[1]
    rim = before.shape[1]
    step = members * width // LANES
    tiles = lax.axis_size("member") * lax.axis_size("region")
    edge = ((senders - (nodes - rim)) * step).reshape(-1)
    return pl.pallas_call(
        forecast_kernel,
        out_shape=(
            jax.ShapeDtypeStruct(latent.shape, BF16),
            jax.ShapeDtypeStruct((tiles, members * grid_r // tiles, LANES), BF16),
        ),
        in_specs=[SM, SM] + [VM] * 11,
        out_specs=(VM, VM),
        scratch_shapes=[
            pltpu.VMEM(((nodes + 2 * rim) * step, LANES), F32),
            pltpu.VMEM((nodes * step, LANES), F32),
            pltpu.VMEM((nodes * members, LANES), F32),
            pltpu.VMEM((grid_r * members, LANES), F32),
        ],
        compiler_params=pltpu.CompilerParams(vmem_limit_bytes=60 * 2**20),
        name="forecast",
    )(edge, parent * members, latent, before, after, back, *weights)


def observe_kernel(loc_ref, count_ref, ens_ref, value_ref, var_ref, pay_ref):
    groups, regions, rows, _ = ens_ref.shape
    size = 8
    members = groups * size
    slots = loc_ref.shape[0]
    lane = lax.broadcasted_iota(jnp.int32, (members, LANES), 1)
    for part in range(slots // LANES):

        def take(i, acc):
            loc = loc_ref[part * LANES + i]
            point, channel = loc % LANES, loc // LANES
            region, place = point // size, point % size
            start = pl.multiple_of(place // 2 * 2 * size, 2 * size)
            second = place % 2
            pieces = []
            for g in range(groups):
                pair = ens_ref[g, region, pl.ds(start, 2 * size), :].astype(F32)
                pieces.append(jnp.where(second == 1, pair[size:], pair[:size]))
            block = jnp.concatenate(pieces, axis=0)
            turned = pltpu.roll(block, (i - channel + LANES) % LANES, 1)
            return jnp.where(lane == i, turned, acc)

        yens = lax.fori_loop(0, LANES, take, jnp.zeros((members, LANES), F32), unroll=2)
        span = slice(part * LANES, (part + 1) * LANES)
        ybar = jnp.mean(yens, axis=0, keepdims=True)
        slot = lax.broadcasted_iota(jnp.int32, (1, LANES), 1) + part * LANES
        rinv = jnp.where(slot < count_ref[0], 1.0, 0.0) / var_ref[:, span]
        dres = (value_ref[:, span] - ybar) * rinv
        row = lax.broadcasted_iota(jnp.int32, (16, LANES), 0)
        extra = jnp.where(row == 0, rinv, jnp.where(row == 1, dres, 0.0))
        pay_ref[0:members, span] = (yens - ybar).astype(BF16)
        pay_ref[members : members + 16, span] = extra.astype(BF16)


def observe(ens, loc, count, value, var):
    groups, regions, rows, _ = ens.shape
    return pl.pallas_call(
        observe_kernel,
        out_shape=jax.ShapeDtypeStruct((groups * 8 + 16, loc.shape[0]), BF16),
        in_specs=[SM, SM, VM, VM, VM],
        out_specs=VM,
        compiler_params=pltpu.CompilerParams(vmem_limit_bytes=40 * 2**20),
        name="observe",
    )(loc, count, ens, value[None], var[None])


def analyse_kernel(
    before_ref,
    own_ref,
    after_ref,
    nbr_ref,
    loc_ref,
    ens_ref,
    inc_ref,
    pay_s,
    bl_s,
    bk_s,
    g_s,
    m_s,
    r_s,
    q_s,
    t_s,
    c_s,
    v_s,
    w_s,
):
    groups, regions, rows, _ = ens_ref.shape
    size = 8
    members = groups * size
    order = nbr_ref.shape[0]
    nb = order // size
    slots = own_ref.shape[1]
    parts = slots // LANES
    sub = lax.broadcasted_iota(jnp.int32, (size, LANES), 0)

    for i, ref in enumerate((before_ref, own_ref, after_ref)):
        for h in range(parts):
            pay_s[i * parts + h] = ref[0 : members + 16, h * LANES : (h + 1) * LANES].astype(F32)

    def full(row):
        return jnp.broadcast_to(row, (size, LANES))

    def gather(l, vec):
        index = nbr_ref[pl.ds(l, 1), :]
        lane = full(index % LANES)
        panel = full(index // LANES)
        masks = [panel == j for j in range(1, 3 * parts)]

        def pick(first):
            out = None
            for j in range(3 * parts):
                got = jnp.take_along_axis(
                    pay_s[j, pl.ds(first, size), :], lane, axis=1, mode="promise_in_bounds"
                )
                out = got if out is None else jnp.where(masks[j - 1], got, out)
            return out

        extra = pick(members)
        weight = loc_ref[pl.ds(l, 1), :]
        root = jnp.sqrt(weight * extra[0:1])
        dl = weight * extra[1:2]
        new = []
        for g in range(groups):
            yl = pick(g * size)
            new.append(vec[g] + yl * dl)
            b = yl * root
            bl_s[pl.ds(pl.multiple_of(l * members + g * size, size), size), :] = b
            bk_s[pl.ds(g * size * order + l, size, stride=order), :] = b
        return tuple(new)

    zero = jnp.zeros((size, LANES), F32)
    vec = lax.fori_loop(0, order, gather, tuple([zero] * groups))

    def row_of(ref, r):
        return jnp.broadcast_to(ref[pl.ds(r, 1), :], (size, LANES))

    def symmetric(count, left, right, left_step, finish):
        for a in range(nb):
            width = nb - a

            def body(k, acc):
                rhs = [
                    right[pl.ds(pl.multiple_of(k * order + (a + j) * size, size), size), :]
                    for j in range(width)
                ]
                out = []
                for i in range(size):
                    lhs = row_of(left, k * left_step + a * size + i)
                    for j in range(width):
                        out.append(acc[i * width + j] + lhs * rhs[j])
                return tuple(out)

            acc = lax.fori_loop(0, count, body, tuple([zero] * (size * width)), unroll=2)
            for i in range(size):
                for j in range(width):
                    finish(a * size + i, a + j, acc[i * width + j])

    def at(ref, i, jb):
        return ref[pl.ds(i * order + jb * size, size), :]

    def put(ref, i, jb, value):
        ref[pl.ds(i * order + jb * size, size), :] = value
        if jb != i // size:
            ref[pl.ds(jb * size * order + i, size, stride=order), :] = value

    symmetric(members, bk_s, bk_s, order, lambda i, jb, v: put(g_s, i, jb, v))

    square, trace = zero, zero
    for i in range(order):
        for jb in range(nb):
            g = at(g_s, i, jb)
            square = square + g * g
            if jb == i // size:
                trace = trace + jnp.where(sub == i % size, g, 0.0)
    base = members - 1.0
    total = (
        base * base * members
        + 2.0 * base * jnp.sum(trace, axis=0, keepdims=True)
        + jnp.sum(square, axis=0, keepdims=True)
    )
    scale = jnp.sqrt(total)
    inv = 1.0 / scale
    a_coef = full(base * inv)

    z = 1.5 - 0.5 * a_coef
    for i in range(order):
        for jb in range(nb):
            g = at(g_s, i, jb) * inv
            g_s[pl.ds(i * order + jb * size, size), :] = g
            if jb == i // size:
                here = sub == i % size
                m = jnp.where(here, -0.5, 0.0)
                r = jnp.where(here, z, 0.0) - 0.5 * g
            else:
                m = zero
                r = -0.5 * g
            m_s[pl.ds(i * order + jb * size, size), :] = m
            r_s[pl.ds(i * order + jb * size, size), :] = r
            q_s[pl.ds(i * order + jb * size, size), :] = a_coef * m + r

    for it in range(1, NS_ITERS):
        last = it == NS_ITERS - 1
        t = 1.5 - 0.5 * a_coef * z * z

        def tmat(i, jb, v):
            q, r = at(q_s, i, jb), at(r_s, i, jb)
            put(t_s, i, jb, -0.5 * (v + z * (q - r)))

        symmetric(order, q_s, r_s, order, tmat)

        def mmat(i, jb, v):
            put(m_s, i, jb, t * at(m_s, i, jb) + v)

        symmetric(order, r_s, t_s, order, mmat)
        z = t * z
        if not last:

            def rmat(i, jb, v):
                if jb == i // size:
                    v = v + jnp.where(sub == i % size, z, 0.0)
                put(r_s, i, jb, v)
                put(q_s, i, jb, a_coef * at(m_s, i, jb) + v)

            symmetric(order, g_s, m_s, order, rmat)

    root = full(lax.rsqrt(scale))
    for i in range(order):
        for jb in range(nb):
            m_s[pl.ds(i * order + jb * size, size), :] = at(m_s, i, jb) * inv

    def cmat(l, carry):
        acc = [zero] * groups
        for k in range(order):
            lhs = row_of(m_s, l * order + k)
            for g in range(groups):
                acc[g] = acc[g] + lhs * bl_s[pl.ds(k * members + g * size, size), :]
        for g in range(groups):
            c_s[pl.ds(pl.multiple_of(l * members + g * size, size), size), :] = acc[g]
        return carry

    lax.fori_loop(0, order, cmat, 0)

    def smat_times(vector):
        for g in range(groups):
            t_s[pl.ds(g * size, size), :] = vector[g]
        down = [zero] * nb
        for k in range(members):
            v = row_of(t_s, k)
            for j in range(nb):
                down[j] = down[j] + v * bk_s[pl.ds(k * order + j * size, size), :]
        for j in range(nb):
            t_s[pl.ds(members + j * size, size), :] = down[j]
        up = [z * vector[g] for g in range(groups)]
        for l in range(order):
            u = row_of(t_s, members + l)
            for g in range(groups):
                up[g] = up[g] + u * c_s[pl.ds(l * members + g * size, size), :]
        return [root * up[g] for g in range(groups)]

    wbar = smat_times(smat_times(vec))
    for g in range(groups):
        t_s[pl.ds(g * size, size), :] = wbar[g]

    gain = full(jnp.float32(base) ** 0.5 * root)

    def vmat(k, carry):
        acc = [zero] * groups
        for l in range(order):
            lhs = row_of(bk_s, k * order + l)
            for g in range(groups):
                acc[g] = acc[g] + lhs * c_s[pl.ds(l * members + g * size, size), :]
        for g in range(groups):
            here = sub + g * size == k
            s = acc[g] + jnp.where(here, z, 0.0)
            v = gain * s + t_s[pl.ds(g * size, size), :] - jnp.where(here, 1.0, 0.0)
            v_s[pl.ds(pl.multiple_of(k * members + g * size, size), size), :] = v
        return carry

    lax.fori_loop(0, members, vmat, 0)

    half = members // 2

    def turn(k, carry):
        both = jnp.concatenate(
            [
                v_s[pl.ds(pl.multiple_of(k * members, members), members), :],
                v_s[pl.ds(pl.multiple_of((k + half) * members, members), members), :],
            ],
            axis=0,
        )
        w_s[pl.ds(pl.multiple_of(k * LANES, LANES), LANES), :] = jnp.transpose(both)
        return carry

    lax.fori_loop(0, half, turn, 0)

    def apply(pair, carry):
        region, place = pair // (size // 2), pair % (size // 2)
        start = pl.multiple_of(place * 2 * size, 2 * size)
        blocks = [
            ens_ref[g, region, pl.ds(start, 2 * size), :].astype(F32) for g in range(groups)
        ]
        outs = []
        for second in range(2):
            x = jnp.concatenate(
                [b[second * size : (second + 1) * size] for b in blocks], axis=0
            )
            x = (x - jnp.mean(x, axis=0, keepdims=True)).astype(BF16)
            gap = jnp.zeros_like(x)
            rhs = jnp.concatenate(
                [jnp.concatenate([x, gap], axis=1), jnp.concatenate([gap, x], axis=1)], axis=0
            )
            lhs = w_s[pl.ds(pair * 2 + second, half, stride=LANES), :].astype(BF16)
            outs.append(dot(lhs, rhs))
        for g in range(groups):
            top, side = g * size % half, g * size // half
            piece = [
                o[top : top + size, side * LANES : (side + 1) * LANES] for o in outs
            ]
            inc_ref[g, region, pl.ds(start, 2 * size), :] = jnp.concatenate(
                piece, axis=0
            ).astype(BF16)
        return carry

    lax.fori_loop(0, regions * size // 2, apply, 0, unroll=2)


def analyse(before, own, after, nbr, loc, ens):
    order, points = nbr.shape
    members = ens.shape[0] * 8
    panels = 3 * own.shape[1] // LANES
    small = pltpu.VMEM((order * order, LANES), F32)
    tall = pltpu.VMEM((order * members, LANES), F32)
    return pl.pallas_call(
        analyse_kernel,
        out_shape=jax.ShapeDtypeStruct(ens.shape, BF16),
        in_specs=[VM] * 6,
        out_specs=VM,
        scratch_shapes=[
            pltpu.VMEM((panels, members + 16, LANES), F32),
            tall,
            tall,
            small,
            small,
            small,
            small,
            small,
            tall,
            pltpu.VMEM((members * members, LANES), F32),
            pltpu.VMEM((members // 2 * LANES, LANES), F32),
        ],
        compiler_params=pltpu.CompilerParams(vmem_limit_bytes=56 * 2**20),
        name="analyse",
    )(before, own, after, nbr, loc, ens)


def finish_kernel(fore_ref, inc_ref, out_ref, sum_s):
    members, grid_r, _ = out_ref.shape
    tiles, rows, _ = fore_ref.shape

    def add(t, carry):
        sum_s[pl.ds(pl.multiple_of(t * rows, rows), rows), :] = fore_ref[t].astype(F32) + inc_ref[
            t
        ].astype(F32)
        return carry

    lax.fori_loop(0, tiles, add, 0, unroll=4)
    for k in range(members):
        out_ref[k] = sum_s[pl.ds(k, grid_r, stride=members), :].astype(BF16)


def finish(fore, inc, members):
    tiles, rows, _ = fore.shape
    grid_r = tiles * rows // members
    return pl.pallas_call(
        finish_kernel,
        out_shape=jax.ShapeDtypeStruct((members, grid_r, LANES), BF16),
        in_specs=[VM, VM],
        out_specs=VM,
        scratch_shapes=[pltpu.VMEM((tiles * rows, LANES), F32)],
        compiler_params=pltpu.CompilerParams(vmem_limit_bytes=40 * 2**20),
        name="finish",
    )(fore, inc)


def neighbours(last, first, axis, wrap):
    count = lax.axis_size(axis)
    up = [(i, (i + 1) % count) for i in range(count if wrap else count - 1)]
    down = [(j, i) for i, j in up]
    return lax.ppermute(last, axis, up), lax.ppermute(first, axis, down)


def exchange(blocks):
    return lax.all_to_all(blocks, MR, split_axis=0, concat_axis=0, tiled=True)


def shards(
    latent_vertex_values,
    background_field,
    edge_senders,
    grid_parent,
    w_send,
    w_recv,
    w_node,
    w_agg,
    w_out,
    norm_gain,
    w_dec,
    obs_loc,
    obs_count,
    obs_value,
    obs_var,
    obs_nbr,
    loc_weight,
):
    members = latent_vertex_values.shape[0]
    groups, regions = lax.axis_size("member"), lax.axis_size("region")
    before, after = neighbours(
        latent_vertex_values[:, -RIM:], latent_vertex_values[:, :RIM], "region", True
    )
    weights = (w_send, w_recv, w_node, w_agg, w_out, norm_gain[None], w_dec)
    processed, fore = forecast(
        latent_vertex_values, before, after, background_field, edge_senders, grid_parent, weights
    )
    ens = exchange(fore)
    ens = ens.reshape(groups, regions, *ens.shape[1:])
    payload = observe(ens, obs_loc, obs_count, obs_value, obs_var)
    pay_before, pay_after = neighbours(payload, payload, MR, False)
    inc = analyse(pay_before, payload, pay_after, obs_nbr, loc_weight, ens)
    landed = exchange(inc.reshape(groups * regions, *inc.shape[2:]))
    return processed, finish(fore, landed, members)


def solution(mesh):
    in_specs = (
        P("member", "region", None),
        P("member", "region", None),
        P("region", None),
        P("region"),
        P(),
        P(),
        P(),
        P(),
        P(),
        P(),
        P(),
        P(MR),
        P(MR),
        P(MR),
        P(MR),
        P(None, MR),
        P(None, MR),
    )
    out_specs = (P("member", "region", None), P("member", "region", None))
    return jax.shard_map(shards, mesh=mesh, in_specs=in_specs, out_specs=out_specs, check_vma=False)
```

time: 731 us -> 227 us (0.31); the launches traced: 721 us -> 227 us
  local copies, waits for them, and re-layouts: 301 us -> 3.67 us
  matrix products: 151 us -> 0 us
  Pallas kernels: 0 us -> 118 us
  other arithmetic: 83.6 us -> 0.6 us
  waiting for transfers between devices: 123 us -> 40.9 us
    gather x21 -> x0, local copies, waits for them, and re-layouts: 191 us -> none  [the longest x8 106 us: propagate_dynamics(): gathered = rows[edge_senders]]
    dot_general x55 -> x0, matrix products: 151 us -> none  [the longest x6 34.7 us: transform(): jnp.einsum('ijp,jkp->ikp', zmat, ymat, precision=hp)]
    pallas_call x0 -> x4, Pallas kernels: none -> 118 us  [the longest x1 53.5 us: forecast(): pl.pallas_call(forecast_kernel, out_shape=(jax.ShapeDtypeStruct(latent.sh...]
    ppermute x4, waiting for transfers between devices: 94 us -> 11.3 us  [neighbours(): return (lax.ppermute(last, axis, up), lax.ppermute(first, axis, down))]
    convert_element_type x10 -> x0, local copies, waits for them, and re-layouts: 56.8 us -> none  [the longest x8 53.6 us: propagate_dynamics(): gathered.astype(jnp.float32) + recv[:, None, :]]
    reduce_sum x18 -> x0, other arithmetic: 53.4 us -> none  [the longest x8 51.5 us: propagate_dynamics(): jnp.sum(jax.nn.silu(gathered.astype(jnp.float32) + recv[:, None, :]), axi...]
    dynamic_update_slice x8 -> x0, other arithmetic: 13.7 us -> none  [shards(): lax.map(propagate_dynamics, (latent_vertex_values, extended, background_f...]
    squeeze x8 -> x0, local copies, waits for them, and re-layouts: 12.1 us -> none  [shards(): lax.map(propagate_dynamics, (latent_vertex_values, extended, background_f...]
where the time goes in v1:
time: 227 us
  Pallas kernels  118 us (52%)
  waiting for transfers between devices  40.9 us (18%)
  blocking collectives  38.9 us (17%)
  starting transfers between devices  23.1 us (10%)
  local copies, waits for them, and re-layouts  3.67 us (2%)
    pallas_call x1, Pallas kernels, forecast(): pl.pallas_call(forecast_kernel, out_shape=(jax.ShapeDtypeStruct(latent.sh...  53.5 us
    pallas_call x1, Pallas kernels, analyse(): pl.pallas_call(analyse_kernel, out_shape=jax.ShapeDtypeStruct(ens.shape,...  49.1 us
    all_to_all x1, blocking collectives, exchange(): return lax.all_to_all(blocks, MR, split_axis=0, concat_axis=0, tiled=True)  38.9 us
    all_to_all x1, waiting for transfers between devices, exchange(): return lax.all_to_all(blocks, MR, split_axis=0, concat_axis=0, tiled=True)  29.7 us
    pallas_call x1, Pallas kernels, observe(): pl.pallas_call(observe_kernel, out_shape=jax.ShapeDtypeStruct((groups * 8...  12.6 us
    all_to_all x1, starting transfers between devices, exchange(): return lax.all_to_all(blocks, MR, split_axis=0, concat_axis=0, tiled=True)  11.6 us
    ppermute x4, starting transfers between devices, neighbours(): return (lax.ppermute(last, axis, up), lax.ppermute(first, axis, down))  11.5 us
    ppermute x4, waiting for transfers between devices, neighbours(): return (lax.ppermute(last, axis, up), lax.ppermute(first, axis, down))  11.3 us
  transfers between devices with their start and end apart: 5, of which 4 were waited for; matrix products, arithmetic and copies ran while one was open for 1% of the time, Pallas kernels for 0%

profile of v1, /device:TPU:1, one launch (start us, length us, event | category | flops | bytes accessed | tf_op | source)
XLA Modules:
  0.0 226.6 jit_solution(8890009304687704336)
XLA Ops:
  0.6 0.0 copy-start.10
  0.6 0.0 copy-start.11
  0.6 1.3 fusion
  2.0 1.5 collective-permute-start.1
  3.5 3.0 %collective-permute-start = (bf16[8,64,512]{2,1,0:T(8,128)(2,1)S(1)}, bf16[8,64,512]{2,1,0:T(8,128)(2,1)S(1)}, u32[]{:S(2)}, u32[]{:S(2)}) collective-permute-start(bf16[8,64,512]{2,1,0:T(8,128)(2,1)S(1)} %get-tuple-element.7), channel_id=1, source_target_pairs={{0,1},{1,2},{2,3},{3,4},{4,5},{5,6},{6,7},{7,8},{8,9},{9,10},{10,1... | collective-permute-start | bytes 1572872 | tf_op jit(solution)/shard_map/ppermute | solution.py:508
  6.4 0.0 copy-done.10
  6.4 0.1 copy.19
  6.6 0.8 reshape.13.edge_ref
  7.3 0.0 copy-done.11
  7.3 0.6 broadcast_multiply_fusion.parent_ref
  7.9 5.3 %collective-permute-done.1.after_ref = bf16[8,64,512]{2,1,0:T(8,128)(2,1)S(1)} collective-permute-done((bf16[8,64,512]{2,1,0:T(8,128)(2,1)S(1)}, bf16[8,64,512]{2,1,0:T(8,128)(2,1)S(1)}, u32[]{:S(2)}, u32[]{:S(2)}) %collective-permute-start.1) | collective-permute-done | bytes 524320 | tf_op jit(solution)/shard_map/ppermute | solution.py:508
  13.2 5.0 %collective-permute-done.before_ref = bf16[8,64,512]{2,1,0:T(8,128)(2,1)S(1)} collective-permute-done((bf16[8,64,512]{2,1,0:T(8,128)(2,1)S(1)}, bf16[8,64,512]{2,1,0:T(8,128)(2,1)S(1)}, u32[]{:S(2)}, u32[]{:S(2)}) %collective-permute-start) | collective-permute-done | bytes 524320 | tf_op jit(solution)/shard_map/ppermute | solution.py:508
  18.2 0.0 copy-done.6
  18.2 0.8 copy-done.7
  19.0 53.5 %forecast.1 = (bf16[8,512,512]{2,1,0:T(8,128)(2,1)}, bf16[128,64,128]{2,1,0:T(8,128)(2,1)}) custom-call(s32[3072]{0:T(1024)} %reshape.13.edge_ref, s32[1024]{0:T(1024)} %broadcast_multiply_fusion.parent_ref, bf16[8,512,512]{2,1,0:T(8,128)(2,1)} %latent_ref.1, bf16[8,64,512]{2,1,0:T(8,128)(2,1)} %copy-done.7, bf16[8,64,512]{2,1,0:T(8,128)(2,1)} %copy-done.6, ...), custom_call_target="tpu_custom_call" | custom-call | tf_op jit(solution)/shard_map/forecast/pallas_call | solution.py:121
  72.5 0.0 copy-start.5
  72.5 11.6 %all-to-all-start = ((bf16[128,64,128]{2,1,0:T(8,128)(2,1)}), bf16[128,64,128]{2,1,0:T(8,128)(2,1)S(1)}, u32[]{:S(2)}, u32[]{:S(2)}) async-start(bf16[128,64,128]{2,1,0:T(8,128)(2,1)} %get-tuple-element.5.fore_ref), calls=%async_computation | async-start | bytes 4194304 | tf_op jit(solution)/shard_map/all_to_all | solution.py:512
  84.8 29.7 %all-to-all-done = bf16[128,64,128]{2,1,0:T(8,128)(2,1)S(1)} async-done(((bf16[128,64,128]{2,1,0:T(8,128)(2,1)}), bf16[128,64,128]{2,1,0:T(8,128)(2,1)S(1)}, u32[]{:S(2)}, u32[]{:S(2)}) %all-to-all-start) | async-done | bytes 2097184 | tf_op jit(solution)/shard_map/all_to_all | solution.py:512
  114.4 0.0 copy-done.3
  114.4 0.0 copy-done.5
  114.4 12.6 %observe.1.own_ref = bf16[80,256]{1,0:T(8,128)(2,1)S(1)} custom-call(s32[256]{0:T(256)S(1)} %copy-done.3, s32[1]{0:T(128)S(6)} %copy.20.count_ref, bf16[8,16,64,128]{3,2,1,0:T(8,128)(2,1)S(1)} %bitcast.5, f32[1,256]{1,0:T(1,128)S(1)} %bitcast.7, f32[1,256]{1,0:T(1,128)S(1)} %bitcast.8), custom_call_target="tpu_custom_call" | custom-call | tf_op jit(solution)/shard_map/observe/pallas_call | solution.py:176
  127.1 1.9 collective-permute-start.3
  129.0 5.1 %collective-permute-start.2 = (bf16[80,256]{1,0:T(8,128)(2,1)S(1)}, bf16[80,256]{1,0:T(8,128)(2,1)S(1)}, u32[]{:S(2)}, u32[]{:S(2)}) collective-permute-start(bf16[80,256]{1,0:T(8,128)(2,1)S(1)} %observe.1.own_ref), channel_id=1, source_target_pairs={{0,1},{1,2},{2,3},{3,4},{4,5},{5,6},{6,7},{7,8},{8,9},{9,10},{10,1... | collective-permute-start | bytes 122888 | tf_op jit(solution)/shard_map/ppermute | solution.py:508
  134.2 0.0 collective-permute-done.3.after_ref
  134.2 1.1 collective-permute-done.2.before_ref
  135.2 0.0 copy-done
  135.3 0.0 copy-done.8
  135.3 0.6 copy-done.9
  135.9 49.1 %analyse.1 = bf16[8,16,64,128]{3,2,1,0:T(8,128)(2,1)} custom-call(bf16[80,256]{1,0:T(8,128)(2,1)} %copy-done.9, bf16[80,256]{1,0:T(8,128)(2,1)} %copy-done.2, bf16[80,256]{1,0:T(8,128)(2,1)} %copy-done.8, s32[32,128]{1,0:T(8,128)} %nbr_ref.1, f32[32,128]{1,0:T(8,128)} %loc_ref.3, bf16[8,16,64,128]{3,2,1,0:T(8,128)(2,1)} %bitcast.6), custom_call_target="tpu_custom_call" | custom-call | tf_op jit(solution)/shard_map/analyse/pallas_call | solution.py:452
  184.9 38.9 %all_to_all.10.inc_ref = bf16[128,64,128]{2,1,0:T(8,128)(2,1)S(1)} all-to-all(bf16[128,64,128]{2,1,0:T(8,128)(2,1)} %bitcast.9), channel_id=1, replica_groups=mesh['member'=8,'region'=16] {'member','region'}, dimensions={0} | all-to-all | bytes 4194304 | tf_op jit(solution)/shard_map/all_to_all | solution.py:512
  223.8 0.0 copy-done.1
  223.8 2.8 %finish.1 = bf16[8,1024,128]{2,1,0:T(8,128)(2,1)} custom-call(bf16[128,64,128]{2,1,0:T(8,128)(2,1)S(1)} %copy-done.1, bf16[128,64,128]{2,1,0:T(8,128)(2,1)S(1)} %all_to_all.10.inc_ref), custom_call_target="tpu_custom_call" | custom-call | tf_op jit(solution)/shard_map/finish/pallas_call | solution.py:493
  (12 shorter events, 0.0 us)
Async XLA Ops:
  0.6 5.8 %copy-start.10 = (s32[512,6]{0,1:T(8,128)S(1)}, s32[512,6]{0,1:T(8,128)}, u32[]{:S(2)}) copy-start(s32[512,6]{0,1:T(8,128)} %param.19) | copy-start | bytes 36868
  0.6 6.7 %copy-start.11 = (s32[1024]{0:T(1024)S(1)}, s32[1024]{0:T(1024)}, u32[]{:S(2)}) copy-start(s32[1024]{0:T(1024)} %param.20) | copy-start | bytes 12292
  2.0 11.2 %collective-permute-start.1 = (bf16[8,64,512]{2,1,0:T(8,128)(2,1)S(1)}, bf16[8,64,512]{2,1,0:T(8,128)(2,1)S(1)}, u32[]{:S(2)}, u32[]{:S(2)}) collective-permute-start(bf16[8,64,512]{2,1,0:T(8,128)(2,1)S(1)} %get-tuple-element.6), channel_id=1, source_target_pairs={{1,0},{2,1},{3,2},{4,3},{5,4},{6,5},{7,6},{8,7},{9,8},{10,9},{11,1... | collective-permute-start | bytes 1572872 | tf_op jit(solution)/shard_map/ppermute | solution.py:508
  3.5 14.7 %collective-permute-start = (bf16[8,64,512]{2,1,0:T(8,128)(2,1)S(1)}, bf16[8,64,512]{2,1,0:T(8,128)(2,1)S(1)}, u32[]{:S(2)}, u32[]{:S(2)}) collective-permute-start(bf16[8,64,512]{2,1,0:T(8,128)(2,1)S(1)} %get-tuple-element.7), channel_id=1, source_target_pairs={{0,1},{1,2},{2,3},{3,4},{4,5},{5,6},{6,7},{7,8},{8,9},{9,10},{10,1... | collective-permute-start | bytes 1572872 | tf_op jit(solution)/shard_map/ppermute | solution.py:508
  13.2 5.0 %copy-start.6 = (bf16[8,64,512]{2,1,0:T(8,128)(2,1)}, bf16[8,64,512]{2,1,0:T(8,128)(2,1)S(1)}, u32[]{:S(2)}) copy-start(bf16[8,64,512]{2,1,0:T(8,128)(2,1)S(1)} %collective-permute-done.1.after_ref) | copy-start | bytes 1572868
  18.2 0.8 copy-start.7
  72.5 41.9 %copy-start.3 = (s32[256]{0:T(256)S(1)}, s32[256]{0:T(256)}, u32[]{:S(2)}) copy-start(s32[256]{0:T(256)} %loc_ref.2) | copy-start | bytes 3076
  72.5 41.9 %copy-start.4 = (f32[256]{0:T(256)S(1)}, f32[256]{0:T(256)}, u32[]{:S(2)}) copy-start(f32[256]{0:T(256)} %param.30) | copy-start | bytes 3076
  72.5 41.9 %copy-start.5 = (f32[256]{0:T(256)S(1)}, f32[256]{0:T(256)}, u32[]{:S(2)}) copy-start(f32[256]{0:T(256)} %param.31) | copy-start | bytes 3076
  72.5 41.9 %all-to-all-start = ((bf16[128,64,128]{2,1,0:T(8,128)(2,1)}), bf16[128,64,128]{2,1,0:T(8,128)(2,1)S(1)}, u32[]{:S(2)}, u32[]{:S(2)}) async-start(bf16[128,64,128]{2,1,0:T(8,128)(2,1)} %get-tuple-element.5.fore_ref), calls=%async_computation | async-start | bytes 4194304 | tf_op jit(solution)/shard_map/all_to_all | solution.py:512
  114.4 20.8 %copy-start = (bf16[128,64,128]{2,1,0:T(8,128)(2,1)}, bf16[128,64,128]{2,1,0:T(8,128)(2,1)S(1)}, u32[]{:S(2)}) copy-start(bf16[128,64,128]{2,1,0:T(8,128)(2,1)S(1)} %all-to-all-done) | copy-start | bytes 6291460
  127.1 8.2 %copy-start.2 = (bf16[80,256]{1,0:T(8,128)(2,1)}, bf16[80,256]{1,0:T(8,128)(2,1)S(1)}, u32[]{:S(2)}) copy-start(bf16[80,256]{1,0:T(8,128)(2,1)S(1)} %observe.1.own_ref) | copy-start | bytes 122884
  127.1 7.1 %collective-permute-start.3 = (bf16[80,256]{1,0:T(8,128)(2,1)S(1)}, bf16[80,256]{1,0:T(8,128)(2,1)S(1)}, u32[]{:S(2)}, u32[]{:S(2)}) collective-permute-start(bf16[80,256]{1,0:T(8,128)(2,1)S(1)} %observe.1.own_ref), channel_id=1, source_target_pairs={{1,0},{2,1},{3,2},{4,3},{5,4},{6,5},{7,6},{8,7},{9,8},{10,9},{11,1... | collective-permute-start | bytes 122888 | tf_op jit(solution)/shard_map/ppermute | solution.py:508
  129.0 6.2 %collective-permute-start.2 = (bf16[80,256]{1,0:T(8,128)(2,1)S(1)}, bf16[80,256]{1,0:T(8,128)(2,1)S(1)}, u32[]{:S(2)}, u32[]{:S(2)}) collective-permute-start(bf16[80,256]{1,0:T(8,128)(2,1)S(1)} %observe.1.own_ref), channel_id=1, source_target_pairs={{0,1},{1,2},{2,3},{3,4},{4,5},{5,6},{6,7},{7,8},{8,9},{9,10},{10,1... | collective-permute-start | bytes 122888 | tf_op jit(solution)/shard_map/ppermute | solution.py:508
  134.2 1.1 copy-start.8
  135.3 0.6 copy-start.9
  184.9 38.9 %copy-start.1 = (bf16[128,64,128]{2,1,0:T(8,128)(2,1)S(1)}, bf16[128,64,128]{2,1,0:T(8,128)(2,1)}, u32[]{:S(2)}) copy-start(bf16[128,64,128]{2,1,0:T(8,128)(2,1)} %get-tuple-element.5.fore_ref) | copy-start | bytes 6291460

commit v2 on v1

--- a/solution.py
+++ b/solution.py
@@ -1,3 +1,5 @@
+import functools
+
 import jax
 import jax.numpy as jnp
 from jax import lax
@@ -8,6 +10,10 @@
 NS_ITERS = 6
 LANES = 128
 RIM = 64
+MEMBERS = 8
+GROUP = 8
+CHUNKS = 4
+UNROLL = 8
 F32 = jnp.float32
 BF16 = jnp.bfloat16
 MR = ("member", "region")
@@ -22,119 +28,177 @@
 def forecast_kernel(
     edge_ref,
     parent_ref,
-    latent_ref,
-    before_ref,
-    after_ref,
-    back_ref,
+    latent_hbm,
+    rim_ref,
+    back_hbm,
     w_send_ref,
     w_recv_ref,
-    w_node_ref,
-    w_agg_ref,
-    w_out_ref,
+    w_node_hbm,
+    w_agg_hbm,
+    w_out_hbm,
     gain_ref,
-    w_dec_ref,
-    proc_ref,
-    fore_ref,
+    w_dec_hbm,
+    proc_hbm,
+    fore_hbm,
     send_s,
     recv_s,
     dec_s,
+    latent_s,
     back_s,
+    proc_s,
+    fore_s,
+    w_node_s,
+    w_agg_s,
+    w_out_s,
+    w_dec_s,
+    in_sem,
+    out_sem,
 ):
-    members, nodes, width = latent_ref.shape
+    members = MEMBERS
+    count, width = latent_hbm.shape
+    nodes = count // members
+    rim = rim_ref.shape[0] // 2
+    degree = edge_ref.shape[0] // nodes
+    rows = count // CHUNKS
+    tile = members * GROUP
+
+    def piece(c):
+        return pl.ds(pl.multiple_of(c * rows, rows), rows)
+
+    loads = [
+        pltpu.make_async_copy(latent_hbm.at[piece(c)], latent_s.at[piece(c)], in_sem.at[c])
+        for c in range(CHUNKS)
+    ]
+    later = [
+        pltpu.make_async_copy(src, dst, in_sem.at[CHUNKS + i])
+        for i, (src, dst) in enumerate(
+            [
+                (w_node_hbm, w_node_s),
+                (w_agg_hbm, w_agg_s),
+                (w_out_hbm, w_out_s),
+                (w_dec_hbm, w_dec_s),
+                (back_hbm, back_s),
+            ]
+        )
+    ]
+    for copy in loads + later:
+        copy.start()
+
+    def send_of(state):
+        return dot(state, w_send_ref[...]).astype(BF16).astype(F32) * 0.5
+
     cols = width // LANES
-    step = cols * members
-    rim = before_ref.shape[1]
-    degree = edge_ref.shape[0] // nodes
-    grid_r = back_ref.shape[1]
-
-    def scatter_rows(ref, first, member, values):
+
+    def spread_rows(ref, first, values):
         for c in range(cols):
-            ref[pl.ds(first * step + c * members + member, values.shape[0], stride=step), :] = (
-                values[:, c * LANES : (c + 1) * LANES]
-            )
-
-    def project(m, carry):
-        state = latent_ref[m]
-        own = dot(state, w_send_ref[...]).astype(BF16).astype(F32) * 0.5
-        scatter_rows(send_s, rim, m, own)
-        edge = dot(before_ref[m], w_send_ref[...]).astype(BF16).astype(F32) * 0.5
-        scatter_rows(send_s, 0, m, edge)
-        edge = dot(after_ref[m], w_send_ref[...]).astype(BF16).astype(F32) * 0.5
-        scatter_rows(send_s, rim + nodes, m, edge)
-        scatter_rows(recv_s, 0, m, dot(state, w_recv_ref[...]) * 0.5)
-        back_s[pl.ds(m, grid_r, stride=members), :] = back_ref[m].astype(F32)
-        return carry
-
-    lax.fori_loop(0, members, project, 0)
+            part = values[:, c * LANES : (c + 1) * LANES].reshape(-1, members, LANES)
+            ref[first // members : first // members + part.shape[0], c] = part
+
+    spread_rows(send_s, 0, send_of(rim_ref[0:rim]))
+    spread_rows(send_s, rim + count, send_of(rim_ref[rim : 2 * rim]))
+    for c in range(CHUNKS):
+        loads[c].wait()
+        state = latent_s[c * rows : (c + 1) * rows]
+        spread_rows(send_s, rim + c * rows, send_of(state))
+        spread_rows(recv_s, c * rows, dot(state, w_recv_ref[...]) * 0.5)
 
     def aggregate(n, carry):
-        mine = recv_s[pl.ds(pl.multiple_of(n * step, step), step), :]
+        mine = recv_s[n]
         total = jnp.zeros_like(mine)
         for e in range(degree):
-            row = pl.multiple_of(edge_ref[n * degree + e], step)
-            half = send_s[pl.ds(row, step), :] + mine
+            half = send_s[edge_ref[n * degree + e]] + mine
             total = total + (half + half * jnp.tanh(half))
-        recv_s[pl.ds(pl.multiple_of(n * step, step), step), :] = total
+        recv_s[n] = total
         return carry
 
-    lax.fori_loop(0, nodes, aggregate, 0, unroll=4)
-
-    def update(m, carry):
-        state = latent_ref[m]
+    lax.fori_loop(0, nodes, aggregate, 0, unroll=8)
+    for copy in later:
+        copy.wait()
+
+    def store_proc(c):
+        return pltpu.make_async_copy(proc_s.at[piece(c)], proc_hbm.at[piece(c)], out_sem.at[c])
+
+    def update(c, carry):
+        state = latent_s[piece(c)]
+        some_nodes = pl.ds(c * (rows // members), rows // members)
         agg = jnp.concatenate(
-            [recv_s[pl.ds(c * members + m, nodes, stride=step), :] for c in range(cols)], axis=1
+            [recv_s[some_nodes, i].reshape(rows, LANES) for i in range(cols)], axis=1
         ).astype(BF16)
-        pre = (dot(state, w_node_ref[...]) + dot(agg, w_agg_ref[...])) * 0.5
+        pre = (dot(state, w_node_s[...]) + dot(agg, w_agg_s[...])) * 0.5
         hidden = (pre + pre * jnp.tanh(pre)).astype(BF16)
-        out = dot(hidden, w_out_ref[...])
+        out = dot(hidden, w_out_s[...])
         mean = jnp.mean(out, axis=-1, keepdims=True)
         centred = out - mean
         var = jnp.mean(centred * centred, axis=-1, keepdims=True)
         norm = centred * lax.rsqrt(var + 1e-05) * gain_ref[...]
         proc = (state.astype(F32) + norm).astype(BF16)
-        proc_ref[m] = proc
-        dec_s[pl.ds(m, nodes, stride=members), :] = dot(proc, w_dec_ref[...])
+        proc_s[piece(c)] = proc
+        store_proc(c).start()
+        dec_s[piece(c)] = dot(proc, w_dec_s[...])
         return carry
 
-    lax.fori_loop(0, members, update, 0)
-
-    share = fore_ref.shape[1] // members
-
-    def spread(t, carry):
-        rows = [
-            dec_s[pl.ds(pl.multiple_of(parent_ref[t * share + q], members), members), :]
-            for q in range(share)
-        ]
-        fore_ref[t] = (jnp.concatenate(rows, axis=0) + back_s[pl.ds(t * share * members, share * members), :]).astype(BF16)
-        return carry
-
-    lax.fori_loop(0, fore_ref.shape[0], spread, 0, unroll=2)
-
-
-def forecast(latent, before, after, back, senders, parent, weights):
-    members, nodes, width = latent.shape
-    grid_r = back.shape[1]
-    rim = before.shape[1]
-    step = members * width // LANES
+    lax.fori_loop(0, CHUNKS, update, 0)
+
+    tiles = fore_s.shape[0]
+    some = tiles // CHUNKS
+
+    def store_fore(c):
+        span = pl.ds(c * some, some)
+        return pltpu.make_async_copy(fore_s.at[span], fore_hbm.at[span], out_sem.at[CHUNKS + c])
+
+    for c in range(CHUNKS):
+
+        def spread(t, carry):
+            parts = [
+                dec_s[pl.ds(pl.multiple_of(parent_ref[t * GROUP + q], members), members), :]
+                for q in range(GROUP)
+            ]
+            back = back_s[pl.ds(pl.multiple_of(t * tile, tile), tile), :].astype(F32)
+            fore_s[t] = (jnp.concatenate(parts, axis=0) + back).astype(BF16)
+            return carry
+
+        lax.fori_loop(c * some, (c + 1) * some, spread, 0, unroll=4)
+        store_fore(c).start()
+
+    for c in range(CHUNKS):
+        store_proc(c).wait()
+        store_fore(c).wait()
+
+
+def forecast(latent, rims, back, senders, parent, weights):
+    count, width = latent.shape
+    grid_rows = back.shape[0]
+    rim = rims.shape[0] // 2
     tiles = lax.axis_size("member") * lax.axis_size("region")
-    edge = ((senders - (nodes - rim)) * step).reshape(-1)
+    edge = (senders - (count - rim) // MEMBERS).reshape(-1)
+    hbm = pl.BlockSpec(memory_space=pl.ANY)
+    w_shape = pltpu.VMEM(weights[2].shape, BF16)
     return pl.pallas_call(
         forecast_kernel,
         out_shape=(
             jax.ShapeDtypeStruct(latent.shape, BF16),
-            jax.ShapeDtypeStruct((tiles, members * grid_r // tiles, LANES), BF16),
+            jax.ShapeDtypeStruct((tiles, grid_rows // tiles, LANES), BF16),
         ),
-        in_specs=[SM, SM] + [VM] * 11,
-        out_specs=(VM, VM),
+        in_specs=[SM, SM, hbm, VM, hbm, VM, VM, hbm, hbm, hbm, VM, hbm],
+        out_specs=(hbm, hbm),
         scratch_shapes=[
-            pltpu.VMEM(((nodes + 2 * rim) * step, LANES), F32),
-            pltpu.VMEM((nodes * step, LANES), F32),
-            pltpu.VMEM((nodes * members, LANES), F32),
-            pltpu.VMEM((grid_r * members, LANES), F32),
+            pltpu.VMEM(((count + 2 * rim) // MEMBERS, width // LANES, MEMBERS, LANES), F32),
+            pltpu.VMEM((count // MEMBERS, width // LANES, MEMBERS, LANES), F32),
+            pltpu.VMEM((count, LANES), F32),
+            pltpu.VMEM(latent.shape, BF16),
+            pltpu.VMEM(back.shape, BF16),
+            pltpu.VMEM(latent.shape, BF16),
+            pltpu.VMEM((tiles, grid_rows // tiles, LANES), BF16),
+            w_shape,
+            w_shape,
+            w_shape,
+            pltpu.VMEM(weights[6].shape, BF16),
+            pltpu.SemaphoreType.DMA((CHUNKS + 5,)),
+            pltpu.SemaphoreType.DMA((2 * CHUNKS,)),
         ],
-        compiler_params=pltpu.CompilerParams(vmem_limit_bytes=60 * 2**20),
+        compiler_params=pltpu.CompilerParams(vmem_limit_bytes=56 * 2**20),
         name="forecast",
-    )(edge, parent * members, latent, before, after, back, *weights)
+    )(edge, parent * MEMBERS, latent, rims, back, *weights)
 
 
 def observe_kernel(loc_ref, count_ref, ens_ref, value_ref, var_ref, pay_ref):
@@ -159,7 +223,7 @@
             turned = pltpu.roll(block, (i - channel + LANES) % LANES, 1)
             return jnp.where(lane == i, turned, acc)
 
-        yens = lax.fori_loop(0, LANES, take, jnp.zeros((members, LANES), F32), unroll=2)
+        yens = lax.fori_loop(0, LANES, take, jnp.zeros((members, LANES), F32), unroll=8)
         span = slice(part * LANES, (part + 1) * LANES)
         ybar = jnp.mean(yens, axis=0, keepdims=True)
         slot = lax.broadcasted_iota(jnp.int32, (1, LANES), 1) + part * LANES
@@ -248,31 +312,67 @@
         return tuple(new)
 
     zero = jnp.zeros((size, LANES), F32)
-    vec = lax.fori_loop(0, order, gather, tuple([zero] * groups))
+    vec = lax.fori_loop(0, order, gather, tuple([zero] * groups), unroll=2)
 
     def row_of(ref, r):
         return jnp.broadcast_to(ref[pl.ds(r, 1), :], (size, LANES))
 
-    def symmetric(count, left, right, left_step, finish):
+    def accumulate(start, stop, left_row, right, a, acc):
+        width = nb - a
+
+        def body(k, acc):
+            rhs = [
+                right[pl.ds(pl.multiple_of(k * order + (a + j) * size, size), size), :]
+                for j in range(width)
+            ]
+            out = []
+            for i in range(size):
+                lhs = left_row(k, i)
+                for j in range(width):
+                    out.append(acc[i * width + j] + lhs * rhs[j])
+            return tuple(out)
+
+        return lax.fori_loop(start, stop, body, acc, unroll=UNROLL)
+
+    def finish_group(a, acc, finish):
+        width = nb - a
+        for i in range(size):
+            for j in range(width):
+                finish(a * size + i, a + j, acc[i * width + j])
+
+    def gram(ref, count, finish):
         for a in range(nb):
-            width = nb - a
-
-            def body(k, acc):
-                rhs = [
-                    right[pl.ds(pl.multiple_of(k * order + (a + j) * size, size), size), :]
-                    for j in range(width)
-                ]
-                out = []
-                for i in range(size):
-                    lhs = row_of(left, k * left_step + a * size + i)
-                    for j in range(width):
-                        out.append(acc[i * width + j] + lhs * rhs[j])
-                return tuple(out)
-
-            acc = lax.fori_loop(0, count, body, tuple([zero] * (size * width)), unroll=2)
-            for i in range(size):
-                for j in range(width):
-                    finish(a * size + i, a + j, acc[i * width + j])
+            acc = accumulate(
+                0,
+                count,
+                lambda k, i: row_of(ref, k * order + a * size + i),
+                ref,
+                a,
+                tuple([zero] * (size * (nb - a))),
+            )
+            finish_group(a, acc, finish)
+
+    def product(left, right, finish):
+        for a in range(nb):
+            edge = (a + 1) * size
+            acc = accumulate(
+                0,
+                edge,
+                lambda k, i: row_of(left, k * order + a * size + i),
+                right,
+                a,
+                tuple([zero] * (size * (nb - a))),
+            )
+            if edge < order:
+                acc = accumulate(
+                    edge,
+                    order,
+                    lambda k, i: row_of(left, (a * size + i) * order + k),
+                    right,
+                    a,
+                    acc,
+                )
+            finish_group(a, acc, finish)
 
     def at(ref, i, jb):
         return ref[pl.ds(i * order + jb * size, size), :]
@@ -282,15 +382,21 @@
         if jb != i // size:
             ref[pl.ds(jb * size * order + i, size, stride=order), :] = value
 
-    symmetric(members, bk_s, bk_s, order, lambda i, jb, v: put(g_s, i, jb, v))
-
-    square, trace = zero, zero
-    for i in range(order):
-        for jb in range(nb):
-            g = at(g_s, i, jb)
+    def upper(ref, i, jb, value):
+        ref[pl.ds(i * order + jb * size, size), :] = value
+
+    blocks = [(i, jb) for i in range(order) for jb in range(i // size, nb)]
+    gram(bk_s, members, functools.partial(upper, g_s))
+
+    square, cross, trace = zero, zero, zero
+    for i, jb in blocks:
+        g = at(g_s, i, jb)
+        if jb == i // size:
             square = square + g * g
-            if jb == i // size:
-                trace = trace + jnp.where(sub == i % size, g, 0.0)
+            trace = trace + jnp.where(sub == i % size, g, 0.0)
+        else:
+            cross = cross + g * g
+    square = square + 2.0 * cross
     base = members - 1.0
     total = (
         base * base * members
@@ -302,35 +408,35 @@
     a_coef = full(base * inv)
 
     z = 1.5 - 0.5 * a_coef
-    for i in range(order):
-        for jb in range(nb):
-            g = at(g_s, i, jb) * inv
-            g_s[pl.ds(i * order + jb * size, size), :] = g
-            if jb == i // size:
-                here = sub == i % size
-                m = jnp.where(here, -0.5, 0.0)
-                r = jnp.where(here, z, 0.0) - 0.5 * g
-            else:
-                m = zero
-                r = -0.5 * g
-            m_s[pl.ds(i * order + jb * size, size), :] = m
-            r_s[pl.ds(i * order + jb * size, size), :] = r
-            q_s[pl.ds(i * order + jb * size, size), :] = a_coef * m + r
+    for i, jb in blocks:
+        g = at(g_s, i, jb) * inv
+        put(g_s, i, jb, g)
+        m, r = zero, -0.5 * g
+        if jb == i // size:
+            here = sub == i % size
+            m = jnp.where(here, -0.5, 0.0)
+            r = r + jnp.where(here, z, 0.0)
+        upper(m_s, i, jb, m)
+        put(r_s, i, jb, r)
+        upper(q_s, i, jb, a_coef * m + r)
 
     for it in range(1, NS_ITERS):
         last = it == NS_ITERS - 1
         t = 1.5 - 0.5 * a_coef * z * z
 
         def tmat(i, jb, v):
-            q, r = at(q_s, i, jb), at(r_s, i, jb)
-            put(t_s, i, jb, -0.5 * (v + z * (q - r)))
-
-        symmetric(order, q_s, r_s, order, tmat)
+            upper(t_s, i, jb, -0.5 * (v + z * (at(q_s, i, jb) - at(r_s, i, jb))))
+
+        product(q_s, r_s, tmat)
 
         def mmat(i, jb, v):
-            put(m_s, i, jb, t * at(m_s, i, jb) + v)
-
-        symmetric(order, r_s, t_s, order, mmat)
+            m = t * at(m_s, i, jb) + v
+            if last:
+                put(m_s, i, jb, m * inv)
+            else:
+                upper(m_s, i, jb, m)
+
+        product(t_s, r_s, mmat)
         z = t * z
         if not last:
 
@@ -338,26 +444,28 @@
                 if jb == i // size:
                     v = v + jnp.where(sub == i % size, z, 0.0)
                 put(r_s, i, jb, v)
-                put(q_s, i, jb, a_coef * at(m_s, i, jb) + v)
-
-            symmetric(order, g_s, m_s, order, rmat)
+                upper(q_s, i, jb, a_coef * at(m_s, i, jb) + v)
+
+            product(m_s, g_s, rmat)
 
     root = full(lax.rsqrt(scale))
-    for i in range(order):
-        for jb in range(nb):
-            m_s[pl.ds(i * order + jb * size, size), :] = at(m_s, i, jb) * inv
-
-    def cmat(l, carry):
-        acc = [zero] * groups
-        for k in range(order):
-            lhs = row_of(m_s, l * order + k)
-            for g in range(groups):
-                acc[g] = acc[g] + lhs * bl_s[pl.ds(k * members + g * size, size), :]
-        for g in range(groups):
-            c_s[pl.ds(pl.multiple_of(l * members + g * size, size), size), :] = acc[g]
+
+    def cmat(step, carry):
+        for g0 in range(0, groups, 4):
+            acc = [zero] * 16
+            for k in range(order):
+                b = [bl_s[pl.ds(k * members + (g0 + g) * size, size), :] for g in range(4)]
+                for i in range(4):
+                    lhs = row_of(m_s, k * order + step * 4 + i)
+                    for g in range(4):
+                        acc[i * 4 + g] = acc[i * 4 + g] + lhs * b[g]
+            for i in range(4):
+                for g in range(4):
+                    start = (step * 4 + i) * members + (g0 + g) * size
+                    c_s[pl.ds(pl.multiple_of(start, size), size), :] = acc[i * 4 + g]
         return carry
 
-    lax.fori_loop(0, order, cmat, 0)
+    lax.fori_loop(0, order // 4, cmat, 0)
 
     def smat_times(vector):
         for g in range(groups):
@@ -382,20 +490,26 @@
 
     gain = full(jnp.float32(base) ** 0.5 * root)
 
-    def vmat(k, carry):
-        acc = [zero] * groups
-        for l in range(order):
-            lhs = row_of(bk_s, k * order + l)
-            for g in range(groups):
-                acc[g] = acc[g] + lhs * c_s[pl.ds(l * members + g * size, size), :]
-        for g in range(groups):
-            here = sub + g * size == k
-            s = acc[g] + jnp.where(here, z, 0.0)
-            v = gain * s + t_s[pl.ds(g * size, size), :] - jnp.where(here, 1.0, 0.0)
-            v_s[pl.ds(pl.multiple_of(k * members + g * size, size), size), :] = v
+    def vmat(step, carry):
+        for g0 in range(0, groups, 4):
+            acc = [zero] * 16
+            for l in range(order):
+                c = [c_s[pl.ds(l * members + (g0 + g) * size, size), :] for g in range(4)]
+                for i in range(4):
+                    lhs = row_of(bk_s, (step * 4 + i) * order + l)
+                    for g in range(4):
+                        acc[i * 4 + g] = acc[i * 4 + g] + lhs * c[g]
+            for i in range(4):
+                k = step * 4 + i
+                for g in range(4):
+                    here = sub + (g0 + g) * size == k
+                    s = gain * (acc[i * 4 + g] + jnp.where(here, z, 0.0))
+                    v = s + t_s[pl.ds((g0 + g) * size, size), :] - jnp.where(here, 1.0, 0.0)
+                    start = k * members + (g0 + g) * size
+                    v_s[pl.ds(pl.multiple_of(start, size), size), :] = v
         return carry
 
-    lax.fori_loop(0, members, vmat, 0)
+    lax.fori_loop(0, members // 4, vmat, 0)
 
     half = members // 2
 
@@ -440,7 +554,7 @@
             ).astype(BF16)
         return carry
 
-    lax.fori_loop(0, regions * size // 2, apply, 0, unroll=2)
+    lax.fori_loop(0, regions * size // 2, apply, 0, unroll=8)
 
 
 def analyse(before, own, after, nbr, loc, ens):
@@ -531,15 +645,29 @@
     obs_nbr,
     loc_weight,
 ):
-    members = latent_vertex_values.shape[0]
+    members, nodes, width = latent_vertex_values.shape
+    grid_r = background_field.shape[1]
     groups, regions = lax.axis_size("member"), lax.axis_size("region")
+
+    def node_major(array):
+        return array.transpose(1, 0, 2).reshape(-1, array.shape[2])
+
     before, after = neighbours(
-        latent_vertex_values[:, -RIM:], latent_vertex_values[:, :RIM], "region", True
+        node_major(latent_vertex_values[:, -RIM:]),
+        node_major(latent_vertex_values[:, :RIM]),
+        "region",
+        True,
     )
     weights = (w_send, w_recv, w_node, w_agg, w_out, norm_gain[None], w_dec)
     processed, fore = forecast(
-        latent_vertex_values, before, after, background_field, edge_senders, grid_parent, weights
+        node_major(latent_vertex_values),
+        jnp.concatenate([before, after], axis=0),
+        node_major(background_field),
+        edge_senders,
+        grid_parent,
+        weights,
     )
+    processed = processed.reshape(nodes, members, width).transpose(1, 0, 2)
     ens = exchange(fore)
     ens = ens.reshape(groups, regions, *ens.shape[1:])
     payload = observe(ens, obs_loc, obs_count, obs_value, obs_var)

time: 227 us -> 190 us (0.84)
  Pallas kernels: 118 us -> 77.1 us
  blocking collectives: 38.9 us -> 0 us
  waiting for transfers between devices: 40.9 us -> 63.8 us
  local copies, waits for them, and re-layouts: 3.67 us -> 16.4 us
  starting transfers between devices: 23.1 us -> 28.9 us
    all_to_all x1 -> x0, blocking collectives: 38.9 us -> none  [exchange(): return lax.all_to_all(blocks, MR, split_axis=0, concat_axis=0, tiled=True)]
    all_to_all x1 -> x2, waiting for transfers between devices: 29.7 us -> 53.8 us  [exchange(): return lax.all_to_all(blocks, MR, split_axis=0, concat_axis=0, tiled=True)]
    pallas_call x1, Pallas kernels: 53.5 us -> 30.1 us  [forecast(): pl.pallas_call(forecast_kernel, out_shape=(jax.ShapeDtypeStruct(latent.sh...]
    pallas_call x1, Pallas kernels: 49.1 us -> 34.9 us  [analyse(): pl.pallas_call(analyse_kernel, out_shape=jax.ShapeDtypeStruct(ens.shape,...]
    transpose x0 -> x5, local copies, waits for them, and re-layouts: none -> 9.11 us  [node_major(): return array.transpose(1, 0, 2).reshape(-1, array.shape[2])]
    all_to_all x1 -> x2, starting transfers between devices: 11.6 us -> 18.7 us  [exchange(): return lax.all_to_all(blocks, MR, split_axis=0, concat_axis=0, tiled=True)]
    reshape x1 -> x2, local copies, waits for them, and re-layouts: 0.77 us -> 6.52 us  [the longest x1 5.75 us: shards(): processed = processed.reshape(nodes, members, width).transpose(1, 0, 2)]
    pallas_call x1, Pallas kernels: 12.6 us -> 7.65 us  [observe(): pl.pallas_call(observe_kernel, out_shape=jax.ShapeDtypeStruct((groups * 8...]
  transfers between devices with their start and end apart: 5 -> 6, of which waited for: 4 -> 5; matrix products, arithmetic and copies ran while one was open for 1% -> 8% of each run, Pallas kernels for 0% -> 0%
where the time goes in v2:
time: 190 us; the launch traced here: 189 us
  Pallas kernels  77.1 us (41%)
  waiting for transfers between devices  63.8 us (34%)
  starting transfers between devices  28.9 us (15%)
  local copies, waits for them, and re-layouts  16.4 us (9%)
    all_to_all x2, waiting for transfers between devices, exchange(): return lax.all_to_all(blocks, MR, split_axis=0, concat_axis=0, tiled=True)  53.8 us
    pallas_call x1, Pallas kernels, analyse(): pl.pallas_call(analyse_kernel, out_shape=jax.ShapeDtypeStruct(ens.shape,...  34.9 us
    pallas_call x1, Pallas kernels, forecast(): pl.pallas_call(forecast_kernel, out_shape=(jax.ShapeDtypeStruct(latent.sh...  30.1 us
    all_to_all x2, starting transfers between devices, exchange(): return lax.all_to_all(blocks, MR, split_axis=0, concat_axis=0, tiled=True)  18.7 us
    ppermute x4, starting transfers between devices, neighbours(): return (lax.ppermute(last, axis, up), lax.ppermute(first, axis, down))  10.2 us
    ppermute x4, waiting for transfers between devices, neighbours(): return (lax.ppermute(last, axis, up), lax.ppermute(first, axis, down))  9.94 us
    transpose x5, local copies, waits for them, and re-layouts, node_major(): return array.transpose(1, 0, 2).reshape(-1, array.shape[2])  9.11 us
    pallas_call x1, Pallas kernels, observe(): pl.pallas_call(observe_kernel, out_shape=jax.ShapeDtypeStruct((groups * 8...  7.65 us
  transfers between devices with their start and end apart: 6, of which 5 were waited for; matrix products, arithmetic and copies ran while one was open for 8% of the time, Pallas kernels for 0%

profile of v2, /device:TPU:1, one launch (start us, length us, event | category | flops | bytes accessed | tf_op | source)
XLA Modules:
  0.0 189.3 jit_solution(9104372526996562184)
XLA Ops:
  0.6 1.4 slice_bitcast_fusion.1
  2.1 0.3 copy.39
  2.4 4.4 %collective-permute-start = (bf16[512,512]{1,0:T(8,128)(2,1)S(1)}, bf16[512,512]{1,0:T(8,128)(2,1)S(1)}, u32[]{:S(2)}, u32[]{:S(2)}) collective-permute-start(bf16[512,512]{1,0:T(8,128)(2,1)S(1)} %bitcast.38), channel_id=1, source_target_pairs={{0,1},{1,2},{2,3},{3,4},{4,5},{5,6},{6,7},{7,8},{8,9},{9,10},{10,1... | collective-permute-start | bytes 1572872 | tf_op jit(solution)/shard_map/ppermute | solution.py:622
  6.8 0.3 copy.38
  7.1 0.1 collective-permute-start.1
  7.2 0.0 copy-start.7
  7.2 4.4 %copy.36 = bf16[512,8,512]{2,1,0:T(8,128)(2,1)} copy(bf16[512,8,512]{2,0,1:T(8,128)(2,1)S(1)} %bitcast.34) | data formatting | bytes 8388608 | tf_op jit(solution)/shard_map/transpose | solution.py:653
  11.6 2.7 %copy.37 = bf16[1024,8,128]{2,1,0:T(8,128)(2,1)} copy(bf16[1024,8,128]{2,0,1:T(8,128)(2,1)S(1)} %bitcast.37) | data formatting | bytes 4194304 | tf_op jit(solution)/shard_map/transpose | solution.py:653
  14.3 0.1 copy.24
  14.4 0.8 reshape.28.edge_ref
  15.2 0.6 broadcast_multiply_fusion.parent_ref
  15.8 2.7 %collective-permute-done = bf16[512,512]{1,0:T(8,128)(2,1)S(1)} collective-permute-done((bf16[512,512]{1,0:T(8,128)(2,1)S(1)}, bf16[512,512]{1,0:T(8,128)(2,1)S(1)}, u32[]{:S(2)}, u32[]{:S(2)}) %collective-permute-start) | collective-permute-done | bytes 524320 | tf_op jit(solution)/shard_map/ppermute | solution.py:622
  18.5 2.5 %collective-permute-done.1 = bf16[512,512]{1,0:T(8,128)(2,1)S(1)} collective-permute-done((bf16[512,512]{1,0:T(8,128)(2,1)S(1)}, bf16[512,512]{1,0:T(8,128)(2,1)S(1)}, u32[]{:S(2)}, u32[]{:S(2)}) %collective-permute-start.1) | collective-permute-done | bytes 524320 | tf_op jit(solution)/shard_map/ppermute | solution.py:622
  21.0 1.0 pad_maximum_fusion.rim_ref
  22.1 30.1 %forecast.1 = (bf16[4096,512]{1,0:T(8,128)(2,1)}, bf16[128,64,128]{2,1,0:T(8,128)(2,1)}) custom-call(s32[3072]{0:T(1024)} %reshape.28.edge_ref, s32[1024]{0:T(1024)} %broadcast_multiply_fusion.parent_ref, bf16[4096,512]{1,0:T(8,128)(2,1)} %bitcast.31, bf16[1024,512]{1,0:T(8,128)(2,1)} %pad_maximum_fusion.rim_ref, bf16[8192,128]{1,0:T(8,128)(2,1)} %bitcast.33, ...), custom_call_target="tpu_custom_call" | custom-call | tf_op jit(solution)/shard_map/forecast/pallas_call | solution.py:176
  52.2 0.0 copy-start.3
  52.2 0.0 copy-start.4
  52.2 0.0 copy-start.5
  52.2 8.7 %all-to-all-start = ((bf16[128,64,128]{2,1,0:T(8,128)(2,1)}), bf16[128,64,128]{2,1,0:T(8,128)(2,1)S(1)}, u32[]{:S(2)}, u32[]{:S(2)}) async-start(bf16[128,64,128]{2,1,0:T(8,128)(2,1)} %get-tuple-element.5.fore_ref), calls=%async_computation | async-start | bytes 4194304 | tf_op jit(solution)/shard_map/all_to_all | solution.py:626
  61.5 29.7 %all-to-all-done = bf16[128,64,128]{2,1,0:T(8,128)(2,1)S(1)} async-done(((bf16[128,64,128]{2,1,0:T(8,128)(2,1)}), bf16[128,64,128]{2,1,0:T(8,128)(2,1)S(1)}, u32[]{:S(2)}, u32[]{:S(2)}) %all-to-all-start) | async-done | bytes 2097184 | tf_op jit(solution)/shard_map/all_to_all | solution.py:626
  91.2 7.7 %observe.1.own_ref = bf16[80,256]{1,0:T(8,128)(2,1)S(1)} custom-call(s32[256]{0:T(256)S(1)} %copy-done.3, s32[1]{0:T(128)S(6)} %copy.40.count_ref, bf16[8,16,64,128]{3,2,1,0:T(8,128)(2,1)S(1)} %bitcast.27, f32[1,256]{1,0:T(1,128)S(1)} %bitcast.29, f32[1,256]{1,0:T(1,128)S(1)} %bitcast.30), custom_call_target="tpu_custom_call" | custom-call | tf_op jit(solution)/shard_map/observe/pallas_call | solution.py:240
  98.9 3.7 %collective-permute-start.2 = (bf16[80,256]{1,0:T(8,128)(2,1)S(1)}, bf16[80,256]{1,0:T(8,128)(2,1)S(1)}, u32[]{:S(2)}, u32[]{:S(2)}) collective-permute-start(bf16[80,256]{1,0:T(8,128)(2,1)S(1)} %observe.1.own_ref), channel_id=1, source_target_pairs={{0,1},{1,2},{2,3},{3,4},{4,5},{5,6},{6,7},{7,8},{8,9},{9,10},{10,1... | collective-permute-start | bytes 122888 | tf_op jit(solution)/shard_map/ppermute | solution.py:622
  102.6 2.1 %collective-permute-start.3 = (bf16[80,256]{1,0:T(8,128)(2,1)S(1)}, bf16[80,256]{1,0:T(8,128)(2,1)S(1)}, u32[]{:S(2)}, u32[]{:S(2)}) collective-permute-start(bf16[80,256]{1,0:T(8,128)(2,1)S(1)} %observe.1.own_ref), channel_id=1, source_target_pairs={{1,0},{2,1},{3,2},{4,3},{5,4},{6,5},{7,6},{8,7},{9,8},{10,9},{11,1... | collective-permute-start | bytes 122888 | tf_op jit(solution)/shard_map/ppermute | solution.py:622
  104.7 0.0 collective-permute-done.2.before_ref
  104.7 0.0 copy-start.8
  104.7 4.7 %collective-permute-done.3.after_ref = bf16[80,256]{1,0:T(8,128)(2,1)S(1)} collective-permute-done((bf16[80,256]{1,0:T(8,128)(2,1)S(1)}, bf16[80,256]{1,0:T(8,128)(2,1)S(1)}, u32[]{:S(2)}, u32[]{:S(2)}) %collective-permute-start.3) | collective-permute-done | bytes 40992 | tf_op jit(solution)/shard_map/ppermute | solution.py:622
  109.4 0.6 copy-done.9
  110.0 34.9 %analyse.1 = bf16[8,16,64,128]{3,2,1,0:T(8,128)(2,1)} custom-call(bf16[80,256]{1,0:T(8,128)(2,1)} %copy-done.8, bf16[80,256]{1,0:T(8,128)(2,1)} %copy-done.2, bf16[80,256]{1,0:T(8,128)(2,1)} %copy-done.9, s32[32,128]{1,0:T(8,128)} %nbr_ref.1, f32[32,128]{1,0:T(8,128)} %loc_ref.3, bf16[8,16,64,128]{3,2,1,0:T(8,128)(2,1)} %bitcast.28), custom_call_target="tpu_custom_call" | custom-call | tf_op jit(solution)/shard_map/analyse/pallas_call | solution.py:566
  144.9 10.0 %all-to-all-start.1 = ((bf16[128,64,128]{2,1,0:T(8,128)(2,1)}), bf16[128,64,128]{2,1,0:T(8,128)(2,1)}, u32[]{:S(2)}, u32[]{:S(2)}) async-start(bf16[128,64,128]{2,1,0:T(8,128)(2,1)} %bitcast.32), calls=%async_computation.1 | async-start | bytes 4194304 | tf_op jit(solution)/shard_map/all_to_all | solution.py:626
  155.0 5.8 %copy.35 = bf16[512,8,512]{2,0,1:T(8,128)(2,1)} copy(bf16[512,8,512]{2,1,0:T(8,128)(2,1)} %bitcast.35) | data formatting | bytes 8388608 | tf_op jit(solution)/shard_map/reshape | solution.py:670
  160.7 24.2 %all-to-all-done.1.inc_ref = bf16[128,64,128]{2,1,0:T(8,128)(2,1)} async-done(((bf16[128,64,128]{2,1,0:T(8,128)(2,1)}), bf16[128,64,128]{2,1,0:T(8,128)(2,1)}, u32[]{:S(2)}, u32[]{:S(2)}) %all-to-all-start.1) | async-done | bytes 2097184 | tf_op jit(solution)/shard_map/all_to_all | solution.py:626
  184.9 4.4 %finish.1 = bf16[8,1024,128]{2,1,0:T(8,128)(2,1)} custom-call(bf16[128,64,128]{2,1,0:T(8,128)(2,1)S(1)} %copy-done.1, bf16[128,64,128]{2,1,0:T(8,128)(2,1)} %all-to-all-done.1.inc_ref), custom_call_target="tpu_custom_call" | custom-call | tf_op jit(solution)/shard_map/finish/pallas_call | solution.py:607
  (19 shorter events, 0.0 us)
Async XLA Ops:
  0.6 6.5 %copy-start.6 = (bf16[8,512,512]{2,1,0:T(8,128)(2,1)S(1)}, bf16[8,512,512]{2,1,0:T(8,128)(2,1)}, u32[]{:S(2)}) copy-start(bf16[8,512,512]{2,1,0:T(8,128)(2,1)} %param.17) | copy-start | bytes 12582916
  2.4 16.1 %collective-permute-start = (bf16[512,512]{1,0:T(8,128)(2,1)S(1)}, bf16[512,512]{1,0:T(8,128)(2,1)S(1)}, u32[]{:S(2)}, u32[]{:S(2)}) collective-permute-start(bf16[512,512]{1,0:T(8,128)(2,1)S(1)} %bitcast.38), channel_id=1, source_target_pairs={{0,1},{1,2},{2,3},{3,4},{4,5},{5,6},{6,7},{7,8},{8,9},{9,10},{10,1... | collective-permute-start | bytes 1572872 | tf_op jit(solution)/shard_map/ppermute | solution.py:622
  7.1 14.0 %collective-permute-start.1 = (bf16[512,512]{1,0:T(8,128)(2,1)S(1)}, bf16[512,512]{1,0:T(8,128)(2,1)S(1)}, u32[]{:S(2)}, u32[]{:S(2)}) collective-permute-start(bf16[512,512]{1,0:T(8,128)(2,1)S(1)} %bitcast.39), channel_id=1, source_target_pairs={{1,0},{2,1},{3,2},{4,3},{5,4},{6,5},{7,6},{8,7},{9,8},{10,9},{11,1... | collective-permute-start | bytes 1572872 | tf_op jit(solution)/shard_map/ppermute | solution.py:622
  7.2 4.4 %copy-start.7 = (bf16[8,1024,128]{2,1,0:T(8,128)(2,1)S(1)}, bf16[8,1024,128]{2,1,0:T(8,128)(2,1)}, u32[]{:S(2)}) copy-start(bf16[8,1024,128]{2,1,0:T(8,128)(2,1)} %param.18) | copy-start | bytes 6291460
  11.6 2.7 %copy-start.10 = (s32[512,6]{0,1:T(8,128)S(1)}, s32[512,6]{0,1:T(8,128)}, u32[]{:S(2)}) copy-start(s32[512,6]{0,1:T(8,128)} %param.19) | copy-start | bytes 36868
  11.6 3.6 %copy-start.11 = (s32[1024]{0:T(1024)S(1)}, s32[1024]{0:T(1024)}, u32[]{:S(2)}) copy-start(s32[1024]{0:T(1024)} %param.20) | copy-start | bytes 12292
  52.2 39.0 %copy-start.3 = (s32[256]{0:T(256)S(1)}, s32[256]{0:T(256)}, u32[]{:S(2)}) copy-start(s32[256]{0:T(256)} %loc_ref.2) | copy-start | bytes 3076
  52.2 39.0 %copy-start.4 = (f32[256]{0:T(256)S(1)}, f32[256]{0:T(256)}, u32[]{:S(2)}) copy-start(f32[256]{0:T(256)} %param.30) | copy-start | bytes 3076
  52.2 39.0 %copy-start.5 = (f32[256]{0:T(256)S(1)}, f32[256]{0:T(256)}, u32[]{:S(2)}) copy-start(f32[256]{0:T(256)} %param.31) | copy-start | bytes 3076
  52.2 39.0 %all-to-all-start = ((bf16[128,64,128]{2,1,0:T(8,128)(2,1)}), bf16[128,64,128]{2,1,0:T(8,128)(2,1)S(1)}, u32[]{:S(2)}, u32[]{:S(2)}) async-start(bf16[128,64,128]{2,1,0:T(8,128)(2,1)} %get-tuple-element.5.fore_ref), calls=%async_computation | async-start | bytes 4194304 | tf_op jit(solution)/shard_map/all_to_all | solution.py:626
  91.2 18.2 %copy-start = (bf16[128,64,128]{2,1,0:T(8,128)(2,1)}, bf16[128,64,128]{2,1,0:T(8,128)(2,1)S(1)}, u32[]{:S(2)}) copy-start(bf16[128,64,128]{2,1,0:T(8,128)(2,1)S(1)} %all-to-all-done) | copy-start | bytes 6291460
  98.9 10.5 %copy-start.2 = (bf16[80,256]{1,0:T(8,128)(2,1)}, bf16[80,256]{1,0:T(8,128)(2,1)S(1)}, u32[]{:S(2)}) copy-start(bf16[80,256]{1,0:T(8,128)(2,1)S(1)} %observe.1.own_ref) | copy-start | bytes 122884
  98.9 5.8 %collective-permute-start.2 = (bf16[80,256]{1,0:T(8,128)(2,1)S(1)}, bf16[80,256]{1,0:T(8,128)(2,1)S(1)}, u32[]{:S(2)}, u32[]{:S(2)}) collective-permute-start(bf16[80,256]{1,0:T(8,128)(2,1)S(1)} %observe.1.own_ref), channel_id=1, source_target_pairs={{0,1},{1,2},{2,3},{3,4},{4,5},{5,6},{6,7},{7,8},{8,9},{9,10},{10,1... | collective-permute-start | bytes 122888 | tf_op jit(solution)/shard_map/ppermute | solution.py:622
  102.6 6.8 %collective-permute-start.3 = (bf16[80,256]{1,0:T(8,128)(2,1)S(1)}, bf16[80,256]{1,0:T(8,128)(2,1)S(1)}, u32[]{:S(2)}, u32[]{:S(2)}) collective-permute-start(bf16[80,256]{1,0:T(8,128)(2,1)S(1)} %observe.1.own_ref), channel_id=1, source_target_pairs={{1,0},{2,1},{3,2},{4,3},{5,4},{6,5},{7,6},{8,7},{9,8},{10,9},{11,1... | collective-permute-start | bytes 122888 | tf_op jit(solution)/shard_map/ppermute | solution.py:622
  104.7 4.7 %copy-start.8 = (bf16[80,256]{1,0:T(8,128)(2,1)}, bf16[80,256]{1,0:T(8,128)(2,1)S(1)}, u32[]{:S(2)}) copy-start(bf16[80,256]{1,0:T(8,128)(2,1)S(1)} %collective-permute-done.2.before_ref) | copy-start | bytes 122884
  109.4 0.6 copy-start.9
  144.9 40.0 %all-to-all-start.1 = ((bf16[128,64,128]{2,1,0:T(8,128)(2,1)}), bf16[128,64,128]{2,1,0:T(8,128)(2,1)}, u32[]{:S(2)}, u32[]{:S(2)}) async-start(bf16[128,64,128]{2,1,0:T(8,128)(2,1)} %bitcast.32), calls=%async_computation.1 | async-start | bytes 4194304 | tf_op jit(solution)/shard_map/all_to_all | solution.py:626
  154.9 30.0 %copy-start.1 = (bf16[128,64,128]{2,1,0:T(8,128)(2,1)S(1)}, bf16[128,64,128]{2,1,0:T(8,128)(2,1)}, u32[]{:S(2)}) copy-start(bf16[128,64,128]{2,1,0:T(8,128)(2,1)} %get-tuple-element.5.fore_ref) | copy-start | bytes 6291460

commit v3 on v2

--- a/solution.py
+++ b/solution.py
@@ -29,7 +29,8 @@
     edge_ref,
     parent_ref,
     latent_hbm,
-    rim_ref,
+    before_ref,
+    after_ref,
     back_hbm,
     w_send_ref,
     w_recv_ref,
@@ -57,13 +58,13 @@
     members = MEMBERS
     count, width = latent_hbm.shape
     nodes = count // members
-    rim = rim_ref.shape[0] // 2
+    rim = before_ref.shape[0]
     degree = edge_ref.shape[0] // nodes
     rows = count // CHUNKS
     tile = members * GROUP
 
     def piece(c):
-        return pl.ds(pl.multiple_of(c * rows, rows), rows)
+        return pl.ds(c * rows, rows)
 
     loads = [
         pltpu.make_async_copy(latent_hbm.at[piece(c)], latent_s.at[piece(c)], in_sem.at[c])
@@ -94,8 +95,8 @@
             part = values[:, c * LANES : (c + 1) * LANES].reshape(-1, members, LANES)
             ref[first // members : first // members + part.shape[0], c] = part
 
-    spread_rows(send_s, 0, send_of(rim_ref[0:rim]))
-    spread_rows(send_s, rim + count, send_of(rim_ref[rim : 2 * rim]))
+    spread_rows(send_s, 0, send_of(before_ref[...]))
+    spread_rows(send_s, rim + count, send_of(after_ref[...]))
     for c in range(CHUNKS):
         loads[c].wait()
         state = latent_s[c * rows : (c + 1) * rows]
@@ -118,7 +119,7 @@
     def store_proc(c):
         return pltpu.make_async_copy(proc_s.at[piece(c)], proc_hbm.at[piece(c)], out_sem.at[c])
 
-    def update(c, carry):
+    def update(c):
         state = latent_s[piece(c)]
         some_nodes = pl.ds(c * (rows // members), rows // members)
         agg = jnp.concatenate(
@@ -134,10 +135,10 @@
         proc = (state.astype(F32) + norm).astype(BF16)
         proc_s[piece(c)] = proc
         store_proc(c).start()
-        dec_s[piece(c)] = dot(proc, w_dec_s[...])
-        return carry
-
-    lax.fori_loop(0, CHUNKS, update, 0)
+        dec_s[some_nodes] = dot(proc, w_dec_s[...]).reshape(-1, members, LANES)
+
+    for c in range(CHUNKS):
+        update(c)
 
     tiles = fore_s.shape[0]
     some = tiles // CHUNKS
@@ -150,8 +151,7 @@
 
         def spread(t, carry):
             parts = [
-                dec_s[pl.ds(pl.multiple_of(parent_ref[t * GROUP + q], members), members), :]
-                for q in range(GROUP)
+                dec_s[parent_ref[t * GROUP + q]] for q in range(GROUP)
             ]
             back = back_s[pl.ds(pl.multiple_of(t * tile, tile), tile), :].astype(F32)
             fore_s[t] = (jnp.concatenate(parts, axis=0) + back).astype(BF16)
@@ -165,12 +165,11 @@
         store_fore(c).wait()
 
 
-def forecast(latent, rims, back, senders, parent, weights):
+def forecast(latent, before, after, back, senders, parent, weights):
     count, width = latent.shape
     grid_rows = back.shape[0]
-    rim = rims.shape[0] // 2
+    rim = before.shape[0]
     tiles = lax.axis_size("member") * lax.axis_size("region")
-    edge = (senders - (count - rim) // MEMBERS).reshape(-1)
     hbm = pl.BlockSpec(memory_space=pl.ANY)
     w_shape = pltpu.VMEM(weights[2].shape, BF16)
     return pl.pallas_call(
@@ -179,12 +178,12 @@
             jax.ShapeDtypeStruct(latent.shape, BF16),
             jax.ShapeDtypeStruct((tiles, grid_rows // tiles, LANES), BF16),
         ),
-        in_specs=[SM, SM, hbm, VM, hbm, VM, VM, hbm, hbm, hbm, VM, hbm],
+        in_specs=[SM, SM, hbm, VM, VM, hbm, VM, VM, hbm, hbm, hbm, VM, hbm],
         out_specs=(hbm, hbm),
         scratch_shapes=[
             pltpu.VMEM(((count + 2 * rim) // MEMBERS, width // LANES, MEMBERS, LANES), F32),
             pltpu.VMEM((count // MEMBERS, width // LANES, MEMBERS, LANES), F32),
-            pltpu.VMEM((count, LANES), F32),
+            pltpu.VMEM((count // MEMBERS, MEMBERS, LANES), F32),
             pltpu.VMEM(latent.shape, BF16),
             pltpu.VMEM(back.shape, BF16),
             pltpu.VMEM(latent.shape, BF16),
@@ -198,41 +197,44 @@
         ],
         compiler_params=pltpu.CompilerParams(vmem_limit_bytes=56 * 2**20),
         name="forecast",
-    )(edge, parent * MEMBERS, latent, rims, back, *weights)
-
-
-def observe_kernel(loc_ref, count_ref, ens_ref, value_ref, var_ref, pay_ref):
+    )(senders.reshape(-1), parent, latent, before, after, back, *weights)
+
+
+def point_rows(ens_ref, region, start):
+    size = 8
+    blocks = [
+        ens_ref[g, region, pl.ds(start, 2 * size), :].astype(F32) for g in range(ens_ref.shape[0])
+    ]
+    return [
+        jnp.concatenate([b[i * size : (i + 1) * size] for b in blocks], axis=0) for i in range(2)
+    ]
+
+
+def observe_kernel(count_ref, loc_ref, ens_ref, value_ref, var_ref, pay_ref):
     groups, regions, rows, _ = ens_ref.shape
     size = 8
     members = groups * size
-    slots = loc_ref.shape[0]
-    lane = lax.broadcasted_iota(jnp.int32, (members, LANES), 1)
-    for part in range(slots // LANES):
-
-        def take(i, acc):
-            loc = loc_ref[part * LANES + i]
-            point, channel = loc % LANES, loc // LANES
-            region, place = point // size, point % size
-            start = pl.multiple_of(place // 2 * 2 * size, 2 * size)
-            second = place % 2
-            pieces = []
-            for g in range(groups):
-                pair = ens_ref[g, region, pl.ds(start, 2 * size), :].astype(F32)
-                pieces.append(jnp.where(second == 1, pair[size:], pair[:size]))
-            block = jnp.concatenate(pieces, axis=0)
-            turned = pltpu.roll(block, (i - channel + LANES) % LANES, 1)
-            return jnp.where(lane == i, turned, acc)
-
-        yens = lax.fori_loop(0, LANES, take, jnp.zeros((members, LANES), F32), unroll=8)
-        span = slice(part * LANES, (part + 1) * LANES)
-        ybar = jnp.mean(yens, axis=0, keepdims=True)
-        slot = lax.broadcasted_iota(jnp.int32, (1, LANES), 1) + part * LANES
-        rinv = jnp.where(slot < count_ref[0], 1.0, 0.0) / var_ref[:, span]
-        dres = (value_ref[:, span] - ybar) * rinv
-        row = lax.broadcasted_iota(jnp.int32, (16, LANES), 0)
-        extra = jnp.where(row == 0, rinv, jnp.where(row == 1, dres, 0.0))
-        pay_ref[0:members, span] = (yens - ybar).astype(BF16)
-        pay_ref[members : members + 16, span] = extra.astype(BF16)
+    slots = loc_ref.shape[1]
+    pairs = size // 2
+    loc = loc_ref[...]
+    flat = loc % LANES * LANES + loc // LANES
+    entry = lax.broadcasted_iota(jnp.int32, (2 * LANES, slots), 0)
+
+    def add(pair, acc):
+        start = pl.multiple_of(pair % pairs * 2 * size, 2 * size)
+        state = jnp.concatenate(point_rows(ens_ref, pair // pairs, start), axis=1).astype(BF16)
+        chosen = jnp.where(entry == flat - pair * 2 * LANES, 1.0, 0.0).astype(BF16)
+        return acc + dot(state, chosen)
+
+    yens = lax.fori_loop(0, regions * pairs, add, jnp.zeros((members, slots), F32), unroll=8)
+    ybar = jnp.mean(yens, axis=0, keepdims=True)
+    slot = lax.broadcasted_iota(jnp.int32, (1, slots), 1)
+    rinv = jnp.where(slot < count_ref[0], 1.0, 0.0) / var_ref[...]
+    dres = (value_ref[...] - ybar) * rinv
+    row = lax.broadcasted_iota(jnp.int32, (16, slots), 0)
+    extra = jnp.where(row == 0, rinv, jnp.where(row == 1, dres, 0.0))
+    pay_ref[0:members] = (yens - ybar).astype(BF16)
+    pay_ref[members : members + 16] = extra.astype(BF16)
 
 
 def observe(ens, loc, count, value, var):
@@ -240,11 +242,11 @@
     return pl.pallas_call(
         observe_kernel,
         out_shape=jax.ShapeDtypeStruct((groups * 8 + 16, loc.shape[0]), BF16),
-        in_specs=[SM, SM, VM, VM, VM],
+        in_specs=[SM, VM, VM, VM, VM],
         out_specs=VM,
         compiler_params=pltpu.CompilerParams(vmem_limit_bytes=40 * 2**20),
         name="observe",
-    )(loc, count, ens, value[None], var[None])
+    )(count, loc[None], ens, value[None], var[None])
 
 
 def analyse_kernel(
@@ -253,6 +255,8 @@
     after_ref,
     nbr_ref,
     loc_ref,
+    ens_hbm,
+    inc_hbm,
     ens_ref,
     inc_ref,
     pay_s,
@@ -264,55 +268,51 @@
     q_s,
     t_s,
     c_s,
-    v_s,
     w_s,
+    in_sem,
+    out_sem,
 ):
     groups, regions, rows, _ = ens_ref.shape
+    load = pltpu.make_async_copy(ens_hbm, ens_ref, in_sem.at[0])
+    load.start()
     size = 8
     members = groups * size
     order = nbr_ref.shape[0]
     nb = order // size
     slots = own_ref.shape[1]
-    parts = slots // LANES
     sub = lax.broadcasted_iota(jnp.int32, (size, LANES), 0)
 
     for i, ref in enumerate((before_ref, own_ref, after_ref)):
-        for h in range(parts):
-            pay_s[i * parts + h] = ref[0 : members + 16, h * LANES : (h + 1) * LANES].astype(F32)
+        pay_s[:, i * slots : (i + 1) * slots] = ref[...]
 
     def full(row):
         return jnp.broadcast_to(row, (size, LANES))
 
-    def gather(l, vec):
-        index = nbr_ref[pl.ds(l, 1), :]
-        lane = full(index % LANES)
-        panel = full(index // LANES)
-        masks = [panel == j for j in range(1, 3 * parts)]
-
-        def pick(first):
-            out = None
-            for j in range(3 * parts):
-                got = jnp.take_along_axis(
-                    pay_s[j, pl.ds(first, size), :], lane, axis=1, mode="promise_in_bounds"
-                )
-                out = got if out is None else jnp.where(masks[j - 1], got, out)
-            return out
-
-        extra = pick(members)
-        weight = loc_ref[pl.ds(l, 1), :]
-        root = jnp.sqrt(weight * extra[0:1])
-        dl = weight * extra[1:2]
-        new = []
-        for g in range(groups):
-            yl = pick(g * size)
-            new.append(vec[g] + yl * dl)
-            b = yl * root
-            bl_s[pl.ds(pl.multiple_of(l * members + g * size, size), size), :] = b
-            bk_s[pl.ds(g * size * order + l, size, stride=order), :] = b
-        return tuple(new)
+    entry = lax.broadcasted_iota(jnp.int32, (3 * slots, 2 * LANES), 0)
+
+    def gather(step, vec):
+        index = jnp.concatenate(
+            [nbr_ref[pl.ds(2 * step, 1), :], nbr_ref[pl.ds(2 * step + 1, 1), :]], axis=1
+        )
+        chosen = jnp.where(entry == index, 1.0, 0.0).astype(BF16)
+        both = dot(pay_s[...], chosen)
+        vec = list(vec)
+        for i in range(2):
+            l = 2 * step + i
+            panel = both[:, i * LANES : (i + 1) * LANES]
+            weight = loc_ref[pl.ds(l, 1), :]
+            root = jnp.sqrt(weight * panel[members : members + 1])
+            dl = weight * panel[members + 1 : members + 2]
+            for g in range(groups):
+                yl = panel[g * size : (g + 1) * size]
+                vec[g] = vec[g] + yl * dl
+                b = yl * root
+                bl_s[pl.ds(pl.multiple_of(l * members + g * size, size), size), :] = b
+                bk_s[pl.ds(g * size * order + l, size, stride=order), :] = b
+        return tuple(vec)
 
     zero = jnp.zeros((size, LANES), F32)
-    vec = lax.fori_loop(0, order, gather, tuple([zero] * groups), unroll=2)
+    vec = lax.fori_loop(0, order // 2, gather, tuple([zero] * groups), unroll=2)
 
     def row_of(ref, r):
         return jnp.broadcast_to(ref[pl.ds(r, 1), :], (size, LANES))
@@ -490,53 +490,39 @@
 
     gain = full(jnp.float32(base) ** 0.5 * root)
 
+    half = members // 2
+
     def vmat(step, carry):
+        ks = [2 * step, 2 * step + 1, half + 2 * step, half + 2 * step + 1]
+        slabs = [[], [], [], []]
         for g0 in range(0, groups, 4):
             acc = [zero] * 16
             for l in range(order):
                 c = [c_s[pl.ds(l * members + (g0 + g) * size, size), :] for g in range(4)]
                 for i in range(4):
-                    lhs = row_of(bk_s, (step * 4 + i) * order + l)
+                    lhs = row_of(bk_s, ks[i] * order + l)
                     for g in range(4):
                         acc[i * 4 + g] = acc[i * 4 + g] + lhs * c[g]
             for i in range(4):
-                k = step * 4 + i
                 for g in range(4):
-                    here = sub + (g0 + g) * size == k
+                    here = sub + (g0 + g) * size == ks[i]
                     s = gain * (acc[i * 4 + g] + jnp.where(here, z, 0.0))
-                    v = s + t_s[pl.ds((g0 + g) * size, size), :] - jnp.where(here, 1.0, 0.0)
-                    start = k * members + (g0 + g) * size
-                    v_s[pl.ds(pl.multiple_of(start, size), size), :] = v
+                    s = s + t_s[pl.ds((g0 + g) * size, size), :]
+                    slabs[i].append(s - jnp.where(here, 1.0, 0.0))
+        for i in range(2):
+            both = jnp.concatenate(slabs[i] + slabs[2 + i], axis=0)
+            start = pl.multiple_of(ks[i] * LANES, LANES)
+            w_s[pl.ds(start, LANES), :] = jnp.transpose(both)
         return carry
 
-    lax.fori_loop(0, members // 4, vmat, 0)
-
-    half = members // 2
-
-    def turn(k, carry):
-        both = jnp.concatenate(
-            [
-                v_s[pl.ds(pl.multiple_of(k * members, members), members), :],
-                v_s[pl.ds(pl.multiple_of((k + half) * members, members), members), :],
-            ],
-            axis=0,
-        )
-        w_s[pl.ds(pl.multiple_of(k * LANES, LANES), LANES), :] = jnp.transpose(both)
-        return carry
-
-    lax.fori_loop(0, half, turn, 0)
+    lax.fori_loop(0, half // 2, vmat, 0)
+    load.wait()
 
     def apply(pair, carry):
         region, place = pair // (size // 2), pair % (size // 2)
         start = pl.multiple_of(place * 2 * size, 2 * size)
-        blocks = [
-            ens_ref[g, region, pl.ds(start, 2 * size), :].astype(F32) for g in range(groups)
-        ]
         outs = []
-        for second in range(2):
-            x = jnp.concatenate(
-                [b[second * size : (second + 1) * size] for b in blocks], axis=0
-            )
+        for second, x in enumerate(point_rows(ens_ref, region, start)):
             x = (x - jnp.mean(x, axis=0, keepdims=True)).astype(BF16)
             gap = jnp.zeros_like(x)
             rhs = jnp.concatenate(
@@ -554,22 +540,35 @@
             ).astype(BF16)
         return carry
 
-    lax.fori_loop(0, regions * size // 2, apply, 0, unroll=8)
+    steps = 4
+    some = regions // steps
+    stores = []
+    for c in range(steps):
+        lax.fori_loop(c * some * size // 2, (c + 1) * some * size // 2, apply, 0, unroll=8)
+        span = pl.ds(c * some, some)
+        stores.append(
+            pltpu.make_async_copy(inc_ref.at[:, span], inc_hbm.at[:, span], out_sem.at[c])
+        )
+        stores[c].start()
+    for copy in stores:
+        copy.wait()
 
 
 def analyse(before, own, after, nbr, loc, ens):
     order, points = nbr.shape
     members = ens.shape[0] * 8
-    panels = 3 * own.shape[1] // LANES
+    hbm = pl.BlockSpec(memory_space=pl.ANY)
     small = pltpu.VMEM((order * order, LANES), F32)
     tall = pltpu.VMEM((order * members, LANES), F32)
     return pl.pallas_call(
         analyse_kernel,
         out_shape=jax.ShapeDtypeStruct(ens.shape, BF16),
-        in_specs=[VM] * 6,
-        out_specs=VM,
+        in_specs=[VM] * 5 + [hbm],
+        out_specs=hbm,
         scratch_shapes=[
-            pltpu.VMEM((panels, members + 16, LANES), F32),
+            pltpu.VMEM(ens.shape, BF16),
+            pltpu.VMEM(ens.shape, BF16),
+            pltpu.VMEM((members + 16, 3 * own.shape[1]), BF16),
             tall,
             tall,
             small,
@@ -578,8 +577,9 @@
             small,
             small,
             tall,
-            pltpu.VMEM((members * members, LANES), F32),
             pltpu.VMEM((members // 2 * LANES, LANES), F32),
+            pltpu.SemaphoreType.DMA((1,)),
+            pltpu.SemaphoreType.DMA((4,)),
         ],
         compiler_params=pltpu.CompilerParams(vmem_limit_bytes=56 * 2**20),
         name="analyse",
@@ -615,11 +615,18 @@
     )(fore, inc)
 
 
-def neighbours(last, first, axis, wrap):
+def neighbours(inner, outer, axis, wrap):
     count = lax.axis_size(axis)
-    up = [(i, (i + 1) % count) for i in range(count if wrap else count - 1)]
-    down = [(j, i) for i, j in up]
-    return lax.ppermute(last, axis, up), lax.ppermute(first, axis, down)
+    within = [(i, i ^ 1) for i in range(count)]
+    links = [(i, (i + 1) % count) for i in range(1, count if wrap else count - 1, 2)]
+    across = links + [(b, a) for a, b in links]
+    got = lax.ppermute(outer, axis, across)
+    return lax.ppermute(inner, axis, within), got
+
+
+def swapped(index, low, high, odd):
+    moved = jnp.where(index < low, index + high, jnp.where(index >= high, index - high, index))
+    return jnp.where(odd == 1, moved, index)
 
 
 def exchange(blocks):
@@ -652,18 +659,25 @@
     def node_major(array):
         return array.transpose(1, 0, 2).reshape(-1, array.shape[2])
 
-    before, after = neighbours(
-        node_major(latent_vertex_values[:, -RIM:]),
-        node_major(latent_vertex_values[:, :RIM]),
+    odd = lax.axis_index("region") % 2
+
+    def rim(start):
+        return node_major(lax.dynamic_slice_in_dim(latent_vertex_values, start, RIM, 1))
+
+    inner, outer = neighbours(
+        rim(jnp.where(odd == 1, 0, nodes - RIM)),
+        rim(jnp.where(odd == 1, nodes - RIM, 0)),
         "region",
         True,
     )
+    edges = swapped(edge_senders - (nodes - RIM), RIM, nodes + RIM, odd)
     weights = (w_send, w_recv, w_node, w_agg, w_out, norm_gain[None], w_dec)
     processed, fore = forecast(
         node_major(latent_vertex_values),
-        jnp.concatenate([before, after], axis=0),
+        outer,
+        inner,
         node_major(background_field),
-        edge_senders,
+        edges,
         grid_parent,
         weights,
     )
@@ -671,8 +685,10 @@
     ens = exchange(fore)
     ens = ens.reshape(groups, regions, *ens.shape[1:])
     payload = observe(ens, obs_loc, obs_count, obs_value, obs_var)
-    pay_before, pay_after = neighbours(payload, payload, MR, False)
-    inc = analyse(pay_before, payload, pay_after, obs_nbr, loc_weight, ens)
+    pay_inner, pay_outer = neighbours(payload, payload, MR, False)
+    slots = obs_loc.shape[0]
+    nbr = swapped(obs_nbr, slots, 2 * slots, odd)
+    inc = analyse(pay_outer, payload, pay_inner, nbr, loc_weight, ens)
     landed = exchange(inc.reshape(groups * regions, *inc.shape[2:]))
     return processed, finish(fore, landed, members)
 

time: 190 us -> 175 us (0.921)
  Pallas kernels: 77.1 us -> 69.2 us
  waiting for transfers between devices: 63.8 us -> 56.3 us
  local copies, waits for them, and re-layouts: 16.4 us -> 20.1 us
    ppermute x4, waiting for transfers between devices: 9.94 us -> 2.44 us  [the longest x2 2.44 us: neighbours(): got = lax.ppermute(outer, axis, across)]
    pallas_call x1, Pallas kernels: 7.65 us -> 2.46 us  [observe(): pl.pallas_call(observe_kernel, out_shape=jax.ShapeDtypeStruct((groups * 8...]
    transpose x5, local copies, waits for them, and re-layouts: 9.11 us -> 11.2 us  [node_major(): return array.transpose(1, 0, 2).reshape(-1, array.shape[2])]
    all_to_all x2, starting transfers between devices: 18.7 us -> 16.8 us  [exchange(): return lax.all_to_all(blocks, MR, split_axis=0, concat_axis=0, tiled=True)]
  transfers between devices with their start and end apart: 6 -> 6, of which waited for: 5 -> 3; matrix products, arithmetic and copies ran while one was open for 8% -> 10% of each run, Pallas kernels for 0% -> 0%
where the time goes in v3:
time: 175 us
  Pallas kernels  69.2 us (40%)
  waiting for transfers between devices  56.3 us (32%)
  starting transfers between devices  27 us (15%)
  local copies, waits for them, and re-layouts  20.1 us (11%)
    all_to_all x2, waiting for transfers between devices, exchange(): return lax.all_to_all(blocks, MR, split_axis=0, concat_axis=0, tiled=True)  53.8 us
    pallas_call x1, Pallas kernels, analyse(): pl.pallas_call(analyse_kernel, out_shape=jax.ShapeDtypeStruct(ens.shape,...  33.1 us
    pallas_call x1, Pallas kernels, forecast(): pl.pallas_call(forecast_kernel, out_shape=(jax.ShapeDtypeStruct(latent.sh...  29.2 us
    all_to_all x2, starting transfers between devices, exchange(): return lax.all_to_all(blocks, MR, split_axis=0, concat_axis=0, tiled=True)  16.8 us
    transpose x5, local copies, waits for them, and re-layouts, node_major(): return array.transpose(1, 0, 2).reshape(-1, array.shape[2])  11.2 us
    ppermute x2, starting transfers between devices, neighbours(): got = lax.ppermute(outer, axis, across)  8.06 us
    reshape x1, local copies, waits for them, and re-layouts, shards(): processed = processed.reshape(nodes, members, width).transpose(1, 0, 2)  5.75 us
    pallas_call x1, Pallas kernels, finish(): pl.pallas_call(finish_kernel, out_shape=jax.ShapeDtypeStruct((members, gr...  4.43 us
  transfers between devices with their start and end apart: 6, of which 3 were waited for; matrix products, arithmetic and copies ran while one was open for 10% of the time, Pallas kernels for 0%

profile of v3, /device:TPU:1, one launch (start us, length us, event | category | flops | bytes accessed | tf_op | source)
XLA Modules:
  0.0 174.7 jit_solution(11150341189480059516)
XLA Ops:
  0.7 1.3 dynamic-slice_bitcast_fusion
  2.0 0.3 copy.39
  2.3 4.4 %collective-permute-start = (bf16[512,512]{1,0:T(8,128)(2,1)S(1)}, bf16[512,512]{1,0:T(8,128)(2,1)S(1)}, u32[]{:S(2)}, u32[]{:S(2)}) collective-permute-start(bf16[512,512]{1,0:T(8,128)(2,1)S(1)} %bitcast.40), channel_id=1, source_target_pairs={{1,2},{3,4},{5,6},{7,8},{9,10},{11,12},{13,14},{15,0},{2,1},{4,3},... | collective-permute-start | bytes 1572872 | tf_op jit(solution)/shard_map/ppermute | solution.py:623
  6.6 0.3 copy.38
  6.9 2.1 %collective-permute-start.1 = (bf16[512,512]{1,0:T(8,128)(2,1)S(1)}, bf16[512,512]{1,0:T(8,128)(2,1)S(1)}, u32[]{:S(2)}, u32[]{:S(2)}) collective-permute-start(bf16[512,512]{1,0:T(8,128)(2,1)S(1)} %bitcast.41), channel_id=1, source_target_pairs={{0,1},{1,0},{2,3},{3,2},{4,5},{5,4},{6,7},{7,6},{8,9},{9,8},{10,11... | collective-permute-start | bytes 1572872 | tf_op jit(solution)/shard_map/ppermute | solution.py:624
  9.1 0.1 copy.24
  9.2 0.8 reshape.28.edge_ref
  10.0 6.7 %copy.36 = bf16[512,8,512]{2,1,0:T(8,128)(2,1)} copy(bf16[512,8,512]{2,0,1:T(8,128)(2,1)} %bitcast.36) | data formatting | bytes 8388608 | tf_op jit(solution)/shard_map/transpose | solution.py:660
  16.7 2.7 %copy.37 = bf16[1024,8,128]{2,1,0:T(8,128)(2,1)} copy(bf16[1024,8,128]{2,0,1:T(8,128)(2,1)S(1)} %bitcast.39) | data formatting | bytes 4194304 | tf_op jit(solution)/shard_map/transpose | solution.py:660
  19.4 0.0 collective-permute-done.before_ref
  19.4 0.0 collective-permute-done.1.after_ref
  19.4 0.8 copy-done.7
  20.2 0.2 copy-done.8
  20.3 29.2 %forecast.1 = (bf16[4096,512]{1,0:T(8,128)(2,1)}, bf16[128,64,128]{2,1,0:T(8,128)(2,1)}) custom-call(s32[3072]{0:T(1024)} %reshape.28.edge_ref, s32[1024]{0:T(1024)} %parent_ref.1, bf16[4096,512]{1,0:T(8,128)(2,1)} %bitcast.33, bf16[512,512]{1,0:T(8,128)(2,1)} %copy-done.7, bf16[512,512]{1,0:T(8,128)(2,1)} %copy-done.8, bf16[8192,128]{1,0:T(8,128)(2,1)} %bitcast.35, ...), custom_call_target="tpu_custom_call" | custom-call | tf_op jit(solution)/shard_map/forecast/pallas_call | solution.py:175
  49.5 0.0 copy-start.3
  49.5 0.0 copy-start.4
  49.5 0.0 copy-start.5
  49.6 10.2 %all-to-all-start = ((bf16[128,64,128]{2,1,0:T(8,128)(2,1)}), bf16[128,64,128]{2,1,0:T(8,128)(2,1)S(1)}, u32[]{:S(2)}, u32[]{:S(2)}) async-start(bf16[128,64,128]{2,1,0:T(8,128)(2,1)} %get-tuple-element.5.fore_ref), calls=%async_computation | async-start | bytes 4194304 | tf_op jit(solution)/shard_map/all_to_all | solution.py:633
  59.8 0.0 copy-start.12
  60.5 29.6 %all-to-all-done = bf16[128,64,128]{2,1,0:T(8,128)(2,1)S(1)} async-done(((bf16[128,64,128]{2,1,0:T(8,128)(2,1)}), bf16[128,64,128]{2,1,0:T(8,128)(2,1)S(1)}, u32[]{:S(2)}, u32[]{:S(2)}) %all-to-all-start) | async-done | bytes 2097184 | tf_op jit(solution)/shard_map/all_to_all | solution.py:633
  90.1 2.5 %observe.1.own_ref = bf16[80,256]{1,0:T(8,128)(2,1)S(1)} custom-call(s32[1]{0:T(128)S(6)} %copy.40.count_ref, s32[1,256]{1,0:T(1,128)S(1)} %bitcast.30, bf16[8,16,64,128]{3,2,1,0:T(8,128)(2,1)S(1)} %bitcast.28, f32[1,256]{1,0:T(1,128)S(1)} %bitcast.31, f32[1,256]{1,0:T(1,128)S(1)} %bitcast.32), custom_call_target="tpu_custom_call" | custom-call | tf_op jit(solution)/shard_map/observe/pallas_call | solution.py:242
  92.6 3.7 %collective-permute-start.2 = (bf16[80,256]{1,0:T(8,128)(2,1)S(1)}, bf16[80,256]{1,0:T(8,128)(2,1)S(1)}, u32[]{:S(2)}, u32[]{:S(2)}) collective-permute-start(bf16[80,256]{1,0:T(8,128)(2,1)S(1)} %observe.1.own_ref), channel_id=1, source_target_pairs={{1,2},{3,4},{5,6},{7,8},{9,10},{11,12},{13,14},{15,16},{17,18},{19... | collective-permute-start | bytes 122888 | tf_op jit(solution)/shard_map/ppermute | solution.py:623
  96.3 0.1 collective-permute-start.3
  96.4 0.6 fusion.3.nbr_ref
  97.0 2.4 %collective-permute-done.2.before_ref = bf16[80,256]{1,0:T(8,128)(2,1)S(1)} collective-permute-done((bf16[80,256]{1,0:T(8,128)(2,1)S(1)}, bf16[80,256]{1,0:T(8,128)(2,1)S(1)}, u32[]{:S(2)}, u32[]{:S(2)}) %collective-permute-start.2) | collective-permute-done | bytes 40992 | tf_op jit(solution)/shard_map/ppermute | solution.py:623
  99.4 0.6 copy-done.9
  100.0 0.6 copy-done.10
  100.6 33.1 %analyse.1 = bf16[8,16,64,128]{3,2,1,0:T(8,128)(2,1)} custom-call(bf16[80,256]{1,0:T(8,128)(2,1)} %copy-done.9, bf16[80,256]{1,0:T(8,128)(2,1)} %copy-done.2, bf16[80,256]{1,0:T(8,128)(2,1)} %copy-done.10, s32[32,128]{1,0:T(8,128)} %fusion.3.nbr_ref, f32[32,128]{1,0:T(8,128)} %loc_ref.1, bf16[8,16,64,128]{3,2,1,0:T(8,128)(2,1)} %bitcast.29), custom_call_target="tpu_custom_call" | custom-call | tf_op jit(solution)/shard_map/analyse/pallas_call | solution.py:563
  133.8 6.5 %all-to-all-start.1 = ((bf16[128,64,128]{2,1,0:T(8,128)(2,1)}), bf16[128,64,128]{2,1,0:T(8,128)(2,1)}, u32[]{:S(2)}, u32[]{:S(2)}) async-start(bf16[128,64,128]{2,1,0:T(8,128)(2,1)} %bitcast.34), calls=%async_computation.1 | async-start | bytes 4194304 | tf_op jit(solution)/shard_map/all_to_all | solution.py:633
  140.3 5.8 %copy.35 = bf16[512,8,512]{2,0,1:T(8,128)(2,1)} copy(bf16[512,8,512]{2,1,0:T(8,128)(2,1)} %bitcast.37) | data formatting | bytes 8388608 | tf_op jit(solution)/shard_map/reshape | solution.py:684
  146.1 24.2 %all-to-all-done.1.inc_ref = bf16[128,64,128]{2,1,0:T(8,128)(2,1)} async-done(((bf16[128,64,128]{2,1,0:T(8,128)(2,1)}), bf16[128,64,128]{2,1,0:T(8,128)(2,1)}, u32[]{:S(2)}, u32[]{:S(2)}) %all-to-all-start.1) | async-done | bytes 2097184 | tf_op jit(solution)/shard_map/all_to_all | solution.py:633
  170.3 4.4 %finish.1 = bf16[8,1024,128]{2,1,0:T(8,128)(2,1)} custom-call(bf16[128,64,128]{2,1,0:T(8,128)(2,1)S(1)} %copy-done.1, bf16[128,64,128]{2,1,0:T(8,128)(2,1)} %all-to-all-done.1.inc_ref), custom_call_target="tpu_custom_call" | custom-call | tf_op jit(solution)/shard_map/finish/pallas_call | solution.py:607
  (20 shorter events, 0.0 us)
Async XLA Ops:
  0.6 8.4 %copy-start.11 = (s32[512,6]{0,1:T(8,128)S(1)}, s32[512,6]{0,1:T(8,128)}, u32[]{:S(2)}) copy-start(s32[512,6]{0,1:T(8,128)} %param.19) | copy-start | bytes 36868
  2.3 17.1 %collective-permute-start = (bf16[512,512]{1,0:T(8,128)(2,1)S(1)}, bf16[512,512]{1,0:T(8,128)(2,1)S(1)}, u32[]{:S(2)}, u32[]{:S(2)}) collective-permute-start(bf16[512,512]{1,0:T(8,128)(2,1)S(1)} %bitcast.40), channel_id=1, source_target_pairs={{1,2},{3,4},{5,6},{7,8},{9,10},{11,12},{13,14},{15,0},{2,1},{4,3},... | collective-permute-start | bytes 1572872 | tf_op jit(solution)/shard_map/ppermute | solution.py:623
  6.9 12.4 %collective-permute-start.1 = (bf16[512,512]{1,0:T(8,128)(2,1)S(1)}, bf16[512,512]{1,0:T(8,128)(2,1)S(1)}, u32[]{:S(2)}, u32[]{:S(2)}) collective-permute-start(bf16[512,512]{1,0:T(8,128)(2,1)S(1)} %bitcast.41), channel_id=1, source_target_pairs={{0,1},{1,0},{2,3},{3,2},{4,5},{5,4},{6,7},{7,6},{8,9},{9,8},{10,11... | collective-permute-start | bytes 1572872 | tf_op jit(solution)/shard_map/ppermute | solution.py:624
  10.0 6.7 %copy-start.6 = (bf16[8,1024,128]{2,1,0:T(8,128)(2,1)S(1)}, bf16[8,1024,128]{2,1,0:T(8,128)(2,1)}, u32[]{:S(2)}) copy-start(bf16[8,1024,128]{2,1,0:T(8,128)(2,1)} %param.18) | copy-start | bytes 6291460
  19.4 0.8 copy-start.7
  19.4 1.0 copy-start.8
  49.5 40.6 %copy-start.3 = (s32[256]{0:T(256)S(1)}, s32[256]{0:T(256)}, u32[]{:S(2)}) copy-start(s32[256]{0:T(256)} %param.28) | copy-start | bytes 3076
  49.5 40.6 %copy-start.4 = (f32[256]{0:T(256)S(1)}, f32[256]{0:T(256)}, u32[]{:S(2)}) copy-start(f32[256]{0:T(256)} %param.30) | copy-start | bytes 3076
  49.5 40.6 %copy-start.5 = (f32[256]{0:T(256)S(1)}, f32[256]{0:T(256)}, u32[]{:S(2)}) copy-start(f32[256]{0:T(256)} %param.31) | copy-start | bytes 3076
  49.6 40.5 %all-to-all-start = ((bf16[128,64,128]{2,1,0:T(8,128)(2,1)}), bf16[128,64,128]{2,1,0:T(8,128)(2,1)S(1)}, u32[]{:S(2)}, u32[]{:S(2)}) async-start(bf16[128,64,128]{2,1,0:T(8,128)(2,1)} %get-tuple-element.5.fore_ref), calls=%async_computation | async-start | bytes 4194304 | tf_op jit(solution)/shard_map/all_to_all | solution.py:633
  59.8 36.6 %copy-start.12 = (s32[32,128]{1,0:T(8,128)S(1)}, s32[32,128]{1,0:T(8,128)}, u32[]{:S(2)}) copy-start(s32[32,128]{1,0:T(8,128)} %param.32) | copy-start | bytes 49156
  90.1 9.3 %copy-start = (bf16[128,64,128]{2,1,0:T(8,128)(2,1)}, bf16[128,64,128]{2,1,0:T(8,128)(2,1)S(1)}, u32[]{:S(2)}) copy-start(bf16[128,64,128]{2,1,0:T(8,128)(2,1)S(1)} %all-to-all-done) | copy-start | bytes 6291460
  92.6 6.8 %copy-start.2 = (bf16[80,256]{1,0:T(8,128)(2,1)}, bf16[80,256]{1,0:T(8,128)(2,1)S(1)}, u32[]{:S(2)}) copy-start(bf16[80,256]{1,0:T(8,128)(2,1)S(1)} %observe.1.own_ref) | copy-start | bytes 122884
  92.6 6.8 %collective-permute-start.2 = (bf16[80,256]{1,0:T(8,128)(2,1)S(1)}, bf16[80,256]{1,0:T(8,128)(2,1)S(1)}, u32[]{:S(2)}, u32[]{:S(2)}) collective-permute-start(bf16[80,256]{1,0:T(8,128)(2,1)S(1)} %observe.1.own_ref), channel_id=1, source_target_pairs={{1,2},{3,4},{5,6},{7,8},{9,10},{11,12},{13,14},{15,16},{17,18},{19... | collective-permute-start | bytes 122888 | tf_op jit(solution)/shard_map/ppermute | solution.py:623
  96.3 3.1 %collective-permute-start.3 = (bf16[80,256]{1,0:T(8,128)(2,1)S(1)}, bf16[80,256]{1,0:T(8,128)(2,1)S(1)}, u32[]{:S(2)}, u32[]{:S(2)}) collective-permute-start(bf16[80,256]{1,0:T(8,128)(2,1)S(1)} %observe.1.own_ref), channel_id=1, source_target_pairs={{0,1},{1,0},{2,3},{3,2},{4,5},{5,4},{6,7},{7,6},{8,9},{9,8},{10,11... | collective-permute-start | bytes 122888 | tf_op jit(solution)/shard_map/ppermute | solution.py:624
  99.4 0.6 copy-start.9
  100.0 0.6 copy-start.10
  133.8 36.5 %all-to-all-start.1 = ((bf16[128,64,128]{2,1,0:T(8,128)(2,1)}), bf16[128,64,128]{2,1,0:T(8,128)(2,1)}, u32[]{:S(2)}, u32[]{:S(2)}) async-start(bf16[128,64,128]{2,1,0:T(8,128)(2,1)} %bitcast.34), calls=%async_computation.1 | async-start | bytes 4194304 | tf_op jit(solution)/shard_map/all_to_all | solution.py:633
  140.3 29.9 %copy-start.1 = (bf16[128,64,128]{2,1,0:T(8,128)(2,1)S(1)}, bf16[128,64,128]{2,1,0:T(8,128)(2,1)}, u32[]{:S(2)}) copy-start(bf16[128,64,128]{2,1,0:T(8,128)(2,1)} %get-tuple-element.5.fore_ref) | copy-start | bytes 6291460

commit v4 on v3

--- a/solution.py
+++ b/solution.py
@@ -44,6 +44,7 @@
     send_s,
     recv_s,
     dec_s,
+    raw_s,
     latent_s,
     back_s,
     proc_s,
@@ -55,9 +56,8 @@
     in_sem,
     out_sem,
 ):
-    members = MEMBERS
-    count, width = latent_hbm.shape
-    nodes = count // members
+    members, nodes, width = latent_hbm.shape
+    count = members * nodes
     rim = before_ref.shape[0]
     degree = edge_ref.shape[0] // nodes
     rows = count // CHUNKS
@@ -66,8 +66,14 @@
     def piece(c):
         return pl.ds(c * rows, rows)
 
+    def own(c):
+        return pl.ds(c * (nodes // CHUNKS), nodes // CHUNKS)
+
+    def node_rows(array):
+        return jnp.swapaxes(array.astype(F32), 0, 1).reshape(-1, array.shape[2]).astype(BF16)
+
     loads = [
-        pltpu.make_async_copy(latent_hbm.at[piece(c)], latent_s.at[piece(c)], in_sem.at[c])
+        pltpu.make_async_copy(latent_hbm.at[:, own(c)], raw_s.at[:, own(c)], in_sem.at[c])
         for c in range(CHUNKS)
     ]
     later = [
@@ -99,7 +105,8 @@
     spread_rows(send_s, rim + count, send_of(after_ref[...]))
     for c in range(CHUNKS):
         loads[c].wait()
-        state = latent_s[c * rows : (c + 1) * rows]
+        state = node_rows(raw_s[:, own(c)])
+        latent_s[piece(c)] = state
         spread_rows(send_s, rim + c * rows, send_of(state))
         spread_rows(recv_s, c * rows, dot(state, w_recv_ref[...]) * 0.5)
 
@@ -149,15 +156,17 @@
 
     for c in range(CHUNKS):
 
-        def spread(t, carry):
-            parts = [
-                dec_s[parent_ref[t * GROUP + q]] for q in range(GROUP)
-            ]
-            back = back_s[pl.ds(pl.multiple_of(t * tile, tile), tile), :].astype(F32)
-            fore_s[t] = (jnp.concatenate(parts, axis=0) + back).astype(BF16)
+        def spread(pair, carry):
+            back = back_s[:, pl.ds(pl.multiple_of(pair * 2 * GROUP, 2 * GROUP), 2 * GROUP), :]
+            back = jnp.swapaxes(back.astype(F32), 0, 1).reshape(2 * tile, LANES)
+            for i in range(2):
+                t = pair * 2 + i
+                parts = [dec_s[parent_ref[t * GROUP + q]] for q in range(GROUP)]
+                values = jnp.concatenate(parts, axis=0) + back[i * tile : (i + 1) * tile]
+                fore_s[t] = values.astype(BF16)
             return carry
 
-        lax.fori_loop(c * some, (c + 1) * some, spread, 0, unroll=4)
+        lax.fori_loop(c * some // 2, (c + 1) * some // 2, spread, 0, unroll=4)
         store_fore(c).start()
 
     for c in range(CHUNKS):
@@ -166,8 +175,9 @@
 
 
 def forecast(latent, before, after, back, senders, parent, weights):
-    count, width = latent.shape
-    grid_rows = back.shape[0]
+    members, nodes, width = latent.shape
+    count = members * nodes
+    grid_rows = members * back.shape[1]
     rim = before.shape[0]
     tiles = lax.axis_size("member") * lax.axis_size("region")
     hbm = pl.BlockSpec(memory_space=pl.ANY)
@@ -175,7 +185,7 @@
     return pl.pallas_call(
         forecast_kernel,
         out_shape=(
-            jax.ShapeDtypeStruct(latent.shape, BF16),
+            jax.ShapeDtypeStruct((count, width), BF16),
             jax.ShapeDtypeStruct((tiles, grid_rows // tiles, LANES), BF16),
         ),
         in_specs=[SM, SM, hbm, VM, VM, hbm, VM, VM, hbm, hbm, hbm, VM, hbm],
@@ -185,8 +195,9 @@
             pltpu.VMEM((count // MEMBERS, width // LANES, MEMBERS, LANES), F32),
             pltpu.VMEM((count // MEMBERS, MEMBERS, LANES), F32),
             pltpu.VMEM(latent.shape, BF16),
+            pltpu.VMEM((count, width), BF16),
             pltpu.VMEM(back.shape, BF16),
-            pltpu.VMEM(latent.shape, BF16),
+            pltpu.VMEM((count, width), BF16),
             pltpu.VMEM((tiles, grid_rows // tiles, LANES), BF16),
             w_shape,
             w_shape,
@@ -586,30 +597,55 @@
     )(before, own, after, nbr, loc, ens)
 
 
-def finish_kernel(fore_ref, inc_ref, out_ref, sum_s):
-    members, grid_r, _ = out_ref.shape
-    tiles, rows, _ = fore_ref.shape
-
-    def add(t, carry):
-        sum_s[pl.ds(pl.multiple_of(t * rows, rows), rows), :] = fore_ref[t].astype(F32) + inc_ref[
-            t
-        ].astype(F32)
-        return carry
-
-    lax.fori_loop(0, tiles, add, 0, unroll=4)
-    for k in range(members):
-        out_ref[k] = sum_s[pl.ds(k, grid_r, stride=members), :].astype(BF16)
+def finish_kernel(fore_hbm, inc_hbm, out_hbm, fore_s, inc_s, out_s, in_sem, out_sem):
+    members, grid_r, _ = out_s.shape
+    tiles, rows, _ = fore_s.shape
+    steps = in_sem.shape[0] // 2
+    some, points = tiles // steps, grid_r // steps
+
+    def loads(c):
+        span = pl.ds(c * some, some)
+        return [
+            pltpu.make_async_copy(fore_hbm.at[span], fore_s.at[span], in_sem.at[c]),
+            pltpu.make_async_copy(inc_hbm.at[span], inc_s.at[span], in_sem.at[steps + c]),
+        ]
+
+    def store(c):
+        span = pl.ds(c * points, points)
+        return pltpu.make_async_copy(out_s.at[:, span], out_hbm.at[:, span], out_sem.at[c])
+
+    for c in range(steps):
+        for copy in loads(c):
+            copy.start()
+    for c in range(steps):
+        for copy in loads(c):
+            copy.wait()
+        span = pl.ds(c * some, some)
+        total = fore_s[span].astype(F32) + inc_s[span].astype(F32)
+        total = jnp.swapaxes(total.reshape(points, members, LANES), 0, 1)
+        out_s[:, pl.ds(c * points, points), :] = total.astype(BF16)
+        store(c).start()
+    for c in range(steps):
+        store(c).wait()
 
 
 def finish(fore, inc, members):
     tiles, rows, _ = fore.shape
-    grid_r = tiles * rows // members
+    shape = (members, tiles * rows // members, LANES)
+    steps = 8
+    hbm = pl.BlockSpec(memory_space=pl.ANY)
     return pl.pallas_call(
         finish_kernel,
-        out_shape=jax.ShapeDtypeStruct((members, grid_r, LANES), BF16),
-        in_specs=[VM, VM],
-        out_specs=VM,
-        scratch_shapes=[pltpu.VMEM((tiles * rows, LANES), F32)],
+        out_shape=jax.ShapeDtypeStruct(shape, BF16),
+        in_specs=[hbm, hbm],
+        out_specs=hbm,
+        scratch_shapes=[
+            pltpu.VMEM(fore.shape, BF16),
+            pltpu.VMEM(fore.shape, BF16),
+            pltpu.VMEM(shape, BF16),
+            pltpu.SemaphoreType.DMA((2 * steps,)),
+            pltpu.SemaphoreType.DMA((steps,)),
+        ],
         compiler_params=pltpu.CompilerParams(vmem_limit_bytes=40 * 2**20),
         name="finish",
     )(fore, inc)
@@ -673,10 +709,10 @@
     edges = swapped(edge_senders - (nodes - RIM), RIM, nodes + RIM, odd)
     weights = (w_send, w_recv, w_node, w_agg, w_out, norm_gain[None], w_dec)
     processed, fore = forecast(
-        node_major(latent_vertex_values),
+        latent_vertex_values,
         outer,
         inner,
-        node_major(background_field),
+        background_field,
         edges,
         grid_parent,
         weights,

time: 175 us -> 175 us (level)
  local copies, waits for them, and re-layouts: 20.1 us -> 10.2 us
  waiting for transfers between devices: 56.3 us -> 65.5 us
    transpose x5 -> x3, local copies, waits for them, and re-layouts: 11.2 us -> 1.89 us  [node_major(): return array.transpose(1, 0, 2).reshape(-1, array.shape[2])]
    ppermute x2, waiting for transfers between devices: 2.44 us -> 11.7 us  [neighbours(): got = lax.ppermute(outer, axis, across)]
  transfers between devices with their start and end apart: 6 -> 6, of which waited for: 3 -> 4; matrix products, arithmetic and copies ran while one was open for 10% -> 4% of each run, Pallas kernels for 0% -> 0%
where the time goes in v4:
time: 175 us; the launch traced here: 174 us
  Pallas kernels  67.9 us (39%)
  waiting for transfers between devices  65.5 us (37%)
  starting transfers between devices  28.3 us (16%)
  local copies, waits for them, and re-layouts  10.2 us (6%)
    all_to_all x2, waiting for transfers between devices, exchange(): return lax.all_to_all(blocks, MR, split_axis=0, concat_axis=0, tiled=True)  53.8 us
    pallas_call x1, Pallas kernels, analyse(): pl.pallas_call(analyse_kernel, out_shape=jax.ShapeDtypeStruct(ens.shape,...  33.1 us
    pallas_call x1, Pallas kernels, forecast(): pl.pallas_call(forecast_kernel, out_shape=(jax.ShapeDtypeStruct((count, w...  29.3 us
    all_to_all x2, starting transfers between devices, exchange(): return lax.all_to_all(blocks, MR, split_axis=0, concat_axis=0, tiled=True)  18.1 us
    ppermute x2, waiting for transfers between devices, neighbours(): got = lax.ppermute(outer, axis, across)  11.7 us
    ppermute x2, starting transfers between devices, neighbours(): got = lax.ppermute(outer, axis, across)  8.06 us
    reshape x1, local copies, waits for them, and re-layouts, shards(): processed = processed.reshape(nodes, members, width).transpose(1, 0, 2)  5.75 us
  transfers between devices with their start and end apart: 6, of which 4 were waited for; matrix products, arithmetic and copies ran while one was open for 4% of the time, Pallas kernels for 0%

profile of v4, /device:TPU:1, one launch (start us, length us, event | category | flops | bytes accessed | tf_op | source)
XLA Modules:
  0.0 174.2 jit_solution(643513837060569298)
XLA Ops:
  0.7 1.3 dynamic-slice_bitcast_fusion
  2.0 0.3 copy.31
  2.3 4.4 %collective-permute-start = (bf16[512,512]{1,0:T(8,128)(2,1)S(1)}, bf16[512,512]{1,0:T(8,128)(2,1)S(1)}, u32[]{:S(2)}, u32[]{:S(2)}) collective-permute-start(bf16[512,512]{1,0:T(8,128)(2,1)S(1)} %bitcast.28), channel_id=1, source_target_pairs={{1,2},{3,4},{5,6},{7,8},{9,10},{11,12},{13,14},{15,0},{2,1},{4,3},... | collective-permute-start | bytes 1572872 | tf_op jit(solution)/shard_map/ppermute | solution.py:659
  6.6 0.3 copy.30
  6.9 2.1 %collective-permute-start.1 = (bf16[512,512]{1,0:T(8,128)(2,1)S(1)}, bf16[512,512]{1,0:T(8,128)(2,1)S(1)}, u32[]{:S(2)}, u32[]{:S(2)}) collective-permute-start(bf16[512,512]{1,0:T(8,128)(2,1)S(1)} %bitcast.29), channel_id=1, source_target_pairs={{0,1},{1,0},{2,3},{3,2},{4,5},{5,4},{6,7},{7,6},{8,9},{9,8},{10,11... | collective-permute-start | bytes 1572872 | tf_op jit(solution)/shard_map/ppermute | solution.py:660
  9.1 0.1 copy.22
  9.2 0.8 reshape.22.edge_ref
  10.0 9.1 %collective-permute-done.before_ref = bf16[512,512]{1,0:T(8,128)(2,1)S(1)} collective-permute-done((bf16[512,512]{1,0:T(8,128)(2,1)S(1)}, bf16[512,512]{1,0:T(8,128)(2,1)S(1)}, u32[]{:S(2)}, u32[]{:S(2)}) %collective-permute-start) | collective-permute-done | bytes 524320 | tf_op jit(solution)/shard_map/ppermute | solution.py:659
  19.1 0.0 collective-permute-done.1.after_ref
  19.1 0.8 copy-done.6
  19.9 0.2 copy-done.7
  20.1 29.3 %forecast.1 = (bf16[4096,512]{1,0:T(8,128)(2,1)}, bf16[128,64,128]{2,1,0:T(8,128)(2,1)}) custom-call(s32[3072]{0:T(1024)} %reshape.22.edge_ref, s32[1024]{0:T(1024)} %parent_ref.1, bf16[8,512,512]{2,1,0:T(8,128)(2,1)} %latent_hbm.1, bf16[512,512]{1,0:T(8,128)(2,1)} %copy-done.6, bf16[512,512]{1,0:T(8,128)(2,1)} %copy-done.7, bf16[8,1024,128]{2,1,0:T(8,128)(2,1)} %back_hbm.1, ...), custom_call_target="tpu_custom_call" | custom-call | tf_op jit(solution)/shard_map/forecast/pallas_call | solution.py:185
  49.4 0.0 copy-start.3
  49.4 0.0 copy-start.4
  49.4 0.0 copy-start.5
  49.4 10.5 %all-to-all-start = ((bf16[128,64,128]{2,1,0:T(8,128)(2,1)}), bf16[128,64,128]{2,1,0:T(8,128)(2,1)S(1)}, u32[]{:S(2)}, u32[]{:S(2)}) async-start(bf16[128,64,128]{2,1,0:T(8,128)(2,1)} %get-tuple-element.5.fore_hbm), calls=%async_computation | async-start | bytes 4194304 | tf_op jit(solution)/shard_map/all_to_all | solution.py:669
  59.9 0.0 copy-start.11
  60.5 29.6 %all-to-all-done = bf16[128,64,128]{2,1,0:T(8,128)(2,1)S(1)} async-done(((bf16[128,64,128]{2,1,0:T(8,128)(2,1)}), bf16[128,64,128]{2,1,0:T(8,128)(2,1)S(1)}, u32[]{:S(2)}, u32[]{:S(2)}) %all-to-all-start) | async-done | bytes 2097184 | tf_op jit(solution)/shard_map/all_to_all | solution.py:669
  90.2 0.0 copy-done.4
  90.2 2.5 %observe.1.own_ref = bf16[80,256]{1,0:T(8,128)(2,1)S(1)} custom-call(s32[1]{0:T(128)S(6)} %copy.32.count_ref, s32[1,256]{1,0:T(1,128)S(1)} %bitcast.22, bf16[8,16,64,128]{3,2,1,0:T(8,128)(2,1)S(1)} %bitcast.20, f32[1,256]{1,0:T(1,128)S(1)} %bitcast.23, f32[1,256]{1,0:T(1,128)S(1)} %bitcast.24), custom_call_target="tpu_custom_call" | custom-call | tf_op jit(solution)/shard_map/observe/pallas_call | solution.py:253
  92.7 0.1 collective-permute-start.3
  92.8 3.7 %collective-permute-start.2 = (bf16[80,256]{1,0:T(8,128)(2,1)S(1)}, bf16[80,256]{1,0:T(8,128)(2,1)S(1)}, u32[]{:S(2)}, u32[]{:S(2)}) collective-permute-start(bf16[80,256]{1,0:T(8,128)(2,1)S(1)} %observe.1.own_ref), channel_id=1, source_target_pairs={{1,2},{3,4},{5,6},{7,8},{9,10},{11,12},{13,14},{15,16},{17,18},{19... | collective-permute-start | bytes 122888 | tf_op jit(solution)/shard_map/ppermute | solution.py:659
  96.5 0.6 fusion.3.nbr_ref
  97.1 0.0 collective-permute-done.3.after_ref
  97.1 2.5 %collective-permute-done.2.before_ref = bf16[80,256]{1,0:T(8,128)(2,1)S(1)} collective-permute-done((bf16[80,256]{1,0:T(8,128)(2,1)S(1)}, bf16[80,256]{1,0:T(8,128)(2,1)S(1)}, u32[]{:S(2)}, u32[]{:S(2)}) %collective-permute-start.2) | collective-permute-done | bytes 40992 | tf_op jit(solution)/shard_map/ppermute | solution.py:659
  99.6 0.6 copy-done.9
  100.2 33.1 %analyse.1 = bf16[8,16,64,128]{3,2,1,0:T(8,128)(2,1)} custom-call(bf16[80,256]{1,0:T(8,128)(2,1)} %copy-done.9, bf16[80,256]{1,0:T(8,128)(2,1)} %copy-done.2, bf16[80,256]{1,0:T(8,128)(2,1)} %copy-done.8, s32[32,128]{1,0:T(8,128)} %fusion.3.nbr_ref, f32[32,128]{1,0:T(8,128)} %loc_ref.1, bf16[8,16,64,128]{3,2,1,0:T(8,128)(2,1)} %bitcast.21), custom_call_target="tpu_custom_call" | custom-call | tf_op jit(solution)/shard_map/analyse/pallas_call | solution.py:574
  133.3 7.6 %all-to-all-start.1 = ((bf16[128,64,128]{2,1,0:T(8,128)(2,1)}), bf16[128,64,128]{2,1,0:T(8,128)(2,1)}, u32[]{:S(2)}, u32[]{:S(2)}) async-start(bf16[128,64,128]{2,1,0:T(8,128)(2,1)} %bitcast.25), calls=%async_computation.1 | async-start | bytes 4194304 | tf_op jit(solution)/shard_map/all_to_all | solution.py:669
  140.9 0.0 copy-start.1
  140.9 5.8 %copy.29 = bf16[512,8,512]{2,0,1:T(8,128)(2,1)} copy(bf16[512,8,512]{2,1,0:T(8,128)(2,1)} %bitcast.26) | data formatting | bytes 8388608 | tf_op jit(solution)/shard_map/reshape | solution.py:720
  146.7 24.2 %all-to-all-done.1.inc_hbm = bf16[128,64,128]{2,1,0:T(8,128)(2,1)} async-done(((bf16[128,64,128]{2,1,0:T(8,128)(2,1)}), bf16[128,64,128]{2,1,0:T(8,128)(2,1)}, u32[]{:S(2)}, u32[]{:S(2)}) %all-to-all-start.1) | async-done | bytes 2097184 | tf_op jit(solution)/shard_map/all_to_all | solution.py:669
  170.9 3.1 %finish.1 = bf16[8,1024,128]{2,1,0:T(8,128)(2,1)} custom-call(bf16[128,64,128]{2,1,0:T(8,128)(2,1)S(1)} %copy-done.1, bf16[128,64,128]{2,1,0:T(8,128)(2,1)} %all-to-all-done.1.inc_hbm), custom_call_target="tpu_custom_call" | custom-call | tf_op jit(solution)/shard_map/finish/pallas_call | solution.py:637
  (16 shorter events, 0.0 us)
Async XLA Ops:
  0.6 8.4 %copy-start.10 = (s32[512,6]{0,1:T(8,128)S(1)}, s32[512,6]{0,1:T(8,128)}, u32[]{:S(2)}) copy-start(s32[512,6]{0,1:T(8,128)} %param.19) | copy-start | bytes 36868
  2.3 16.9 %collective-permute-start = (bf16[512,512]{1,0:T(8,128)(2,1)S(1)}, bf16[512,512]{1,0:T(8,128)(2,1)S(1)}, u32[]{:S(2)}, u32[]{:S(2)}) collective-permute-start(bf16[512,512]{1,0:T(8,128)(2,1)S(1)} %bitcast.28), channel_id=1, source_target_pairs={{1,2},{3,4},{5,6},{7,8},{9,10},{11,12},{13,14},{15,0},{2,1},{4,3},... | collective-permute-start | bytes 1572872 | tf_op jit(solution)/shard_map/ppermute | solution.py:659
  6.9 12.2 %collective-permute-start.1 = (bf16[512,512]{1,0:T(8,128)(2,1)S(1)}, bf16[512,512]{1,0:T(8,128)(2,1)S(1)}, u32[]{:S(2)}, u32[]{:S(2)}) collective-permute-start(bf16[512,512]{1,0:T(8,128)(2,1)S(1)} %bitcast.29), channel_id=1, source_target_pairs={{0,1},{1,0},{2,3},{3,2},{4,5},{5,4},{6,7},{7,6},{8,9},{9,8},{10,11... | collective-permute-start | bytes 1572872 | tf_op jit(solution)/shard_map/ppermute | solution.py:660
  19.1 0.8 copy-start.6
  19.1 1.0 copy-start.7
  49.4 40.8 %copy-start.3 = (s32[256]{0:T(256)S(1)}, s32[256]{0:T(256)}, u32[]{:S(2)}) copy-start(s32[256]{0:T(256)} %param.28) | copy-start | bytes 3076
  49.4 40.8 %copy-start.4 = (f32[256]{0:T(256)S(1)}, f32[256]{0:T(256)}, u32[]{:S(2)}) copy-start(f32[256]{0:T(256)} %param.30) | copy-start | bytes 3076
  49.4 40.8 %copy-start.5 = (f32[256]{0:T(256)S(1)}, f32[256]{0:T(256)}, u32[]{:S(2)}) copy-start(f32[256]{0:T(256)} %param.31) | copy-start | bytes 3076
  49.4 40.8 %all-to-all-start = ((bf16[128,64,128]{2,1,0:T(8,128)(2,1)}), bf16[128,64,128]{2,1,0:T(8,128)(2,1)S(1)}, u32[]{:S(2)}, u32[]{:S(2)}) async-start(bf16[128,64,128]{2,1,0:T(8,128)(2,1)} %get-tuple-element.5.fore_hbm), calls=%async_computation | async-start | bytes 4194304 | tf_op jit(solution)/shard_map/all_to_all | solution.py:669
  59.9 36.6 %copy-start.11 = (s32[32,128]{1,0:T(8,128)S(1)}, s32[32,128]{1,0:T(8,128)}, u32[]{:S(2)}) copy-start(s32[32,128]{1,0:T(8,128)} %param.32) | copy-start | bytes 49156
  90.2 9.4 %copy-start = (bf16[128,64,128]{2,1,0:T(8,128)(2,1)}, bf16[128,64,128]{2,1,0:T(8,128)(2,1)S(1)}, u32[]{:S(2)}) copy-start(bf16[128,64,128]{2,1,0:T(8,128)(2,1)S(1)} %all-to-all-done) | copy-start | bytes 6291460
  92.7 6.9 %copy-start.2 = (bf16[80,256]{1,0:T(8,128)(2,1)}, bf16[80,256]{1,0:T(8,128)(2,1)S(1)}, u32[]{:S(2)}) copy-start(bf16[80,256]{1,0:T(8,128)(2,1)S(1)} %observe.1.own_ref) | copy-start | bytes 122884
  92.7 4.4 %collective-permute-start.3 = (bf16[80,256]{1,0:T(8,128)(2,1)S(1)}, bf16[80,256]{1,0:T(8,128)(2,1)S(1)}, u32[]{:S(2)}, u32[]{:S(2)}) collective-permute-start(bf16[80,256]{1,0:T(8,128)(2,1)S(1)} %observe.1.own_ref), channel_id=1, source_target_pairs={{0,1},{1,0},{2,3},{3,2},{4,5},{5,4},{6,7},{7,6},{8,9},{9,8},{10,11... | collective-permute-start | bytes 122888 | tf_op jit(solution)/shard_map/ppermute | solution.py:660
  92.8 6.8 %collective-permute-start.2 = (bf16[80,256]{1,0:T(8,128)(2,1)S(1)}, bf16[80,256]{1,0:T(8,128)(2,1)S(1)}, u32[]{:S(2)}, u32[]{:S(2)}) collective-permute-start(bf16[80,256]{1,0:T(8,128)(2,1)S(1)} %observe.1.own_ref), channel_id=1, source_target_pairs={{1,2},{3,4},{5,6},{7,8},{9,10},{11,12},{13,14},{15,16},{17,18},{19... | collective-permute-start | bytes 122888 | tf_op jit(solution)/shard_map/ppermute | solution.py:659
  97.1 2.5 %copy-start.8 = (bf16[80,256]{1,0:T(8,128)(2,1)}, bf16[80,256]{1,0:T(8,128)(2,1)S(1)}, u32[]{:S(2)}) copy-start(bf16[80,256]{1,0:T(8,128)(2,1)S(1)} %collective-permute-done.3.after_ref) | copy-start | bytes 122884
  99.6 0.6 copy-start.9
  133.3 37.6 %all-to-all-start.1 = ((bf16[128,64,128]{2,1,0:T(8,128)(2,1)}), bf16[128,64,128]{2,1,0:T(8,128)(2,1)}, u32[]{:S(2)}, u32[]{:S(2)}) async-start(bf16[128,64,128]{2,1,0:T(8,128)(2,1)} %bitcast.25), calls=%async_computation.1 | async-start | bytes 4194304 | tf_op jit(solution)/shard_map/all_to_all | solution.py:669
  140.9 29.9 %copy-start.1 = (bf16[128,64,128]{2,1,0:T(8,128)(2,1)S(1)}, bf16[128,64,128]{2,1,0:T(8,128)(2,1)}, u32[]{:S(2)}) copy-start(bf16[128,64,128]{2,1,0:T(8,128)(2,1)} %get-tuple-element.5.fore_hbm) | copy-start | bytes 6291460

commit v5 on v4

--- a/solution.py
+++ b/solution.py
@@ -25,15 +25,104 @@
     return jnp.dot(a, b, preferred_element_type=F32)
 
 
+def lane_blocks(ref, first, values):
+    for c in range(values.shape[1] // LANES):
+        part = values[:, c * LANES : (c + 1) * LANES].reshape(-1, MEMBERS, LANES)
+        ref[first // MEMBERS : first // MEMBERS + part.shape[0], c] = part
+
+
+def project_kernel(
+    latent_hbm,
+    w_send_ref,
+    w_recv_ref,
+    state_hbm,
+    send_hbm,
+    recv_hbm,
+    raw_s,
+    state_s,
+    send_s,
+    recv_s,
+    in_sem,
+    out_sem,
+):
+    members, nodes, width = latent_hbm.shape
+    some = nodes // CHUNKS
+    rows = members * some
+
+    def own(c):
+        return pl.ds(c * some, some)
+
+    def piece(c):
+        return pl.ds(c * rows, rows)
+
+    loads = [
+        pltpu.make_async_copy(latent_hbm.at[:, own(c)], raw_s.at[:, own(c)], in_sem.at[c])
+        for c in range(CHUNKS)
+    ]
+    for copy in loads:
+        copy.start()
+    stores = []
+    for c in range(CHUNKS):
+        loads[c].wait()
+        turned = jnp.swapaxes(raw_s[:, own(c)].astype(F32), 0, 1)
+        state = turned.reshape(rows, width).astype(BF16)
+        state_s[piece(c)] = state
+        send_s[piece(c)] = dot(state, w_send_ref[...]).astype(BF16)
+        lane_blocks(recv_s, c * rows, dot(state, w_recv_ref[...]) * 0.5)
+        pairs = [
+            (state_s.at[piece(c)], state_hbm.at[piece(c)]),
+            (send_s.at[piece(c)], send_hbm.at[piece(c)]),
+            (recv_s.at[own(c)], recv_hbm.at[own(c)]),
+        ]
+        for k, (src, dst) in enumerate(pairs):
+            copy = pltpu.make_async_copy(src, dst, out_sem.at[3 * c + k])
+            copy.start()
+            stores.append(copy)
+    for copy in stores:
+        copy.wait()
+
+
+def project(latent, w_send, w_recv):
+    members, nodes, width = latent.shape
+    count = members * nodes
+    flat = (count, width)
+    blocks = (nodes, width // LANES, members, LANES)
+    hbm = pl.BlockSpec(memory_space=pl.ANY)
+    return pl.pallas_call(
+        project_kernel,
+        out_shape=(
+            jax.ShapeDtypeStruct(flat, BF16),
+            jax.ShapeDtypeStruct(flat, BF16),
+            jax.ShapeDtypeStruct(blocks, F32),
+        ),
+        in_specs=[hbm, VM, VM],
+        out_specs=(hbm, hbm, hbm),
+        scratch_shapes=[
+            pltpu.VMEM(latent.shape, BF16),
+            pltpu.VMEM(flat, BF16),
+            pltpu.VMEM(flat, BF16),
+            pltpu.VMEM(blocks, F32),
+            pltpu.SemaphoreType.DMA((CHUNKS,)),
+            pltpu.SemaphoreType.DMA((3 * CHUNKS,)),
+        ],
+        compiler_params=pltpu.CompilerParams(vmem_limit_bytes=48 * 2**20),
+        cost_estimate=pl.CostEstimate(
+            flops=4 * count * width * width, bytes_accessed=10 * count * width, transcendentals=0
+        ),
+        name="project",
+    )(latent, w_send, w_recv)
+
+
 def forecast_kernel(
     edge_ref,
     parent_ref,
     latent_hbm,
+    sent_hbm,
+    recv_hbm,
     before_ref,
     after_ref,
     back_hbm,
     w_send_ref,
-    w_recv_ref,
     w_node_hbm,
     w_agg_hbm,
     w_out_hbm,
@@ -44,7 +133,7 @@
     send_s,
     recv_s,
     dec_s,
-    raw_s,
+    sent_s,
     latent_s,
     back_s,
     proc_s,
@@ -56,8 +145,8 @@
     in_sem,
     out_sem,
 ):
-    members, nodes, width = latent_hbm.shape
-    count = members * nodes
+    nodes, cols, members, _ = recv_hbm.shape
+    count, width = latent_hbm.shape
     rim = before_ref.shape[0]
     degree = edge_ref.shape[0] // nodes
     rows = count // CHUNKS
@@ -69,17 +158,19 @@
     def own(c):
         return pl.ds(c * (nodes // CHUNKS), nodes // CHUNKS)
 
-    def node_rows(array):
-        return jnp.swapaxes(array.astype(F32), 0, 1).reshape(-1, array.shape[2]).astype(BF16)
-
-    loads = [
-        pltpu.make_async_copy(latent_hbm.at[:, own(c)], raw_s.at[:, own(c)], in_sem.at[c])
+    sent = [
+        pltpu.make_async_copy(sent_hbm.at[piece(c)], sent_s.at[piece(c)], in_sem.at[c])
+        for c in range(CHUNKS)
+    ]
+    mine = [
+        pltpu.make_async_copy(recv_hbm.at[own(c)], recv_s.at[own(c)], in_sem.at[CHUNKS + c])
         for c in range(CHUNKS)
     ]
     later = [
-        pltpu.make_async_copy(src, dst, in_sem.at[CHUNKS + i])
+        pltpu.make_async_copy(src, dst, in_sem.at[2 * CHUNKS + i])
         for i, (src, dst) in enumerate(
             [
+                (latent_hbm, latent_s),
                 (w_node_hbm, w_node_s),
                 (w_agg_hbm, w_agg_s),
                 (w_out_hbm, w_out_s),
@@ -88,27 +179,17 @@
             ]
         )
     ]
-    for copy in loads + later:
+    for copy in sent + mine + later:
         copy.start()
 
-    def send_of(state):
+    def rim_of(state):
         return dot(state, w_send_ref[...]).astype(BF16).astype(F32) * 0.5
 
-    cols = width // LANES
-
-    def spread_rows(ref, first, values):
-        for c in range(cols):
-            part = values[:, c * LANES : (c + 1) * LANES].reshape(-1, members, LANES)
-            ref[first // members : first // members + part.shape[0], c] = part
-
-    spread_rows(send_s, 0, send_of(before_ref[...]))
-    spread_rows(send_s, rim + count, send_of(after_ref[...]))
+    lane_blocks(send_s, 0, rim_of(before_ref[...]))
+    lane_blocks(send_s, rim + count, rim_of(after_ref[...]))
     for c in range(CHUNKS):
-        loads[c].wait()
-        state = node_rows(raw_s[:, own(c)])
-        latent_s[piece(c)] = state
-        spread_rows(send_s, rim + c * rows, send_of(state))
-        spread_rows(recv_s, c * rows, dot(state, w_recv_ref[...]) * 0.5)
+        sent[c].wait()
+        lane_blocks(send_s, rim + c * rows, sent_s[piece(c)].astype(F32) * 0.5)
 
     def aggregate(n, carry):
         mine = recv_s[n]
@@ -119,7 +200,9 @@
         recv_s[n] = total
         return carry
 
-    lax.fori_loop(0, nodes, aggregate, 0, unroll=8)
+    for c in range(CHUNKS):
+        mine[c].wait()
+        lax.fori_loop(c * nodes // CHUNKS, (c + 1) * nodes // CHUNKS, aggregate, 0, unroll=8)
     for copy in later:
         copy.wait()
 
@@ -174,27 +257,28 @@
         store_fore(c).wait()
 
 
-def forecast(latent, before, after, back, senders, parent, weights):
-    members, nodes, width = latent.shape
-    count = members * nodes
+def forecast(projected, before, after, back, senders, parent, weights):
+    latent, sent, recv = projected
+    count, width = latent.shape
+    members = back.shape[0]
     grid_rows = members * back.shape[1]
     rim = before.shape[0]
     tiles = lax.axis_size("member") * lax.axis_size("region")
     hbm = pl.BlockSpec(memory_space=pl.ANY)
-    w_shape = pltpu.VMEM(weights[2].shape, BF16)
+    w_shape = pltpu.VMEM(weights[1].shape, BF16)
     return pl.pallas_call(
         forecast_kernel,
         out_shape=(
             jax.ShapeDtypeStruct((count, width), BF16),
             jax.ShapeDtypeStruct((tiles, grid_rows // tiles, LANES), BF16),
         ),
-        in_specs=[SM, SM, hbm, VM, VM, hbm, VM, VM, hbm, hbm, hbm, VM, hbm],
+        in_specs=[SM, SM, hbm, hbm, hbm, VM, VM, hbm, VM, hbm, hbm, hbm, VM, hbm],
         out_specs=(hbm, hbm),
         scratch_shapes=[
             pltpu.VMEM(((count + 2 * rim) // MEMBERS, width // LANES, MEMBERS, LANES), F32),
             pltpu.VMEM((count // MEMBERS, width // LANES, MEMBERS, LANES), F32),
             pltpu.VMEM((count // MEMBERS, MEMBERS, LANES), F32),
-            pltpu.VMEM(latent.shape, BF16),
+            pltpu.VMEM((count, width), BF16),
             pltpu.VMEM((count, width), BF16),
             pltpu.VMEM(back.shape, BF16),
             pltpu.VMEM((count, width), BF16),
@@ -202,13 +286,13 @@
             w_shape,
             w_shape,
             w_shape,
-            pltpu.VMEM(weights[6].shape, BF16),
-            pltpu.SemaphoreType.DMA((CHUNKS + 5,)),
+            pltpu.VMEM(weights[5].shape, BF16),
+            pltpu.SemaphoreType.DMA((2 * CHUNKS + 6,)),
             pltpu.SemaphoreType.DMA((2 * CHUNKS,)),
         ],
         compiler_params=pltpu.CompilerParams(vmem_limit_bytes=56 * 2**20),
         name="forecast",
-    )(senders.reshape(-1), parent, latent, before, after, back, *weights)
+    )(senders.reshape(-1), parent, latent, sent, recv, before, after, back, *weights)
 
 
 def point_rows(ens_ref, region, start):
@@ -707,9 +791,9 @@
         True,
     )
     edges = swapped(edge_senders - (nodes - RIM), RIM, nodes + RIM, odd)
-    weights = (w_send, w_recv, w_node, w_agg, w_out, norm_gain[None], w_dec)
+    weights = (w_send, w_node, w_agg, w_out, norm_gain[None], w_dec)
     processed, fore = forecast(
-        latent_vertex_values,
+        project(latent_vertex_values, w_send, w_recv),
         outer,
         inner,
         background_field,

time: 175 us -> 170 us (0.971)
  waiting for transfers between devices: 65.5 us -> 56.3 us
  Pallas kernels: 67.9 us -> 72.7 us
  local copies, waits for them, and re-layouts: 10.2 us -> 12.8 us
  starting transfers between devices: 28.3 us -> 25.9 us
    ppermute x2, waiting for transfers between devices: 11.7 us -> 2.44 us  [neighbours(): got = lax.ppermute(outer, axis, across)]
    pallas_call x0 -> x1, Pallas kernels: none -> 8.46 us  [project(): pl.pallas_call(project_kernel, out_shape=(jax.ShapeDtypeStruct(flat, BF16...]
    pallas_call x1, Pallas kernels: 29.3 us -> 25.5 us  [forecast(): pl.pallas_call(forecast_kernel, out_shape=(jax.ShapeDtypeStruct((count, w...]
    unnamed x24 -> x30, local copies, waits for them, and re-layouts: 1.62 us -> 4.17 us
    all_to_all x2, starting transfers between devices: 18.1 us -> 15.7 us  [exchange(): return lax.all_to_all(blocks, MR, split_axis=0, concat_axis=0, tiled=True)]
  transfers between devices with their start and end apart: 6 -> 6, of which waited for: 4 -> 3; matrix products, arithmetic and copies ran while one was open for 4% -> 4% of each run, Pallas kernels for 0% -> 5%
where the time goes in v5:
time: 170 us
  Pallas kernels  72.7 us (43%)
  waiting for transfers between devices  56.3 us (33%)
  starting transfers between devices  25.9 us (15%)
  local copies, waits for them, and re-layouts  12.8 us (8%)
  between operations  1.71 us (1%)
    all_to_all x2, waiting for transfers between devices, exchange(): return lax.all_to_all(blocks, MR, split_axis=0, concat_axis=0, tiled=True)  53.8 us
    pallas_call x1, Pallas kernels, analyse(): pl.pallas_call(analyse_kernel, out_shape=jax.ShapeDtypeStruct(ens.shape,...  33.1 us
    pallas_call x1, Pallas kernels, forecast(): pl.pallas_call(forecast_kernel, out_shape=(jax.ShapeDtypeStruct((count, w...  25.5 us
    all_to_all x2, starting transfers between devices, exchange(): return lax.all_to_all(blocks, MR, split_axis=0, concat_axis=0, tiled=True)  15.7 us
    pallas_call x1, Pallas kernels, project(): pl.pallas_call(project_kernel, out_shape=(jax.ShapeDtypeStruct(flat, BF16...  8.46 us
    ppermute x2, starting transfers between devices, neighbours(): got = lax.ppermute(outer, axis, across)  8.05 us
    reshape x1, local copies, waits for them, and re-layouts, shards(): processed = processed.reshape(nodes, members, width).transpose(1, 0, 2)  5.75 us
    unnamed x30, local copies, waits for them, and re-layouts  4.17 us
  transfers between devices with their start and end apart: 6, of which 3 were waited for; matrix products, arithmetic and copies ran while one was open for 4% of the time, Pallas kernels for 5%

profile of v5, /device:TPU:1, one launch (start us, length us, event | category | flops | bytes accessed | tf_op | source)
XLA Modules:
  0.0 170.0 jit_solution(16102843866236146783)
XLA Ops:
  0.6 0.0 copy-start.3
  0.7 1.4 dynamic-slice_bitcast_fusion
  2.1 0.3 copy.31
  2.4 4.4 %collective-permute-start = (bf16[512,512]{1,0:T(8,128)(2,1)S(1)}, bf16[512,512]{1,0:T(8,128)(2,1)S(1)}, u32[]{:S(2)}, u32[]{:S(2)}) collective-permute-start(bf16[512,512]{1,0:T(8,128)(2,1)S(1)} %bitcast.28), channel_id=1, source_target_pairs={{1,2},{3,4},{5,6},{7,8},{9,10},{11,12},{13,14},{15,0},{2,1},{4,3},... | collective-permute-start | bytes 1572872 | tf_op jit(solution)/shard_map/ppermute | solution.py:743
  6.8 0.3 copy.30
  7.0 2.1 %collective-permute-start.1 = (bf16[512,512]{1,0:T(8,128)(2,1)S(1)}, bf16[512,512]{1,0:T(8,128)(2,1)S(1)}, u32[]{:S(2)}, u32[]{:S(2)}) collective-permute-start(bf16[512,512]{1,0:T(8,128)(2,1)S(1)} %bitcast.29), channel_id=1, source_target_pairs={{0,1},{1,0},{2,3},{3,2},{4,5},{5,4},{6,7},{7,6},{8,9},{9,8},{10,11... | collective-permute-start | bytes 1572872 | tf_op jit(solution)/shard_map/ppermute | solution.py:744
  9.2 0.1 copy.22
  9.3 0.8 reshape.22.edge_ref
  10.1 8.5 %project.1 = (bf16[4096,512]{1,0:T(8,128)(2,1)S(1)}, bf16[4096,512]{1,0:T(8,128)(2,1)}, f32[512,4,8,128]{3,2,1,0:T(8,128)}) custom-call(bf16[8,512,512]{2,1,0:T(8,128)(2,1)} %latent_hbm.1, bf16[512,512]{1,0:T(8,128)(2,1)S(1)} %copy-done.3, bf16[512,512]{1,0:T(8,128)(2,1)S(1)} %copy-done.8), custom_call_target="tpu_custom_call" | custom-call | flops 4294967296 | bytes 20971520 | tf_op jit(solution)/shard_map/project/pallas_call | solution.py:91
  18.6 1.9 %copy-done.2 = bf16[4096,512]{1,0:T(8,128)(2,1)} copy-done((bf16[4096,512]{1,0:T(8,128)(2,1)}, bf16[4096,512]{1,0:T(8,128)(2,1)S(1)}, u32[]{:S(2)}) %copy-start.2) | copy-done | bytes 4194328
  20.5 0.8 copy-done.9
  21.3 0.2 copy-done.10
  21.5 25.5 %forecast.1 = (bf16[4096,512]{1,0:T(8,128)(2,1)}, bf16[128,64,128]{2,1,0:T(8,128)(2,1)}) custom-call(s32[3072]{0:T(1024)} %reshape.22.edge_ref, s32[1024]{0:T(1024)} %parent_ref.1, bf16[4096,512]{1,0:T(8,128)(2,1)} %copy-done.2, bf16[4096,512]{1,0:T(8,128)(2,1)} %get-tuple-element.8.sent_hbm, f32[512,4,8,128]{3,2,1,0:T(8,128)} %get-tuple-element.9.recv_hbm, ...), custom_call_target="tpu_custom_call" | custom-call | tf_op jit(solution)/shard_map/forecast/pallas_call | solution.py:269
  47.1 0.0 copy-start.5
  47.1 0.0 copy-start.6
  47.1 0.0 copy-start.7
  47.1 0.0 copy-start.14
  47.1 9.2 %all-to-all-start = ((bf16[128,64,128]{2,1,0:T(8,128)(2,1)}), bf16[128,64,128]{2,1,0:T(8,128)(2,1)S(1)}, u32[]{:S(2)}, u32[]{:S(2)}) async-start(bf16[128,64,128]{2,1,0:T(8,128)(2,1)} %get-tuple-element.11.fore_hbm), calls=%async_computation | async-start | bytes 4194304 | tf_op jit(solution)/shard_map/all_to_all | solution.py:753
  56.9 29.7 %all-to-all-done = bf16[128,64,128]{2,1,0:T(8,128)(2,1)S(1)} async-done(((bf16[128,64,128]{2,1,0:T(8,128)(2,1)}), bf16[128,64,128]{2,1,0:T(8,128)(2,1)S(1)}, u32[]{:S(2)}, u32[]{:S(2)}) %all-to-all-start) | async-done | bytes 2097184 | tf_op jit(solution)/shard_map/all_to_all | solution.py:753
  86.6 2.5 %observe.1.own_ref = bf16[80,256]{1,0:T(8,128)(2,1)S(1)} custom-call(s32[1]{0:T(128)S(6)} %copy.32.count_ref, s32[1,256]{1,0:T(1,128)S(1)} %bitcast.22, bf16[8,16,64,128]{3,2,1,0:T(8,128)(2,1)S(1)} %bitcast.20, f32[1,256]{1,0:T(1,128)S(1)} %bitcast.23, f32[1,256]{1,0:T(1,128)S(1)} %bitcast.24), custom_call_target="tpu_custom_call" | custom-call | tf_op jit(solution)/shard_map/observe/pallas_call | solution.py:337
  89.1 3.7 %collective-permute-start.2 = (bf16[80,256]{1,0:T(8,128)(2,1)S(1)}, bf16[80,256]{1,0:T(8,128)(2,1)S(1)}, u32[]{:S(2)}, u32[]{:S(2)}) collective-permute-start(bf16[80,256]{1,0:T(8,128)(2,1)S(1)} %observe.1.own_ref), channel_id=1, source_target_pairs={{1,2},{3,4},{5,6},{7,8},{9,10},{11,12},{13,14},{15,16},{17,18},{19... | collective-permute-start | bytes 122888 | tf_op jit(solution)/shard_map/ppermute | solution.py:743
  92.8 0.1 collective-permute-start.3
  92.9 0.6 fusion.3.nbr_ref
  93.5 2.4 %collective-permute-done.2.before_ref = bf16[80,256]{1,0:T(8,128)(2,1)S(1)} collective-permute-done((bf16[80,256]{1,0:T(8,128)(2,1)S(1)}, bf16[80,256]{1,0:T(8,128)(2,1)S(1)}, u32[]{:S(2)}, u32[]{:S(2)}) %collective-permute-start.2) | collective-permute-done | bytes 40992 | tf_op jit(solution)/shard_map/ppermute | solution.py:743
  95.9 0.6 copy-done.11
  96.5 0.6 copy-done.12
  97.1 33.1 %analyse.1 = bf16[8,16,64,128]{3,2,1,0:T(8,128)(2,1)} custom-call(bf16[80,256]{1,0:T(8,128)(2,1)} %copy-done.11, bf16[80,256]{1,0:T(8,128)(2,1)} %copy-done.4, bf16[80,256]{1,0:T(8,128)(2,1)} %copy-done.12, s32[32,128]{1,0:T(8,128)} %fusion.3.nbr_ref, f32[32,128]{1,0:T(8,128)} %loc_ref.1, bf16[8,16,64,128]{3,2,1,0:T(8,128)(2,1)} %bitcast.21), custom_call_target="tpu_custom_call" | custom-call | tf_op jit(solution)/shard_map/analyse/pallas_call | solution.py:658
  130.3 6.5 %all-to-all-start.1 = ((bf16[128,64,128]{2,1,0:T(8,128)(2,1)}), bf16[128,64,128]{2,1,0:T(8,128)(2,1)}, u32[]{:S(2)}, u32[]{:S(2)}) async-start(bf16[128,64,128]{2,1,0:T(8,128)(2,1)} %bitcast.25), calls=%async_computation.1 | async-start | bytes 4194304 | tf_op jit(solution)/shard_map/all_to_all | solution.py:753
  136.8 0.0 copy-start.1
  136.8 5.8 %copy.29 = bf16[512,8,512]{2,0,1:T(8,128)(2,1)} copy(bf16[512,8,512]{2,1,0:T(8,128)(2,1)} %bitcast.26) | data formatting | bytes 8388608 | tf_op jit(solution)/shard_map/reshape | solution.py:804
  142.5 24.2 %all-to-all-done.1.inc_hbm = bf16[128,64,128]{2,1,0:T(8,128)(2,1)} async-done(((bf16[128,64,128]{2,1,0:T(8,128)(2,1)}), bf16[128,64,128]{2,1,0:T(8,128)(2,1)}, u32[]{:S(2)}, u32[]{:S(2)}) %all-to-all-start.1) | async-done | bytes 2097184 | tf_op jit(solution)/shard_map/all_to_all | solution.py:753
  166.7 3.1 %finish.1 = bf16[8,1024,128]{2,1,0:T(8,128)(2,1)} custom-call(bf16[128,64,128]{2,1,0:T(8,128)(2,1)S(1)} %copy-done.1, bf16[128,64,128]{2,1,0:T(8,128)(2,1)} %all-to-all-done.1.inc_hbm), custom_call_target="tpu_custom_call" | custom-call | tf_op jit(solution)/shard_map/finish/pallas_call | solution.py:721
  (23 shorter events, 0.1 us)
Async XLA Ops:
  0.6 8.5 %copy-start.13 = (s32[512,6]{0,1:T(8,128)S(1)}, s32[512,6]{0,1:T(8,128)}, u32[]{:S(2)}) copy-start(s32[512,6]{0,1:T(8,128)} %param.19) | copy-start | bytes 36868
  0.6 9.4 %copy-start.3 = (bf16[512,512]{1,0:T(8,128)(2,1)S(1)}, bf16[512,512]{1,0:T(8,128)(2,1)}, u32[]{:S(2)}) copy-start(bf16[512,512]{1,0:T(8,128)(2,1)} %w_send_ref.3) | copy-start | bytes 1572868
  0.7 9.4 %copy-start.8 = (bf16[512,512]{1,0:T(8,128)(2,1)S(1)}, bf16[512,512]{1,0:T(8,128)(2,1)}, u32[]{:S(2)}) copy-start(bf16[512,512]{1,0:T(8,128)(2,1)} %w_recv_ref.1) | copy-start | bytes 1572868
  2.4 18.1 %collective-permute-start = (bf16[512,512]{1,0:T(8,128)(2,1)S(1)}, bf16[512,512]{1,0:T(8,128)(2,1)S(1)}, u32[]{:S(2)}, u32[]{:S(2)}) collective-permute-start(bf16[512,512]{1,0:T(8,128)(2,1)S(1)} %bitcast.28), channel_id=1, source_target_pairs={{1,2},{3,4},{5,6},{7,8},{9,10},{11,12},{13,14},{15,0},{2,1},{4,3},... | collective-permute-start | bytes 1572872 | tf_op jit(solution)/shard_map/ppermute | solution.py:743
  7.0 13.5 %collective-permute-start.1 = (bf16[512,512]{1,0:T(8,128)(2,1)S(1)}, bf16[512,512]{1,0:T(8,128)(2,1)S(1)}, u32[]{:S(2)}, u32[]{:S(2)}) collective-permute-start(bf16[512,512]{1,0:T(8,128)(2,1)S(1)} %bitcast.29), channel_id=1, source_target_pairs={{0,1},{1,0},{2,3},{3,2},{4,5},{5,4},{6,7},{7,6},{8,9},{9,8},{10,11... | collective-permute-start | bytes 1572872 | tf_op jit(solution)/shard_map/ppermute | solution.py:744
  18.6 1.9 %copy-start.2 = (bf16[4096,512]{1,0:T(8,128)(2,1)}, bf16[4096,512]{1,0:T(8,128)(2,1)S(1)}, u32[]{:S(2)}) copy-start(bf16[4096,512]{1,0:T(8,128)(2,1)S(1)} %get-tuple-element.7.latent_hbm) | copy-start | bytes 12582916
  20.5 0.8 copy-start.9
  20.5 1.0 copy-start.10
  47.1 39.5 %copy-start.5 = (s32[256]{0:T(256)S(1)}, s32[256]{0:T(256)}, u32[]{:S(2)}) copy-start(s32[256]{0:T(256)} %param.28) | copy-start | bytes 3076
  47.1 39.5 %copy-start.6 = (f32[256]{0:T(256)S(1)}, f32[256]{0:T(256)}, u32[]{:S(2)}) copy-start(f32[256]{0:T(256)} %param.30) | copy-start | bytes 3076
  47.1 39.5 %copy-start.7 = (f32[256]{0:T(256)S(1)}, f32[256]{0:T(256)}, u32[]{:S(2)}) copy-start(f32[256]{0:T(256)} %param.31) | copy-start | bytes 3076
  47.1 45.8 %copy-start.14 = (s32[32,128]{1,0:T(8,128)S(1)}, s32[32,128]{1,0:T(8,128)}, u32[]{:S(2)}) copy-start(s32[32,128]{1,0:T(8,128)} %param.32) | copy-start | bytes 49156
  47.1 39.5 %all-to-all-start = ((bf16[128,64,128]{2,1,0:T(8,128)(2,1)}), bf16[128,64,128]{2,1,0:T(8,128)(2,1)S(1)}, u32[]{:S(2)}, u32[]{:S(2)}) async-start(bf16[128,64,128]{2,1,0:T(8,128)(2,1)} %get-tuple-element.11.fore_hbm), calls=%async_computation | async-start | bytes 4194304 | tf_op jit(solution)/shard_map/all_to_all | solution.py:753
  86.6 9.3 %copy-start = (bf16[128,64,128]{2,1,0:T(8,128)(2,1)}, bf16[128,64,128]{2,1,0:T(8,128)(2,1)S(1)}, u32[]{:S(2)}) copy-start(bf16[128,64,128]{2,1,0:T(8,128)(2,1)S(1)} %all-to-all-done) | copy-start | bytes 6291460
  89.1 6.8 %copy-start.4 = (bf16[80,256]{1,0:T(8,128)(2,1)}, bf16[80,256]{1,0:T(8,128)(2,1)S(1)}, u32[]{:S(2)}) copy-start(bf16[80,256]{1,0:T(8,128)(2,1)S(1)} %observe.1.own_ref) | copy-start | bytes 122884
  89.1 6.8 %collective-permute-start.2 = (bf16[80,256]{1,0:T(8,128)(2,1)S(1)}, bf16[80,256]{1,0:T(8,128)(2,1)S(1)}, u32[]{:S(2)}, u32[]{:S(2)}) collective-permute-start(bf16[80,256]{1,0:T(8,128)(2,1)S(1)} %observe.1.own_ref), channel_id=1, source_target_pairs={{1,2},{3,4},{5,6},{7,8},{9,10},{11,12},{13,14},{15,16},{17,18},{19... | collective-permute-start | bytes 122888 | tf_op jit(solution)/shard_map/ppermute | solution.py:743
  92.8 3.2 %collective-permute-start.3 = (bf16[80,256]{1,0:T(8,128)(2,1)S(1)}, bf16[80,256]{1,0:T(8,128)(2,1)S(1)}, u32[]{:S(2)}, u32[]{:S(2)}) collective-permute-start(bf16[80,256]{1,0:T(8,128)(2,1)S(1)} %observe.1.own_ref), channel_id=1, source_target_pairs={{0,1},{1,0},{2,3},{3,2},{4,5},{5,4},{6,7},{7,6},{8,9},{9,8},{10,11... | collective-permute-start | bytes 122888 | tf_op jit(solution)/shard_map/ppermute | solution.py:744
  95.9 0.6 copy-start.11
  96.5 0.6 copy-start.12
  130.3 36.5 %all-to-all-start.1 = ((bf16[128,64,128]{2,1,0:T(8,128)(2,1)}), bf16[128,64,128]{2,1,0:T(8,128)(2,1)}, u32[]{:S(2)}, u32[]{:S(2)}) async-start(bf16[128,64,128]{2,1,0:T(8,128)(2,1)} %bitcast.25), calls=%async_computation.1 | async-start | bytes 4194304 | tf_op jit(solution)/shard_map/all_to_all | solution.py:753
  136.8 29.9 %copy-start.1 = (bf16[128,64,128]{2,1,0:T(8,128)(2,1)S(1)}, bf16[128,64,128]{2,1,0:T(8,128)(2,1)}, u32[]{:S(2)}) copy-start(bf16[128,64,128]{2,1,0:T(8,128)(2,1)} %get-tuple-element.11.fore_hbm) | copy-start | bytes 6291460

commit v6 on v5

--- a/solution.py
+++ b/solution.py
@@ -105,7 +105,7 @@
             pltpu.SemaphoreType.DMA((CHUNKS,)),
             pltpu.SemaphoreType.DMA((3 * CHUNKS,)),
         ],
-        compiler_params=pltpu.CompilerParams(vmem_limit_bytes=48 * 2**20),
+        compiler_params=pltpu.CompilerParams(vmem_limit_bytes=61 * 2**20),
         cost_estimate=pl.CostEstimate(
             flops=4 * count * width * width, bytes_accessed=10 * count * width, transcendentals=0
         ),
@@ -122,7 +122,7 @@
     before_ref,
     after_ref,
     back_hbm,
-    w_send_ref,
+    w_send_hbm,
     w_node_hbm,
     w_agg_hbm,
     w_out_hbm,
@@ -138,6 +138,7 @@
     back_s,
     proc_s,
     fore_s,
+    w_send_s,
     w_node_s,
     w_agg_s,
     w_out_s,
@@ -179,17 +180,19 @@
             ]
         )
     ]
-    for copy in sent + mine + later:
+    first = pltpu.make_async_copy(w_send_hbm, w_send_s, in_sem.at[2 * CHUNKS + 6])
+    for copy in sent + [first] + mine + later:
         copy.start()
 
     def rim_of(state):
-        return dot(state, w_send_ref[...]).astype(BF16).astype(F32) * 0.5
-
-    lane_blocks(send_s, 0, rim_of(before_ref[...]))
-    lane_blocks(send_s, rim + count, rim_of(after_ref[...]))
+        return dot(state, w_send_s[...]).astype(BF16).astype(F32) * 0.5
+
     for c in range(CHUNKS):
         sent[c].wait()
         lane_blocks(send_s, rim + c * rows, sent_s[piece(c)].astype(F32) * 0.5)
+    first.wait()
+    lane_blocks(send_s, 0, rim_of(before_ref[...]))
+    lane_blocks(send_s, rim + count, rim_of(after_ref[...]))
 
     def aggregate(n, carry):
         mine = recv_s[n]
@@ -272,7 +275,7 @@
             jax.ShapeDtypeStruct((count, width), BF16),
             jax.ShapeDtypeStruct((tiles, grid_rows // tiles, LANES), BF16),
         ),
-        in_specs=[SM, SM, hbm, hbm, hbm, VM, VM, hbm, VM, hbm, hbm, hbm, VM, hbm],
+        in_specs=[SM, SM, hbm, hbm, hbm, VM, VM, hbm, hbm, hbm, hbm, hbm, VM, hbm],
         out_specs=(hbm, hbm),
         scratch_shapes=[
             pltpu.VMEM(((count + 2 * rim) // MEMBERS, width // LANES, MEMBERS, LANES), F32),
@@ -286,11 +289,12 @@
             w_shape,
             w_shape,
             w_shape,
+            w_shape,
             pltpu.VMEM(weights[5].shape, BF16),
-            pltpu.SemaphoreType.DMA((2 * CHUNKS + 6,)),
+            pltpu.SemaphoreType.DMA((2 * CHUNKS + 7,)),
             pltpu.SemaphoreType.DMA((2 * CHUNKS,)),
         ],
-        compiler_params=pltpu.CompilerParams(vmem_limit_bytes=56 * 2**20),
+        compiler_params=pltpu.CompilerParams(vmem_limit_bytes=60 * 2**20),
         name="forecast",
     )(senders.reshape(-1), parent, latent, sent, recv, before, after, back, *weights)
 

time: 170 us -> 171 us (level)
  local copies, waits for them, and re-layouts: 12.8 us -> 10.8 us
    unnamed x30 -> x24, local copies, waits for them, and re-layouts: 4.17 us -> 2.24 us
  transfers between devices with their start and end apart: 6 -> 6, of which waited for: 3 -> 4; matrix products, arithmetic and copies ran while one was open for 4% -> 4% of each run, Pallas kernels for 5% -> 5%
where the time goes in v6:
time: 171 us; the launch traced here: 170 us
  Pallas kernels  73.4 us (43%)
  waiting for transfers between devices  56.4 us (33%)
  starting transfers between devices  27.2 us (16%)
  local copies, waits for them, and re-layouts  10.8 us (6%)
    all_to_all x2, waiting for transfers between devices, exchange(): return lax.all_to_all(blocks, MR, split_axis=0, concat_axis=0, tiled=True)  53.8 us
    pallas_call x1, Pallas kernels, analyse(): pl.pallas_call(analyse_kernel, out_shape=jax.ShapeDtypeStruct(ens.shape,...  33.1 us
    pallas_call x1, Pallas kernels, forecast(): pl.pallas_call(forecast_kernel, out_shape=(jax.ShapeDtypeStruct((count, w...  25.7 us
    all_to_all x2, starting transfers between devices, exchange(): return lax.all_to_all(blocks, MR, split_axis=0, concat_axis=0, tiled=True)  17 us
    pallas_call x1, Pallas kernels, project(): pl.pallas_call(project_kernel, out_shape=(jax.ShapeDtypeStruct(flat, BF16...  9.04 us
    ppermute x2, starting transfers between devices, neighbours(): got = lax.ppermute(outer, axis, across)  8.05 us
    reshape x1, local copies, waits for them, and re-layouts, shards(): processed = processed.reshape(nodes, members, width).transpose(1, 0, 2)  5.75 us
  transfers between devices with their start and end apart: 6, of which 4 were waited for; matrix products, arithmetic and copies ran while one was open for 4% of the time, Pallas kernels for 5%

profile of v6, /device:TPU:1, one launch (start us, length us, event | category | flops | bytes accessed | tf_op | source)
XLA Modules:
  0.0 170.1 jit_solution(15333666980728791657)
XLA Ops:
  0.7 1.3 dynamic-slice_bitcast_fusion
  2.0 0.3 copy.31
  2.3 4.4 %collective-permute-start = (bf16[512,512]{1,0:T(8,128)(2,1)S(1)}, bf16[512,512]{1,0:T(8,128)(2,1)S(1)}, u32[]{:S(2)}, u32[]{:S(2)}) collective-permute-start(bf16[512,512]{1,0:T(8,128)(2,1)S(1)} %bitcast.28), channel_id=1, source_target_pairs={{1,2},{3,4},{5,6},{7,8},{9,10},{11,12},{13,14},{15,0},{2,1},{4,3},... | collective-permute-start | bytes 1572872 | tf_op jit(solution)/shard_map/ppermute | solution.py:747
  6.6 0.3 copy.30
  6.9 2.1 %collective-permute-start.1 = (bf16[512,512]{1,0:T(8,128)(2,1)S(1)}, bf16[512,512]{1,0:T(8,128)(2,1)S(1)}, u32[]{:S(2)}, u32[]{:S(2)}) collective-permute-start(bf16[512,512]{1,0:T(8,128)(2,1)S(1)} %bitcast.29), channel_id=1, source_target_pairs={{0,1},{1,0},{2,3},{3,2},{4,5},{5,4},{6,7},{7,6},{8,9},{9,8},{10,11... | collective-permute-start | bytes 1572872 | tf_op jit(solution)/shard_map/ppermute | solution.py:748
  9.1 0.1 copy.22
  9.2 0.8 reshape.22.edge_ref
  10.0 9.0 %project.1 = (bf16[4096,512]{1,0:T(8,128)(2,1)}, bf16[4096,512]{1,0:T(8,128)(2,1)}, f32[512,4,8,128]{3,2,1,0:T(8,128)}) custom-call(bf16[8,512,512]{2,1,0:T(8,128)(2,1)} %latent_hbm.1, bf16[512,512]{1,0:T(8,128)(2,1)} %w_send_hbm.1, bf16[512,512]{1,0:T(8,128)(2,1)} %w_recv_ref.1), custom_call_target="tpu_custom_call" | custom-call | flops 4294967296 | bytes 20971520 | tf_op jit(solution)/shard_map/project/pallas_call | solution.py:91
  19.0 0.1 collective-permute-done.before_ref
  19.1 0.0 collective-permute-done.1.after_ref
  19.1 0.8 copy-done.6
  19.9 0.2 copy-done.7
  20.1 25.7 %forecast.1 = (bf16[4096,512]{1,0:T(8,128)(2,1)}, bf16[128,64,128]{2,1,0:T(8,128)(2,1)}) custom-call(s32[3072]{0:T(1024)} %reshape.22.edge_ref, s32[1024]{0:T(1024)} %parent_ref.1, bf16[4096,512]{1,0:T(8,128)(2,1)} %get-tuple-element.7.latent_hbm, bf16[4096,512]{1,0:T(8,128)(2,1)} %get-tuple-element.8.sent_hbm, ...), custom_call_target="tpu_custom_call" | custom-call | tf_op jit(solution)/shard_map/forecast/pallas_call | solution.py:272
  45.8 0.0 copy-start.3
  45.8 0.0 copy-start.4
  45.9 0.0 copy-start.5
  45.9 0.0 copy-start.11
  45.9 10.4 %all-to-all-start = ((bf16[128,64,128]{2,1,0:T(8,128)(2,1)}), bf16[128,64,128]{2,1,0:T(8,128)(2,1)S(1)}, u32[]{:S(2)}, u32[]{:S(2)}) async-start(bf16[128,64,128]{2,1,0:T(8,128)(2,1)} %get-tuple-element.11.fore_hbm), calls=%async_computation | async-start | bytes 4194304 | tf_op jit(solution)/shard_map/all_to_all | solution.py:757
  57.0 29.7 %all-to-all-done = bf16[128,64,128]{2,1,0:T(8,128)(2,1)S(1)} async-done(((bf16[128,64,128]{2,1,0:T(8,128)(2,1)}), bf16[128,64,128]{2,1,0:T(8,128)(2,1)S(1)}, u32[]{:S(2)}, u32[]{:S(2)}) %all-to-all-start) | async-done | bytes 2097184 | tf_op jit(solution)/shard_map/all_to_all | solution.py:757
  86.6 2.5 %observe.1.own_ref = bf16[80,256]{1,0:T(8,128)(2,1)S(1)} custom-call(s32[1]{0:T(128)S(6)} %copy.32.count_ref, s32[1,256]{1,0:T(1,128)S(1)} %bitcast.22, bf16[8,16,64,128]{3,2,1,0:T(8,128)(2,1)S(1)} %bitcast.20, f32[1,256]{1,0:T(1,128)S(1)} %bitcast.23, f32[1,256]{1,0:T(1,128)S(1)} %bitcast.24), custom_call_target="tpu_custom_call" | custom-call | tf_op jit(solution)/shard_map/observe/pallas_call | solution.py:341
  89.1 3.7 %collective-permute-start.2 = (bf16[80,256]{1,0:T(8,128)(2,1)S(1)}, bf16[80,256]{1,0:T(8,128)(2,1)S(1)}, u32[]{:S(2)}, u32[]{:S(2)}) collective-permute-start(bf16[80,256]{1,0:T(8,128)(2,1)S(1)} %observe.1.own_ref), channel_id=1, source_target_pairs={{1,2},{3,4},{5,6},{7,8},{9,10},{11,12},{13,14},{15,16},{17,18},{19... | collective-permute-start | bytes 122888 | tf_op jit(solution)/shard_map/ppermute | solution.py:747
  92.8 0.1 collective-permute-start.3
  92.9 0.6 fusion.3.nbr_ref
  93.5 2.4 %collective-permute-done.2.before_ref = bf16[80,256]{1,0:T(8,128)(2,1)S(1)} collective-permute-done((bf16[80,256]{1,0:T(8,128)(2,1)S(1)}, bf16[80,256]{1,0:T(8,128)(2,1)S(1)}, u32[]{:S(2)}, u32[]{:S(2)}) %collective-permute-start.2) | collective-permute-done | bytes 40992 | tf_op jit(solution)/shard_map/ppermute | solution.py:747
  96.0 0.6 copy-done.8
  96.6 0.6 copy-done.9
  97.2 33.1 %analyse.1 = bf16[8,16,64,128]{3,2,1,0:T(8,128)(2,1)} custom-call(bf16[80,256]{1,0:T(8,128)(2,1)} %copy-done.8, bf16[80,256]{1,0:T(8,128)(2,1)} %copy-done.2, bf16[80,256]{1,0:T(8,128)(2,1)} %copy-done.9, s32[32,128]{1,0:T(8,128)} %fusion.3.nbr_ref, f32[32,128]{1,0:T(8,128)} %loc_ref.1, bf16[8,16,64,128]{3,2,1,0:T(8,128)(2,1)} %bitcast.21), custom_call_target="tpu_custom_call" | custom-call | tf_op jit(solution)/shard_map/analyse/pallas_call | solution.py:662
  130.3 6.5 %all-to-all-start.1 = ((bf16[128,64,128]{2,1,0:T(8,128)(2,1)}), bf16[128,64,128]{2,1,0:T(8,128)(2,1)}, u32[]{:S(2)}, u32[]{:S(2)}) async-start(bf16[128,64,128]{2,1,0:T(8,128)(2,1)} %bitcast.25), calls=%async_computation.1 | async-start | bytes 4194304 | tf_op jit(solution)/shard_map/all_to_all | solution.py:757
  136.8 0.0 copy-start.1
  136.8 5.8 %copy.29 = bf16[512,8,512]{2,0,1:T(8,128)(2,1)} copy(bf16[512,8,512]{2,1,0:T(8,128)(2,1)} %bitcast.26) | data formatting | bytes 8388608 | tf_op jit(solution)/shard_map/reshape | solution.py:808
  142.6 24.2 %all-to-all-done.1.inc_hbm = bf16[128,64,128]{2,1,0:T(8,128)(2,1)} async-done(((bf16[128,64,128]{2,1,0:T(8,128)(2,1)}), bf16[128,64,128]{2,1,0:T(8,128)(2,1)}, u32[]{:S(2)}, u32[]{:S(2)}) %all-to-all-start.1) | async-done | bytes 2097184 | tf_op jit(solution)/shard_map/all_to_all | solution.py:757
  166.8 3.1 %finish.1 = bf16[8,1024,128]{2,1,0:T(8,128)(2,1)} custom-call(bf16[128,64,128]{2,1,0:T(8,128)(2,1)S(1)} %copy-done.1, bf16[128,64,128]{2,1,0:T(8,128)(2,1)} %all-to-all-done.1.inc_hbm), custom_call_target="tpu_custom_call" | custom-call | tf_op jit(solution)/shard_map/finish/pallas_call | solution.py:725
  (17 shorter events, 0.0 us)
Async XLA Ops:
  0.6 8.4 %copy-start.10 = (s32[512,6]{0,1:T(8,128)S(1)}, s32[512,6]{0,1:T(8,128)}, u32[]{:S(2)}) copy-start(s32[512,6]{0,1:T(8,128)} %param.19) | copy-start | bytes 36868
  2.3 16.9 %collective-permute-start = (bf16[512,512]{1,0:T(8,128)(2,1)S(1)}, bf16[512,512]{1,0:T(8,128)(2,1)S(1)}, u32[]{:S(2)}, u32[]{:S(2)}) collective-permute-start(bf16[512,512]{1,0:T(8,128)(2,1)S(1)} %bitcast.28), channel_id=1, source_target_pairs={{1,2},{3,4},{5,6},{7,8},{9,10},{11,12},{13,14},{15,0},{2,1},{4,3},... | collective-permute-start | bytes 1572872 | tf_op jit(solution)/shard_map/ppermute | solution.py:747
  6.9 12.2 %collective-permute-start.1 = (bf16[512,512]{1,0:T(8,128)(2,1)S(1)}, bf16[512,512]{1,0:T(8,128)(2,1)S(1)}, u32[]{:S(2)}, u32[]{:S(2)}) collective-permute-start(bf16[512,512]{1,0:T(8,128)(2,1)S(1)} %bitcast.29), channel_id=1, source_target_pairs={{0,1},{1,0},{2,3},{3,2},{4,5},{5,4},{6,7},{7,6},{8,9},{9,8},{10,11... | collective-permute-start | bytes 1572872 | tf_op jit(solution)/shard_map/ppermute | solution.py:748
  19.1 0.8 copy-start.6
  19.1 1.0 copy-start.7
  45.8 40.8 %copy-start.3 = (s32[256]{0:T(256)S(1)}, s32[256]{0:T(256)}, u32[]{:S(2)}) copy-start(s32[256]{0:T(256)} %param.28) | copy-start | bytes 3076
  45.8 40.8 %copy-start.4 = (f32[256]{0:T(256)S(1)}, f32[256]{0:T(256)}, u32[]{:S(2)}) copy-start(f32[256]{0:T(256)} %param.30) | copy-start | bytes 3076
  45.9 40.8 %copy-start.5 = (f32[256]{0:T(256)S(1)}, f32[256]{0:T(256)}, u32[]{:S(2)}) copy-start(f32[256]{0:T(256)} %param.31) | copy-start | bytes 3076
  45.9 47.0 %copy-start.11 = (s32[32,128]{1,0:T(8,128)S(1)}, s32[32,128]{1,0:T(8,128)}, u32[]{:S(2)}) copy-start(s32[32,128]{1,0:T(8,128)} %param.32) | copy-start | bytes 49156
  45.9 40.8 %all-to-all-start = ((bf16[128,64,128]{2,1,0:T(8,128)(2,1)}), bf16[128,64,128]{2,1,0:T(8,128)(2,1)S(1)}, u32[]{:S(2)}, u32[]{:S(2)}) async-start(bf16[128,64,128]{2,1,0:T(8,128)(2,1)} %get-tuple-element.11.fore_hbm), calls=%async_computation | async-start | bytes 4194304 | tf_op jit(solution)/shard_map/all_to_all | solution.py:757
  86.6 9.3 %copy-start = (bf16[128,64,128]{2,1,0:T(8,128)(2,1)}, bf16[128,64,128]{2,1,0:T(8,128)(2,1)S(1)}, u32[]{:S(2)}) copy-start(bf16[128,64,128]{2,1,0:T(8,128)(2,1)S(1)} %all-to-all-done) | copy-start | bytes 6291460
  89.1 6.8 %copy-start.2 = (bf16[80,256]{1,0:T(8,128)(2,1)}, bf16[80,256]{1,0:T(8,128)(2,1)S(1)}, u32[]{:S(2)}) copy-start(bf16[80,256]{1,0:T(8,128)(2,1)S(1)} %observe.1.own_ref) | copy-start | bytes 122884
  89.1 6.8 %collective-permute-start.2 = (bf16[80,256]{1,0:T(8,128)(2,1)S(1)}, bf16[80,256]{1,0:T(8,128)(2,1)S(1)}, u32[]{:S(2)}, u32[]{:S(2)}) collective-permute-start(bf16[80,256]{1,0:T(8,128)(2,1)S(1)} %observe.1.own_ref), channel_id=1, source_target_pairs={{1,2},{3,4},{5,6},{7,8},{9,10},{11,12},{13,14},{15,16},{17,18},{19... | collective-permute-start | bytes 122888 | tf_op jit(solution)/shard_map/ppermute | solution.py:747
  92.8 3.2 %collective-permute-start.3 = (bf16[80,256]{1,0:T(8,128)(2,1)S(1)}, bf16[80,256]{1,0:T(8,128)(2,1)S(1)}, u32[]{:S(2)}, u32[]{:S(2)}) collective-permute-start(bf16[80,256]{1,0:T(8,128)(2,1)S(1)} %observe.1.own_ref), channel_id=1, source_target_pairs={{0,1},{1,0},{2,3},{3,2},{4,5},{5,4},{6,7},{7,6},{8,9},{9,8},{10,11... | collective-permute-start | bytes 122888 | tf_op jit(solution)/shard_map/ppermute | solution.py:748
  95.9 0.6 copy-start.8
  96.6 0.6 copy-start.9
  130.3 36.5 %all-to-all-start.1 = ((bf16[128,64,128]{2,1,0:T(8,128)(2,1)}), bf16[128,64,128]{2,1,0:T(8,128)(2,1)}, u32[]{:S(2)}, u32[]{:S(2)}) async-start(bf16[128,64,128]{2,1,0:T(8,128)(2,1)} %bitcast.25), calls=%async_computation.1 | async-start | bytes 4194304 | tf_op jit(solution)/shard_map/all_to_all | solution.py:757
  136.8 29.9 %copy-start.1 = (bf16[128,64,128]{2,1,0:T(8,128)(2,1)S(1)}, bf16[128,64,128]{2,1,0:T(8,128)(2,1)}, u32[]{:S(2)}) copy-start(bf16[128,64,128]{2,1,0:T(8,128)(2,1)} %get-tuple-element.11.fore_hbm) | copy-start | bytes 6291460
